TPU v7x, 256 devices: a whole 4x4x8 slice. The times are simulated.
256 devices in a mesh: tm: 16 (over x, y), band: 16 (over z, core).
Axes of the slice: x: 4, y: 4, z: 8, core: 2. Of those that a mesh axis runs over, the one named last changes fastest.
Arguments:
- features: bfloat16 [32, 128, 64, 256], P('tm', 'band'), may hold values from -31 to 31
- first_gain: float32 [256], replicated, may hold values from 0.1 to 1.9
- first_shift: float32 [256], replicated, may hold values from -3 to 3
- first_weight: bfloat16 [3, 3, 3, 256, 256], replicated, may hold values from -0.078125 to 0.078125
- second_gain: float32 [256], replicated, may hold values from 0.1 to 1.9
- second_shift: float32 [256], replicated, may hold values from -3 to 3
- second_weight: bfloat16 [3, 3, 3, 256, 256], replicated, may hold values from -0.078125 to 0.078125
Outputs:
- decoded: bfloat16 [32, 128, 64, 256], P('tm', 'band')
All inputs are finite; a program needn't handle non-finite values.
Results may differ from a plain program's by a relative error of at most 0.012.
Values may be sent and summed in bfloat16 or wider, within the bound.
No kernel may reach another device: no remote copies, remote signals or barrier semaphores. Data moves between devices by JAX's collectives and lax.ppermute only.
A program may use at most 64 MiB of HBM per device.

v0:
```python
import jax
import jax.numpy as jnp
from jax import lax
from jax.sharding import PartitionSpec as P

GROUPS = 32


EPSILON = 1e-06


def passed_along(value, axis, by):
    devices = lax.axis_size(axis)
    pairs = [(i, i + by) for i in range(devices) if 0 <= i + by < devices]
    return lax.ppermute(value, axis, pairs)


def with_halo(cells, sides, width):
    for axis, dim in sides:
        count = lax.axis_size(axis)
        ends = count - 1
        head = lax.slice_in_dim(cells, 0, width, axis=dim)
        tail = lax.slice_in_dim(cells, cells.shape[dim] - width, cells.shape[dim], axis=dim)
        cells = jnp.concatenate(
            [
                lax.ppermute(tail, axis, [(i, (i + 1) % count) for i in range(ends)]),
                cells,
                lax.ppermute(head, axis, [((i + 1) % count, i) for i in range(ends)]),
            ],
            axis=dim,
        )
    return cells


def group_stats(values):
    frames, row_count, col_count, channels = values.shape
    group_size = channels // GROUPS
    shaped = values.astype(jnp.float32).reshape(frames * row_count * col_count, GROUPS, group_size)
    members = (
        frames * row_count * col_count * group_size * lax.axis_size("tm") * lax.axis_size("band")
    )
    summed = lax.psum(jnp.sum(shaped, axis=(0, 2)), ("tm", "band"))
    centre = summed / members
    centred = shaped - centre[None, :, None]
    spread = lax.psum(jnp.sum(centred * centred, axis=(0, 2)), ("tm", "band"))
    variance = spread / members
    return (centre, variance)


def activate(values, statistics, gain, shift):
    centre, variance = statistics
    group_size = values.shape[-1] // GROUPS
    centre_wide = jnp.repeat(centre, group_size)
    inverse = jnp.repeat(lax.rsqrt(variance + EPSILON), group_size)
    normed = (values.astype(jnp.float32) - centre_wide) * inverse * gain + shift
    return jax.nn.silu(normed).astype(jnp.bfloat16)


def causal_frames(before, current):
    leading = lax.axis_index("tm") == 0
    repeated = jnp.broadcast_to(current[:1], (2,) + current.shape[1:])
    return jnp.concatenate([jnp.where(leading, repeated, before), current], axis=0)


def edge_rows(padded):
    position = lax.axis_index("band")
    upper_row = jnp.where(position == 0, padded[:, 1:2], padded[:, :1])
    lower_row = jnp.where(position == lax.axis_size("band") - 1, padded[:, -2:-1], padded[:, -1:])
    return jnp.concatenate([upper_row, padded[:, 1:-1], lower_row], axis=1)


def edge_cols(values):
    return jnp.pad(values, ((0, 0), (0, 0), (1, 1), (0, 0)), mode="edge")


def convolve(padded, weight):
    frames = padded.shape[0] - 2
    row_count = padded.shape[1] - 2
    col_count = padded.shape[2] - 2
    channels = padded.shape[3]
    outputs = weight.shape[-1]
    shifted = [
        padded[:, row_tap : row_tap + row_count, col_tap : col_tap + col_count, :]
        for row_tap in range(3)
        for col_tap in range(3)
    ]
    columns = jnp.concatenate(shifted, axis=-1)
    matrix = weight.reshape(3, 9 * channels, outputs)
    summed = jnp.zeros((frames * row_count * col_count, outputs), jnp.float32)
    for time_tap in range(3):
        window_rows = columns[time_tap : time_tap + frames].reshape(
            frames * row_count * col_count, 9 * channels
        )
        summed = summed + jnp.dot(window_rows, matrix[time_tap], preferred_element_type=jnp.float32)
    return summed.reshape(frames, row_count, col_count, outputs)


def local(
    features, first_gain, first_shift, first_weight, second_gain, second_shift, second_weight
):
    first_statistics = group_stats(features)
    active = activate(features, first_statistics, first_gain, first_shift)
    earlier = passed_along(active, "tm", 1)
    padded = with_halo(causal_frames(earlier, active), (("band", 1),), 1)
    first_input = edge_cols(edge_rows(padded))
    hidden = convolve(first_input, first_weight).astype(jnp.bfloat16)
    second_statistics = group_stats(hidden)
    active_two = activate(hidden, second_statistics, second_gain, second_shift)
    earlier_two = passed_along(active_two, "tm", 1)
    padded_two = with_halo(causal_frames(earlier_two, active_two), (("band", 1),), 1)
    summed = features.astype(jnp.float32) + convolve(
        edge_cols(edge_rows(padded_two)), second_weight
    )
    return summed.astype(jnp.bfloat16)


def solution(mesh):
    in_specs = (P("tm", "band", None, None), P(), P(), P(), P(), P(), P())
    out_specs = P("tm", "band", None, None)
    return jax.shard_map(local, mesh=mesh, in_specs=in_specs, out_specs=out_specs, check_vma=False)
```

profile of v0, /device:TPU:1, one launch (start us, length us, event | category | flops | bytes accessed | tf_op | source)
XLA Modules:
  0.0 389.0 jit_solution(16272538749429239231)
XLA Ops:
  0.0 1.2 convert_reduce_fusion
  1.4 81.4 %psum.28 = f32[32]{0:T(128)S(1)} all-reduce(f32[32]{0:T(128)S(1)} %reduce_sum.51), channel_id=1, replica_groups=mesh['tm'=16,'band'=16] {'tm','band'}, use_global_device_ids=true, to_apply=%region_2.0 | all-reduce | flops 32 | bytes 256 | tf_op jit(solution)/shard_map/psum | solution.py:42
  83.0 1.2 fusion.36
  84.4 72.4 %psum.29 = f32[32]{0:T(128)S(1)} all-reduce(f32[32]{0:T(128)S(1)} %reduce_sum.54), channel_id=1, replica_groups=mesh['tm'=16,'band'=16] {'tm','band'}, use_global_device_ids=true, to_apply=%region_5.6 | all-reduce | flops 32 | bytes 256 | tf_op jit(solution)/shard_map/psum | solution.py:45
  157.0 1.4 fusion.44
  158.5 2.2 collective-permute-start
  160.8 10.5 %collective-permute-done = bf16[2,8,64,256]{3,2,1,0:T(8,128)(2,1)S(1)} collective-permute-done((bf16[2,8,64,256]{3,2,1,0:T(8,128)(2,1)S(1)}, bf16[2,8,64,256]{3,2,1,0:T(8,128)(2,1)S(1)}, u32[]{:S(2)}, u32[]{:S(2)}) %collective-permute-start) | collective-permute-done | bytes 524320 | tf_op jit(solution)/shard_map/ppermute | solution.py:15
  171.3 5.1 %collective-permute-start.1 = (bf16[4,1,64,256]{3,2,1,0:T(8,128)(2,1)S(1)}, bf16[4,1,64,256]{3,2,1,0:T(8,128)(2,1)S(1)}, u32[]{:S(2)}, u32[]{:S(2)}) collective-permute-start(bf16[4,1,64,256]{3,2,1,0:T(8,128)(2,1)S(1)} %fusion.55), channel_id=1, source_target_pairs={{0,1},{1,2},{2,3},{3,4},{4,5},{5,6},{6,7},{7,8},{8,9},{9,10},{10,1... | collective-permute-start | bytes 393224 | tf_op jit(solution)/shard_map/ppermute | solution.py:26
  176.5 1.9 collective-permute-done.1
  179.1 1.9 collective-permute-start.2
  181.0 3.3 fusion.61
  184.3 2.1 collective-permute-done.2
  186.4 0.9 broadcast_select_fusion.3
  187.3 2.2 fusion.18
  191.7 1.6 fusion.59
  193.4 1.4 fusion.63
  194.8 1.4 convolution_add_fusion.3
  196.2 1.4 fusion.62
  197.8 77.6 %psum.30 = f32[32]{0:T(128)S(1)} all-reduce(f32[32]{0:T(128)S(1)} %reduce_sum.72), channel_id=1, replica_groups=mesh['tm'=16,'band'=16] {'tm','band'}, use_global_device_ids=true, to_apply=%region_8.9 | all-reduce | flops 32 | bytes 256 | tf_op jit(solution)/shard_map/psum | solution.py:42
  276.0 73.6 %psum.31 = f32[32]{0:T(128)S(1)} all-reduce(f32[32]{0:T(128)S(1)} %reduce_sum.75), channel_id=1, replica_groups=mesh['tm'=16,'band'=16] {'tm','band'}, use_global_device_ids=true, to_apply=%region_11.12 | all-reduce | flops 32 | bytes 256 | tf_op jit(solution)/shard_map/psum | solution.py:45
  350.1 3.2 collective-permute-start.3
  353.3 10.3 %collective-permute-done.3 = bf16[2,8,64,256]{3,2,1,0:T(8,128)(2,1)S(1)} collective-permute-done((bf16[2,8,64,256]{3,2,1,0:T(8,128)(2,1)S(1)}, bf16[2,8,64,256]{3,2,1,0:T(8,128)(2,1)S(1)}, u32[]{:S(2)}, u32[]{:S(2)}) %collective-permute-start.3) | collective-permute-done | bytes 524320 | tf_op jit(solution)/shard_map/ppermute | solution.py:15
  363.7 5.1 %collective-permute-start.4 = (bf16[4,1,64,256]{3,2,1,0:T(8,128)(2,1)S(1)}, bf16[4,1,64,256]{3,2,1,0:T(8,128)(2,1)S(1)}, u32[]{:S(2)}, u32[]{:S(2)}) collective-permute-start(bf16[4,1,64,256]{3,2,1,0:T(8,128)(2,1)S(1)} %fusion.53), channel_id=1, source_target_pairs={{0,1},{1,2},{2,3},{3,4},{4,5},{5,6},{6,7},{7,8},{8,9},{9,10},{10,1... | collective-permute-start | bytes 393224 | tf_op jit(solution)/shard_map/ppermute | solution.py:26
  368.9 1.9 collective-permute-done.4
  370.8 1.9 collective-permute-start.5
  373.0 4.8 %collective-permute-done.5 = bf16[4,1,64,256]{3,2,1,0:T(8,128)(2,1)S(1)} collective-permute-done((bf16[4,1,64,256]{3,2,1,0:T(8,128)(2,1)S(1)}, bf16[4,1,64,256]{3,2,1,0:T(8,128)(2,1)S(1)}, u32[]{:S(2)}, u32[]{:S(2)}) %collective-permute-start.5) | collective-permute-done | bytes 131104 | tf_op jit(solution)/shard_map/ppermute | solution.py:28
  377.8 2.2 fusion.19
  382.3 1.6 fusion.58
  383.9 1.4 fusion.64
  385.3 1.4 convolution_add_fusion.1
  386.7 1.4 convolution_add_fusion
  388.1 1.0 fusion.47
  (62 shorter events, 7.4 us)
Async XLA Ops:
  158.5 12.8 %collective-permute-start = (bf16[2,8,64,256]{3,2,1,0:T(8,128)(2,1)S(1)}, bf16[2,8,64,256]{3,2,1,0:T(8,128)(2,1)S(1)}, u32[]{:S(2)}, u32[]{:S(2)}) collective-permute-start(bf16[2,8,64,256]{3,2,1,0:T(8,128)(2,1)S(1)} %fusion.44), channel_id=1, source_target_pairs={{0,16},{16,32},{32,48},{48,64},{64,80},{80,96},{96,112},{112,128},... | collective-permute-start | bytes 1572872 | tf_op jit(solution)/shard_map/ppermute | solution.py:15
  171.3 7.7 %copy-start.3 = (bf16[4,1,64,256]{3,2,1,0:T(8,128)(2,1)}, bf16[4,1,64,256]{3,2,1,0:T(8,128)(2,1)S(1)}, u32[]{:S(2)}) copy-start(bf16[4,1,64,256]{3,2,1,0:T(8,128)(2,1)S(1)} %fusion.55) | copy-start | bytes 393220
  171.3 7.1 %collective-permute-start.1 = (bf16[4,1,64,256]{3,2,1,0:T(8,128)(2,1)S(1)}, bf16[4,1,64,256]{3,2,1,0:T(8,128)(2,1)S(1)}, u32[]{:S(2)}, u32[]{:S(2)}) collective-permute-start(bf16[4,1,64,256]{3,2,1,0:T(8,128)(2,1)S(1)} %fusion.55), channel_id=1, source_target_pairs={{0,1},{1,2},{2,3},{3,4},{4,5},{5,6},{6,7},{7,8},{8,9},{9,10},{10,1... | collective-permute-start | bytes 393224 | tf_op jit(solution)/shard_map/ppermute | solution.py:26
  179.1 7.3 %collective-permute-start.2 = (bf16[4,1,64,256]{3,2,1,0:T(8,128)(2,1)}, bf16[4,1,64,256]{3,2,1,0:T(8,128)(2,1)}, u32[]{:S(2)}, u32[]{:S(2)}) collective-permute-start(bf16[4,1,64,256]{3,2,1,0:T(8,128)(2,1)} %get-tuple-element.8), channel_id=1, source_target_pairs={{1,0},{2,1},{3,2},{4,3},{5,4},{6,5},{7,6},{8,7},{9,8},{10,9},{11,1... | collective-permute-start | bytes 393224 | tf_op jit(solution)/shard_map/ppermute | solution.py:28
  191.7 1.6 copy-start.2
  196.2 153.5 %copy-start.4 = (f32[256]{0:T(256)S(1)}, f32[256]{0:T(256)}, u32[]{:S(2)}) copy-start(f32[256]{0:T(256)} %param.12) | copy-start | bytes 3076
  196.2 153.5 %copy-start.5 = (f32[256]{0:T(256)S(1)}, f32[256]{0:T(256)}, u32[]{:S(2)}) copy-start(f32[256]{0:T(256)} %param.11) | copy-start | bytes 3076
  349.7 23.0 %copy-start.1 = (bf16[3,3,3,256,256]{4,3,2,1,0:T(8,128)(2,1)S(1)}, bf16[3,3,3,256,256]{4,3,2,1,0:T(8,128)(2,1)}, u32[]{:S(2)}) copy-start(bf16[3,3,3,256,256]{4,3,2,1,0:T(8,128)(2,1)} %param.13) | copy-start | bytes 10616836
  350.1 13.6 %collective-permute-start.3 = (bf16[2,8,64,256]{3,2,1,0:T(8,128)(2,1)S(1)}, bf16[2,8,64,256]{3,2,1,0:T(8,128)(2,1)S(1)}, u32[]{:S(2)}, u32[]{:S(2)}) collective-permute-start(bf16[2,8,64,256]{3,2,1,0:T(8,128)(2,1)S(1)} %multiply_convert_fusion), channel_id=1, source_target_pairs={{0,16},{16,32},{32,48},{48,64},{64,80},{80,96},{96,112},{112,128},... | collective-permute-start | bytes 1572872 | tf_op jit(solution)/shard_map/ppermute | solution.py:15
  363.7 7.1 %collective-permute-start.4 = (bf16[4,1,64,256]{3,2,1,0:T(8,128)(2,1)S(1)}, bf16[4,1,64,256]{3,2,1,0:T(8,128)(2,1)S(1)}, u32[]{:S(2)}, u32[]{:S(2)}) collective-permute-start(bf16[4,1,64,256]{3,2,1,0:T(8,128)(2,1)S(1)} %fusion.53), channel_id=1, source_target_pairs={{0,1},{1,2},{2,3},{3,4},{4,5},{5,6},{6,7},{7,8},{8,9},{9,10},{10,1... | collective-permute-start | bytes 393224 | tf_op jit(solution)/shard_map/ppermute | solution.py:26
  370.8 7.0 %collective-permute-start.5 = (bf16[4,1,64,256]{3,2,1,0:T(8,128)(2,1)S(1)}, bf16[4,1,64,256]{3,2,1,0:T(8,128)(2,1)S(1)}, u32[]{:S(2)}, u32[]{:S(2)}) collective-permute-start(bf16[4,1,64,256]{3,2,1,0:T(8,128)(2,1)S(1)} %get-tuple-element.6), channel_id=1, source_target_pairs={{1,0},{2,1},{3,2},{4,3},{5,4},{6,5},{7,6},{8,7},{9,8},{10,9},{11,1... | collective-permute-start | bytes 393224 | tf_op jit(solution)/shard_map/ppermute | solution.py:28
  386.7 1.4 copy-start
where the time goes:
time: 392 us; the launch traced here: 389 us
  blocking collectives  305 us (78%)
  waiting for transfers between devices  31.6 us (8%)
  starting transfers between devices  19.5 us (5%)
  other arithmetic  12.6 us (3%)
  local copies, waits for them, and re-layouts  11.5 us (3%)
  matrix products  8.35 us (2%)
    psum x2, blocking collectives, group_stats(): summed = lax.psum(jnp.sum(shaped, axis=(0, 2)), ('tm', 'band'))  159 us
    psum x2, blocking collectives, group_stats(): spread = lax.psum(jnp.sum(centred * centred, axis=(0, 2)), ('tm', 'band'))  146 us
    ppermute x2, waiting for transfers between devices, passed_along(): return lax.ppermute(value, axis, pairs)  20.8 us
    ppermute x2, starting transfers between devices, with_halo(): lax.ppermute(tail, axis, [(i, (i + 1) % count) for i in range(ends)])  10.2 us
    dot_general x6, matrix products, convolve(): jnp.dot(window_rows, matrix[time_tap], preferred_element_type=jnp.float32)  8.35 us
  transfers between devices with their start and end apart: 6, of which 6 were waited for; matrix products, arithmetic and copies ran while one was open for 1% of the time, Pallas kernels for 0%

commit v1 on v0

v1 whole, which is shorter than its diff:
```python
import functools

import jax
import jax.numpy as jnp
from jax import lax
from jax.experimental import pallas as pl
from jax.experimental.pallas import tpu as pltpu
from jax.sharding import PartitionSpec as P

GROUPS = 32
EPSILON = 1e-06
AXES = ("tm", "band")
LANES = 128
VMEM_LIMIT = 32 * 1024 * 1024
HIGHEST = lax.Precision.HIGHEST


def shifted(value, axis, by):
    count = lax.axis_size(axis)
    pairs = [(i, i + by) for i in range(count) if 0 <= i + by < count]
    return lax.ppermute(value, axis, pairs)


def shifted_both(value, tm_by, band_by):
    tm, band = lax.axis_size("tm"), lax.axis_size("band")
    pairs = [
        (t * band + b, (t + tm_by) * band + b + band_by)
        for t in range(tm)
        for b in range(band)
        if 0 <= t + tm_by < tm and 0 <= b + band_by < band
    ]
    return lax.ppermute(value, AXES, pairs)


def indicator(rows, cols, fn):
    r = lax.broadcasted_iota(jnp.int32, (rows, cols), 0)
    c = lax.broadcasted_iota(jnp.int32, (rows, cols), 1)
    return jnp.where(fn(r, c), 1.0, 0.0).astype(jnp.float32)


def exact_dot(a, b):
    return jnp.dot(a, b, precision=HIGHEST, preferred_element_type=jnp.float32)


def folded(block):
    cols, channels = block.shape
    return jnp.sum(block.reshape(cols // 8, 8, channels), axis=0)


def local_moments(rows, channels):
    size = channels // GROUPS
    total = folded(rows[0]().astype(jnp.float32))
    for row in rows[1:]:
        total = total + folded(row().astype(jnp.float32))
    positions = len(rows) * rows[0]().shape[0]
    channel_mean = jnp.sum(total, axis=0, keepdims=True) * (1.0 / positions)
    channel_mean = jnp.broadcast_to(channel_mean, (8, channels))
    same = indicator(channels, channels, lambda r, c: r // size == c // size)
    group_mean = exact_dot(channel_mean, same) * (1.0 / size)
    centre = group_mean[:1]
    spread = None
    for row in rows:
        off = row().astype(jnp.float32) - centre
        part = folded(off * off)
        spread = part if spread is None else spread + part
    first = indicator(channels, LANES, lambda r, c: r // size == c)
    second = indicator(channels, LANES, lambda r, c: r // size + GROUPS == c)
    spread = jnp.broadcast_to(jnp.sum(spread, axis=0, keepdims=True), (8, channels))
    line = exact_dot(channel_mean, first) * (1.0 / size) + exact_dot(spread, second)
    return line[:1]


def merged_moments(lines, members, channels):
    size = channels // GROUPS
    devices = lines.shape[0]
    mean = jnp.sum(lines, axis=0, keepdims=True) * (1.0 / devices)
    off = lines - mean
    between = jnp.sum(off * off, axis=0, keepdims=True) * (1.0 / devices)
    within = mean * (1.0 / members)
    pick_first = indicator(LANES, channels, lambda r, c: c // size == r)
    pick_second = indicator(LANES, channels, lambda r, c: c // size + GROUPS == r)
    wide = lambda line, pick: exact_dot(jnp.broadcast_to(line, (8, LANES)), pick)[:1]
    centre = wide(mean, pick_first)
    variance = wide(within, pick_second) + wide(between, pick_first)
    return centre, lax.rsqrt(variance + EPSILON)


def activated(x, centre, scale, offset):
    half = (x.astype(jnp.float32) - centre) * scale + offset
    return (half + half * jnp.tanh(half)).astype(jnp.bfloat16)


def load_weight(weight_ref, held_ref, sems):
    channels, outputs = weight_ref.shape[2:]
    copies = []
    for ij in range(9):
        for k in range(3):
            copies.append(
                pltpu.make_async_copy(
                    weight_ref.at[ij, k],
                    held_ref.at[pl.ds(ij * channels, channels), pl.ds(k * outputs, outputs)],
                    sems.at[ij * 3 + k],
                )
            )
    return copies


def convolved(act_ref, held_ref, frame, row_count):
    cols, channels = act_ref.shape[2:]
    outputs = held_ref.shape[1] // 3
    window = jnp.concatenate(
        [
            act_ref[frame + i, j : j + row_count].reshape(row_count * cols, channels)
            for i in range(3)
            for j in range(3)
        ],
        axis=-1,
    )
    taps = jnp.dot(window, held_ref[...], preferred_element_type=jnp.float32)
    taps = taps.reshape(row_count, cols, 3 * outputs)
    column = lax.broadcasted_iota(jnp.int32, (row_count, cols, outputs), 1)
    left = taps[..., :outputs]
    right = taps[..., 2 * outputs :]
    left = jnp.where(column == 0, left, pltpu.roll(left, 1, 1))
    right = jnp.where(column == cols - 1, right, pltpu.roll(right, cols - 1, 1))
    return left + taps[..., outputs : 2 * outputs] + right


def stats_kernel(x_ref, line_ref):
    frames, rows, _, channels = x_ref.shape
    reads = [functools.partial(lambda f, r: x_ref[f, r], f, r) for f in range(frames) for r in range(rows)]
    line_ref[...] = jnp.broadcast_to(local_moments(reads, channels), line_ref.shape)


def first_kernel(members, x_ref, prev_ref, up_ref, down_ref, prev_up_ref, prev_down_ref, lines_ref, gain_ref, shift_ref,
                 weight_ref, hidden_ref, line_ref, act_ref, held_ref, sems):
    copies = load_weight(weight_ref, held_ref, sems)
    for copy in copies:
        copy.start()
    frames, rows, cols, channels = x_ref.shape
    leading = lax.axis_index("tm") == 0
    top = lax.axis_index("band") == 0
    bottom = lax.axis_index("band") == lax.axis_size("band") - 1
    centre, inverse = merged_moments(lines_ref[...], members, channels)
    scale = 0.5 * inverse * gain_ref[...]
    offset = 0.5 * shift_ref[...]

    def own(f, r):
        if r == 0:
            return up_ref[f, 0]
        if r == 1:
            return jnp.where(top, x_ref[f, 0], up_ref[f, 1])
        if r == rows + 2:
            return jnp.where(bottom, x_ref[f, rows - 1], down_ref[f, 0])
        if r == rows + 3:
            return down_ref[f, 1]
        return x_ref[f, r - 2]

    def before(f, r):
        if r == 0:
            return prev_up_ref[f, 0]
        if r == 1:
            return jnp.where(top, prev_ref[f, 0], prev_up_ref[f, 1])
        if r == rows + 2:
            return jnp.where(bottom, prev_ref[f, rows - 1], prev_down_ref[f, 0])
        if r == rows + 3:
            return prev_down_ref[f, 1]
        return prev_ref[f, r - 2]

    for f in range(2 + frames):
        for r in range(rows + 4):
            x = jnp.where(leading, own(0, r), before(f, r)) if f < 2 else own(f - 2, r)
            act_ref[f, r] = activated(x, centre, scale, offset)
    for copy in copies:
        copy.wait()
    for f in range(frames):
        hidden_ref[f] = convolved(act_ref, held_ref, f, rows + 2).astype(jnp.bfloat16)
    reads = [
        functools.partial(lambda f, r: hidden_ref[f, r + 1], f, r) for f in range(frames) for r in range(rows)
    ]
    line_ref[...] = jnp.broadcast_to(local_moments(reads, channels), line_ref.shape)


def second_kernel(members, hidden_ref, prev_ref, lines_ref, gain_ref, shift_ref, x_ref, weight_ref, out_ref, act_ref,
                  held_ref, sems):
    copies = load_weight(weight_ref, held_ref, sems)
    for copy in copies:
        copy.start()
    frames, rows, cols, channels = x_ref.shape
    leading = lax.axis_index("tm") == 0
    top = lax.axis_index("band") == 0
    bottom = lax.axis_index("band") == lax.axis_size("band") - 1
    centre, inverse = merged_moments(lines_ref[...], members, channels)
    scale = 0.5 * inverse * gain_ref[...]
    offset = 0.5 * shift_ref[...]

    def row_of(ref, f, r):
        if r == 0:
            return jnp.where(top, ref[f, 1], ref[f, 0])
        if r == rows + 1:
            return jnp.where(bottom, ref[f, rows], ref[f, rows + 1])
        return ref[f, r]

    for f in range(2 + frames):
        for r in range(rows + 2):
            if f < 2:
                x = jnp.where(leading, row_of(hidden_ref, 0, r), row_of(prev_ref, f, r))
            else:
                x = row_of(hidden_ref, f - 2, r)
            act_ref[f, r] = activated(x, centre, scale, offset)
    for copy in copies:
        copy.wait()
    for f in range(frames):
        out_ref[f] = (x_ref[f].astype(jnp.float32) + convolved(act_ref, held_ref, f, rows)).astype(jnp.bfloat16)


def local(
    features, first_gain, first_shift, first_weight, second_gain, second_shift, second_weight
):
    frames, rows, cols, channels = features.shape
    outputs = first_weight.shape[-1]
    devices = lax.axis_size("tm") * lax.axis_size("band")
    members = frames * rows * cols * (channels // GROUPS)
    vmem = pl.BlockSpec(memory_space=pltpu.VMEM)
    anywhere = pl.BlockSpec(memory_space=pl.ANY)
    params = pltpu.CompilerParams(vmem_limit_bytes=VMEM_LIMIT)
    line = jax.ShapeDtypeStruct((devices, LANES), jnp.float32)
    row = lambda vector: vector.reshape(1, channels)
    taps = lambda weight: weight.reshape(9, 3, channels, outputs)
    scratch = lambda halo_rows: [
        pltpu.VMEM((frames + 2, rows + halo_rows, cols, channels), jnp.bfloat16),
        pltpu.VMEM((9 * channels, 3 * outputs), jnp.bfloat16),
        pltpu.SemaphoreType.DMA((27,)),
    ]

    bottom_rows = features[:, rows - 2 :]
    top_rows = features[:, :2]
    prev = shifted(features, "tm", 1)
    up = shifted(bottom_rows, "band", 1)
    down = shifted(top_rows, "band", -1)
    prev_up = shifted_both(bottom_rows, 1, 1)
    prev_down = shifted_both(top_rows, 1, -1)
    lines = pl.pallas_call(
        stats_kernel, out_shape=line, in_specs=[vmem], out_specs=vmem, compiler_params=params, name="moments"
    )(features)
    lines = lax.all_to_all(lines, AXES, 0, 0, tiled=True)

    hidden, lines = pl.pallas_call(
        functools.partial(first_kernel, members),
        out_shape=[jax.ShapeDtypeStruct((frames, rows + 2, cols, outputs), jnp.bfloat16), line],
        in_specs=[vmem] * 9 + [anywhere],
        out_specs=[vmem, vmem],
        scratch_shapes=scratch(4),
        compiler_params=params,
        name="first_conv",
    )(features, prev, up, down, prev_up, prev_down, lines, row(first_gain), row(first_shift), taps(first_weight))

    prev = shifted(hidden, "tm", 1)
    lines = lax.all_to_all(lines, AXES, 0, 0, tiled=True)

    return pl.pallas_call(
        functools.partial(second_kernel, members),
        out_shape=jax.ShapeDtypeStruct(features.shape, jnp.bfloat16),
        in_specs=[vmem] * 6 + [anywhere],
        out_specs=vmem,
        scratch_shapes=scratch(2),
        compiler_params=params,
        name="second_conv",
    )(hidden, prev, lines, row(second_gain), row(second_shift), features, taps(second_weight))


def solution(mesh):
    in_specs = (P("tm", "band", None, None), P(), P(), P(), P(), P(), P())
    out_specs = P("tm", "band", None, None)
    return jax.shard_map(local, mesh=mesh, in_specs=in_specs, out_specs=out_specs, check_vma=False)
```

time: 392 us -> 85.8 us (0.22)
  blocking collectives: 305 us -> 28.1 us
  waiting for transfers between devices: 31.6 us -> 1.91 us
  Pallas kernels: 0 us -> 14.6 us
  starting transfers between devices: 19.5 us -> 33.9 us
  other arithmetic: 12.6 us -> 0 us
  matrix products: 8.35 us -> 0 us
  local copies, waits for them, and re-layouts: 11.5 us -> 6.46 us
    psum x4 -> x0, blocking collectives: 305 us -> none  [the longest x2 159 us: group_stats(): summed = lax.psum(jnp.sum(shaped, axis=(0, 2)), ('tm', 'band'))]
    ppermute x6, waiting for transfers between devices: 31.6 us -> 1.91 us  [the longest x4 1.9 us: shifted(): return lax.ppermute(value, axis, pairs)]
    all_to_all x0 -> x1, blocking collectives: none -> 28.1 us  [local(): lines = lax.all_to_all(lines, AXES, 0, 0, tiled=True)]
    all_to_all x0 -> x1, starting transfers between devices: none -> 14.8 us  [local(): lines = lax.all_to_all(lines, AXES, 0, 0, tiled=True)]
    pallas_call x0 -> x3, Pallas kernels: none -> 14.6 us  [the longest x1 7.02 us: local(): pl.pallas_call(functools.partial(first_kernel, members), out_shape=[jax.S...]
    dot_general x6 -> x0, matrix products: 8.35 us -> none  [convolve(): jnp.dot(window_rows, matrix[time_tap], preferred_element_type=jnp.float32)]
    slice x4 -> x1, local copies, waits for them, and re-layouts: 6.74 us -> 0.99 us  [local(): top_rows = features[:, :2]]
    concatenate x4 -> x0, other arithmetic: 4.5 us -> none  [the longest x2 4.47 us: edge_cols(): return jnp.pad(values, ((0, 0), (0, 0), (1, 1), (0, 0)), mode='edge')]
  transfers between devices with their start and end apart: 6 -> 7, of which waited for: 6 -> 1; matrix products, arithmetic and copies ran while one was open for 1% -> 1% of each run, Pallas kernels for 0% -> 2%
where the time goes in v1:
time: 85.8 us; the launch traced here: 85.3 us
  starting transfers between devices  33.9 us (40%)
  blocking collectives  28.1 us (33%)
  Pallas kernels  14.6 us (17%)
  local copies, waits for them, and re-layouts  6.46 us (8%)
  waiting for transfers between devices  1.91 us (2%)
    all_to_all x1, blocking collectives, local(): lines = lax.all_to_all(lines, AXES, 0, 0, tiled=True)  28.1 us
    all_to_all x1, starting transfers between devices, local(): lines = lax.all_to_all(lines, AXES, 0, 0, tiled=True)  14.8 us
    ppermute x4, starting transfers between devices, shifted(): return lax.ppermute(value, axis, pairs)  11 us
    ppermute x2, starting transfers between devices, shifted_both(): return lax.ppermute(value, AXES, pairs)  8.09 us
    pallas_call x1, Pallas kernels, local(): pl.pallas_call(functools.partial(first_kernel, members), out_shape=[jax.S...  7.02 us
    pallas_call x1, Pallas kernels, local(): pl.pallas_call(functools.partial(second_kernel, members), out_shape=jax.S...  6.18 us
    unnamed x18, local copies, waits for them, and re-layouts  5.47 us
    ppermute x4, waiting for transfers between devices, shifted(): return lax.ppermute(value, axis, pairs)  1.9 us
  transfers between devices with their start and end apart: 7, of which 1 were waited for; matrix products, arithmetic and copies ran while one was open for 1% of the time, Pallas kernels for 2%

profile of v1, /device:TPU:1, one launch (start us, length us, event | category | flops | bytes accessed | tf_op | source)
XLA Modules:
  0.0 85.3 jit_solution(1342759526960852673)
XLA Ops:
  0.0 4.1 %collective-permute-start = (bf16[2,8,64,256]{3,2,1,0:T(8,128)(2,1)}, bf16[2,8,64,256]{3,2,1,0:T(8,128)(2,1)S(1)}, u32[]{:S(2)}, u32[]{:S(2)}) collective-permute-start(bf16[2,8,64,256]{3,2,1,0:T(8,128)(2,1)} %x_ref.5), channel_id=1, source_target_pairs={{0,16},{16,32},{32,48},{48,64},{64,80},{80,96},{96,112},{112,128},... | collective-permute-start | bytes 1572872 | tf_op jit(solution)/shard_map/ppermute | solution.py:21
  4.1 0.0 copy-start
  4.1 1.1 %copy-done = bf16[2,8,64,256]{3,2,1,0:T(8,128)(2,1)S(1)} copy-done((bf16[2,8,64,256]{3,2,1,0:T(8,128)(2,1)S(1)}, bf16[2,8,64,256]{3,2,1,0:T(8,128)(2,1)}, u32[]{:S(2)}) %copy-start) | copy-done | bytes 524312
  5.1 0.0 copy-start.2
  5.1 0.0 copy-start.8
  5.1 1.4 %moments.1 = f32[256,128]{1,0:T(8,128)} custom-call(bf16[2,8,64,256]{3,2,1,0:T(8,128)(2,1)S(1)} %copy-done), custom_call_target="tpu_custom_call" | custom-call | tf_op jit(solution)/shard_map/moments/pallas_call | solution.py:243
  6.6 14.8 %all-to-all-start = ((f32[256,1,128]{2,1,0:T(1,128)}), f32[256,1,128]{2,1,0:T(1,128)S(1)}, u32[]{:S(2)}, u32[]{:S(2)}) async-start(f32[256,1,128]{2,1,0:T(1,128)} %bitcast.1), calls=%async_computation | async-start | bytes 262144 | tf_op jit(solution)/shard_map/all_to_all | solution.py:246
  21.4 1.0 %fusion = (bf16[2,2,64,256]{3,2,1,0:T(8,128)(2,1)S(1)}, bf16[2,2,64,256]{3,2,1,0:T(8,128)(2,1)S(1)}) fusion(bf16[2,8,64,256]{3,2,1,0:T(8,128)(2,1)} %x_ref.5), kind=kLoop, calls=%fused_computation | loop fusion | bytes 524288 | tf_op jit(solution)/shard_map/slice | solution.py:237
  22.4 3.5 %collective-permute-start.4 = (bf16[2,2,64,256]{3,2,1,0:T(8,128)(2,1)S(1)}, bf16[2,2,64,256]{3,2,1,0:T(8,128)(2,1)S(1)}, u32[]{:S(2)}, u32[]{:S(2)}) collective-permute-start(bf16[2,2,64,256]{3,2,1,0:T(8,128)(2,1)S(1)} %get-tuple-element.9), channel_id=1, source_target_pairs={{1,16},{2,17},{3,18},{4,19},{5,20},{6,21},{7,22},{8,23},{9,24},{10... | collective-permute-start | bytes 393224 | tf_op jit(solution)/shard_map/ppermute | solution.py:32
  25.9 1.9 %collective-permute-start.2 = (bf16[2,2,64,256]{3,2,1,0:T(8,128)(2,1)S(1)}, bf16[2,2,64,256]{3,2,1,0:T(8,128)(2,1)S(1)}, u32[]{:S(2)}, u32[]{:S(2)}) collective-permute-start(bf16[2,2,64,256]{3,2,1,0:T(8,128)(2,1)S(1)} %get-tuple-element.9), channel_id=1, source_target_pairs={{1,0},{2,1},{3,2},{4,3},{5,4},{6,5},{7,6},{8,7},{9,8},{10,9},{11,1... | collective-permute-start | bytes 393224 | tf_op jit(solution)/shard_map/ppermute | solution.py:21
  27.8 4.5 %collective-permute-start.3 = (bf16[2,2,64,256]{3,2,1,0:T(8,128)(2,1)S(1)}, bf16[2,2,64,256]{3,2,1,0:T(8,128)(2,1)S(1)}, u32[]{:S(2)}, u32[]{:S(2)}) collective-permute-start(bf16[2,2,64,256]{3,2,1,0:T(8,128)(2,1)S(1)} %get-tuple-element.10), channel_id=1, source_target_pairs={{0,17},{1,18},{2,19},{3,20},{4,21},{5,22},{6,23},{7,24},{8,25},{9,... | collective-permute-start | bytes 393224 | tf_op jit(solution)/shard_map/ppermute | solution.py:32
  32.4 2.2 %collective-permute-start.1 = (bf16[2,2,64,256]{3,2,1,0:T(8,128)(2,1)S(1)}, bf16[2,2,64,256]{3,2,1,0:T(8,128)(2,1)S(1)}, u32[]{:S(2)}, u32[]{:S(2)}) collective-permute-start(bf16[2,2,64,256]{3,2,1,0:T(8,128)(2,1)S(1)} %get-tuple-element.10), channel_id=1, source_target_pairs={{0,1},{1,2},{2,3},{3,4},{4,5},{5,6},{6,7},{7,8},{8,9},{9,10},{10,1... | collective-permute-start | bytes 393224 | tf_op jit(solution)/shard_map/ppermute | solution.py:21
  34.6 0.0 collective-permute-done.4.prev_down_ref
  34.6 0.0 collective-permute-done.2.down_ref
  34.6 0.0 collective-permute-done.3.prev_up_ref
  34.6 1.9 %collective-permute-done.1.up_ref = bf16[2,2,64,256]{3,2,1,0:T(8,128)(2,1)S(1)} collective-permute-done((bf16[2,2,64,256]{3,2,1,0:T(8,128)(2,1)S(1)}, bf16[2,2,64,256]{3,2,1,0:T(8,128)(2,1)S(1)}, u32[]{:S(2)}, u32[]{:S(2)}) %collective-permute-start.1) | collective-permute-done | bytes 131104 | tf_op jit(solution)/shard_map/ppermute | solution.py:21
  36.5 0.0 all-to-all-done
  36.5 0.0 collective-permute-done.prev_ref
  36.5 0.0 copy-start.1
  36.5 1.0 %copy-done.1 = bf16[2,8,64,256]{3,2,1,0:T(8,128)(2,1)S(1)} copy-done((bf16[2,8,64,256]{3,2,1,0:T(8,128)(2,1)S(1)}, bf16[2,8,64,256]{3,2,1,0:T(8,128)(2,1)}, u32[]{:S(2)}) %copy-start.1) | copy-done | bytes 524312
  37.6 2.0 %copy-done.3 = bf16[3,3,3,256,256]{4,3,2,1,0:T(8,128)(2,1)S(1)} copy-done((bf16[3,3,3,256,256]{4,3,2,1,0:T(8,128)(2,1)S(1)}, bf16[3,3,3,256,256]{4,3,2,1,0:T(8,128)(2,1)}, u32[]{:S(2)}) %copy-start.3) | copy-done | bytes 3538968
  39.6 0.7 copy-done.5
  40.2 0.7 copy-done.6
  40.9 7.0 %first_conv.1 = (bf16[2,10,64,256]{3,2,1,0:T(8,128)(2,1)S(1)}, f32[256,128]{1,0:T(8,128)S(1)}) custom-call(bf16[2,8,64,256]{3,2,1,0:T(8,128)(2,1)S(1)} %copy-done.1, bf16[2,8,64,256]{3,2,1,0:T(8,128)(2,1)S(1)} %collective-permute-done.prev_ref, bf16[2,2,64,256]{3,2,1,0:T(8,128)(2,1)S(1)} %collective-permute-done.1.up_ref, ...), custom_call_target="tpu_custom_call" | custom-call | tf_op jit(solution)/shard_map/first_conv/pallas_call | solution.py:248
  47.9 2.9 %collective-permute-start.5 = (bf16[2,10,64,256]{3,2,1,0:T(8,128)(2,1)S(1)}, bf16[2,10,64,256]{3,2,1,0:T(8,128)(2,1)S(1)}, u32[]{:S(2)}, u32[]{:S(2)}) collective-permute-start(bf16[2,10,64,256]{3,2,1,0:T(8,128)(2,1)S(1)} %get-tuple-element.7.hidden_ref), channel_id=1, source_target_pairs={{0,16},{16,32},{32,48},{48,64},{64,80},{80,96},{96,112},{112,128},... | collective-permute-start | bytes 1966088 | tf_op jit(solution)/shard_map/ppermute | solution.py:21
  50.9 28.1 %all_to_all.22 = f32[256,1,128]{2,1,0:T(1,128)S(1)} all-to-all(f32[256,1,128]{2,1,0:T(1,128)S(1)} %bitcast.18), channel_id=1, replica_groups=mesh['tm'=16,'band'=16] {'tm','band'}, dimensions={0} | all-to-all | bytes 262144 | tf_op jit(solution)/shard_map/all_to_all | solution.py:259
  79.0 0.0 collective-permute-done.5.prev_ref
  79.0 0.0 copy-done.2
  79.0 0.0 copy-done.7
  79.0 0.0 copy-done.8
  79.0 0.0 copy-done.4
  79.0 6.2 %second_conv.1 = bf16[2,8,64,256]{3,2,1,0:T(8,128)(2,1)} custom-call(bf16[2,10,64,256]{3,2,1,0:T(8,128)(2,1)S(1)} %get-tuple-element.7.hidden_ref, bf16[2,10,64,256]{3,2,1,0:T(8,128)(2,1)S(1)} %collective-permute-done.5.prev_ref, f32[256,128]{1,0:T(8,128)S(1)} %bitcast.17, f32[1,256]{1,0:T(1,128)S(1)} %bitcast.21, f32[1,256]{1,0:T(1,128)S(1)} %bitcast.22, ...), custom_call_target="tpu_custom_call" | custom-call | tf_op jit(solution)/shard_map/second_conv/pallas_call | solution.py:261
  (5 shorter events, 0.0 us)
Async XLA Ops:
  0.0 36.5 %collective-permute-start = (bf16[2,8,64,256]{3,2,1,0:T(8,128)(2,1)}, bf16[2,8,64,256]{3,2,1,0:T(8,128)(2,1)S(1)}, u32[]{:S(2)}, u32[]{:S(2)}) collective-permute-start(bf16[2,8,64,256]{3,2,1,0:T(8,128)(2,1)} %x_ref.5), channel_id=1, source_target_pairs={{0,16},{16,32},{32,48},{48,64},{64,80},{80,96},{96,112},{112,128},... | collective-permute-start | bytes 1572872 | tf_op jit(solution)/shard_map/ppermute | solution.py:21
  4.1 1.1 %copy-start = (bf16[2,8,64,256]{3,2,1,0:T(8,128)(2,1)S(1)}, bf16[2,8,64,256]{3,2,1,0:T(8,128)(2,1)}, u32[]{:S(2)}) copy-start(bf16[2,8,64,256]{3,2,1,0:T(8,128)(2,1)} %x_ref.5) | copy-start | bytes 1572868
  5.1 73.9 %copy-start.2 = (bf16[2,8,64,256]{3,2,1,0:T(8,128)(2,1)S(1)}, bf16[2,8,64,256]{3,2,1,0:T(8,128)(2,1)}, u32[]{:S(2)}) copy-start(bf16[2,8,64,256]{3,2,1,0:T(8,128)(2,1)} %x_ref.5) | copy-start | bytes 1572868
  5.1 73.9 %copy-start.7 = (f32[256]{0:T(256)S(1)}, f32[256]{0:T(256)}, u32[]{:S(2)}) copy-start(f32[256]{0:T(256)} %param.11) | copy-start | bytes 3076
  5.1 73.9 %copy-start.8 = (f32[256]{0:T(256)S(1)}, f32[256]{0:T(256)}, u32[]{:S(2)}) copy-start(f32[256]{0:T(256)} %param.12) | copy-start | bytes 3076
  6.6 29.9 %all-to-all-start = ((f32[256,1,128]{2,1,0:T(1,128)}), f32[256,1,128]{2,1,0:T(1,128)S(1)}, u32[]{:S(2)}, u32[]{:S(2)}) async-start(f32[256,1,128]{2,1,0:T(1,128)} %bitcast.1), calls=%async_computation | async-start | bytes 262144 | tf_op jit(solution)/shard_map/all_to_all | solution.py:246
  22.4 12.2 %collective-permute-start.4 = (bf16[2,2,64,256]{3,2,1,0:T(8,128)(2,1)S(1)}, bf16[2,2,64,256]{3,2,1,0:T(8,128)(2,1)S(1)}, u32[]{:S(2)}, u32[]{:S(2)}) collective-permute-start(bf16[2,2,64,256]{3,2,1,0:T(8,128)(2,1)S(1)} %get-tuple-element.9), channel_id=1, source_target_pairs={{1,16},{2,17},{3,18},{4,19},{5,20},{6,21},{7,22},{8,23},{9,24},{10... | collective-permute-start | bytes 393224 | tf_op jit(solution)/shard_map/ppermute | solution.py:32
  25.9 8.7 %collective-permute-start.2 = (bf16[2,2,64,256]{3,2,1,0:T(8,128)(2,1)S(1)}, bf16[2,2,64,256]{3,2,1,0:T(8,128)(2,1)S(1)}, u32[]{:S(2)}, u32[]{:S(2)}) collective-permute-start(bf16[2,2,64,256]{3,2,1,0:T(8,128)(2,1)S(1)} %get-tuple-element.9), channel_id=1, source_target_pairs={{1,0},{2,1},{3,2},{4,3},{5,4},{6,5},{7,6},{8,7},{9,8},{10,9},{11,1... | collective-permute-start | bytes 393224 | tf_op jit(solution)/shard_map/ppermute | solution.py:21
  27.8 6.8 %collective-permute-start.3 = (bf16[2,2,64,256]{3,2,1,0:T(8,128)(2,1)S(1)}, bf16[2,2,64,256]{3,2,1,0:T(8,128)(2,1)S(1)}, u32[]{:S(2)}, u32[]{:S(2)}) collective-permute-start(bf16[2,2,64,256]{3,2,1,0:T(8,128)(2,1)S(1)} %get-tuple-element.10), channel_id=1, source_target_pairs={{0,17},{1,18},{2,19},{3,20},{4,21},{5,22},{6,23},{7,24},{8,25},{9,... | collective-permute-start | bytes 393224 | tf_op jit(solution)/shard_map/ppermute | solution.py:32
  32.4 4.1 %collective-permute-start.1 = (bf16[2,2,64,256]{3,2,1,0:T(8,128)(2,1)S(1)}, bf16[2,2,64,256]{3,2,1,0:T(8,128)(2,1)S(1)}, u32[]{:S(2)}, u32[]{:S(2)}) collective-permute-start(bf16[2,2,64,256]{3,2,1,0:T(8,128)(2,1)S(1)} %get-tuple-element.10), channel_id=1, source_target_pairs={{0,1},{1,2},{2,3},{3,4},{4,5},{5,6},{6,7},{7,8},{8,9},{9,10},{10,1... | collective-permute-start | bytes 393224 | tf_op jit(solution)/shard_map/ppermute | solution.py:21
  36.5 1.0 %copy-start.1 = (bf16[2,8,64,256]{3,2,1,0:T(8,128)(2,1)S(1)}, bf16[2,8,64,256]{3,2,1,0:T(8,128)(2,1)}, u32[]{:S(2)}) copy-start(bf16[2,8,64,256]{3,2,1,0:T(8,128)(2,1)} %x_ref.5) | copy-start | bytes 1572868
  37.5 2.0 %copy-start.3 = (bf16[3,3,3,256,256]{4,3,2,1,0:T(8,128)(2,1)S(1)}, bf16[3,3,3,256,256]{4,3,2,1,0:T(8,128)(2,1)}, u32[]{:S(2)}) copy-start(bf16[3,3,3,256,256]{4,3,2,1,0:T(8,128)(2,1)} %param.10) | copy-start | bytes 10616836
  39.6 0.7 copy-start.5
  40.2 0.7 copy-start.6
  40.9 38.1 %copy-start.4 = (bf16[3,3,3,256,256]{4,3,2,1,0:T(8,128)(2,1)S(1)}, bf16[3,3,3,256,256]{4,3,2,1,0:T(8,128)(2,1)}, u32[]{:S(2)}) copy-start(bf16[3,3,3,256,256]{4,3,2,1,0:T(8,128)(2,1)} %param.13) | copy-start | bytes 10616836
  47.9 31.0 %collective-permute-start.5 = (bf16[2,10,64,256]{3,2,1,0:T(8,128)(2,1)S(1)}, bf16[2,10,64,256]{3,2,1,0:T(8,128)(2,1)S(1)}, u32[]{:S(2)}, u32[]{:S(2)}) collective-permute-start(bf16[2,10,64,256]{3,2,1,0:T(8,128)(2,1)S(1)} %get-tuple-element.7.hidden_ref), channel_id=1, source_target_pairs={{0,16},{16,32},{32,48},{48,64},{64,80},{80,96},{96,112},{112,128},... | collective-permute-start | bytes 1966088 | tf_op jit(solution)/shard_map/ppermute | solution.py:21

commit v2 on v1

v2 whole, which is shorter than its diff:
```python
import functools

import jax
import jax.numpy as jnp
from jax import lax
from jax.experimental import pallas as pl
from jax.experimental.pallas import tpu as pltpu
from jax.sharding import PartitionSpec as P

GROUPS = 32
EPSILON = 1e-06
LANES = 128
VMEM_LIMIT = 32 * 1024 * 1024
HIGHEST = lax.Precision.HIGHEST


def next_frames(value):
    count = lax.axis_size("tm")
    return lax.ppermute(value, "tm", [(i, i + 1) for i in range(count - 1)])


def swapped(value, axis, first):
    count = lax.axis_size(axis)
    pairs = []
    for i in range(first, count - 1, 2):
        pairs += [(i, i + 1), (i + 1, i)]
    return lax.ppermute(value, axis, pairs)


def indicator(rows, cols, fn):
    r = lax.broadcasted_iota(jnp.int32, (rows, cols), 0)
    c = lax.broadcasted_iota(jnp.int32, (rows, cols), 1)
    return jnp.where(fn(r, c), 1.0, 0.0).astype(jnp.float32)


def exact_dot(a, b):
    return jnp.dot(a, b, precision=HIGHEST, preferred_element_type=jnp.float32)


def folded(block):
    cols, channels = block.shape
    return jnp.sum(block.reshape(cols // 8, 8, channels), axis=0)


def local_moments(rows, channels):
    size = channels // GROUPS
    total = folded(rows[0]().astype(jnp.float32))
    for row in rows[1:]:
        total = total + folded(row().astype(jnp.float32))
    positions = len(rows) * rows[0]().shape[0]
    channel_mean = jnp.sum(total, axis=0, keepdims=True) * (1.0 / positions)
    channel_mean = jnp.broadcast_to(channel_mean, (8, channels))
    same = indicator(channels, channels, lambda r, c: r // size == c // size)
    group_mean = exact_dot(channel_mean, same) * (1.0 / size)
    centre = group_mean[:1]
    spread = None
    for row in rows:
        off = row().astype(jnp.float32) - centre
        part = folded(off * off)
        spread = part if spread is None else spread + part
    first = indicator(channels, LANES, lambda r, c: r // size == c)
    second = indicator(channels, LANES, lambda r, c: r // size + GROUPS == c)
    spread = jnp.broadcast_to(jnp.sum(spread, axis=0, keepdims=True), (8, channels))
    line = exact_dot(channel_mean, first) * (1.0 / size) + exact_dot(spread, second)
    return line[:1]


def merged_lines(lines, members):
    count = lines.shape[0]
    total = jnp.sum(lines, axis=0, keepdims=True)
    mean = total * (1.0 / count)
    off = lines - mean
    between = jnp.sum(off * off, axis=0, keepdims=True) * members
    lane = lax.broadcasted_iota(jnp.int32, (1, LANES), 1)
    between = jnp.broadcast_to(between, (8, LANES))
    between = pltpu.roll(between, GROUPS, 1)[:1]
    return jnp.where(lane < GROUPS, mean, jnp.where(lane < 2 * GROUPS, total + between, 0.0))


def channel_moments(line, members, channels):
    size = channels // GROUPS
    pick_first = indicator(LANES, channels, lambda r, c: c // size == r)
    pick_second = indicator(LANES, channels, lambda r, c: c // size + GROUPS == r)
    line = jnp.broadcast_to(line, (8, LANES))
    centre = exact_dot(line, pick_first)[:1]
    variance = exact_dot(line, pick_second)[:1] * (1.0 / members)
    return centre, lax.rsqrt(variance + EPSILON)


def activated(x, centre, scale, offset):
    half = (x.astype(jnp.float32) - centre) * scale + offset
    return (half + half * jnp.tanh(half)).astype(jnp.bfloat16)


def convolved(act_ref, weight_ref, frame, row_count):
    cols, channels = act_ref.shape[2:]
    outputs = weight_ref.shape[-1]
    window = jnp.concatenate(
        [
            act_ref[frame + i, j : j + row_count].reshape(row_count * cols, channels)
            for i in range(3)
            for j in range(3)
        ],
        axis=-1,
    )
    left, middle, right = (
        jnp.dot(
            window,
            weight_ref[:, k].reshape(9 * channels, outputs),
            preferred_element_type=jnp.float32,
        ).reshape(row_count, cols, outputs)
        for k in range(3)
    )
    column = lax.broadcasted_iota(jnp.int32, (row_count, cols, outputs), 1)
    left = jnp.where(column == 0, left, pltpu.roll(left, 1, 1))
    right = jnp.where(column == cols - 1, right, pltpu.roll(right, cols - 1, 1))
    return left + middle + right


def places(rows):
    even = lax.rem(lax.axis_index("band"), 2) == 0
    pair_at, cross_at = jnp.where(even, rows + 2, 0), jnp.where(even, 0, rows + 2)
    pair_from, cross_from = jnp.where(even, rows - 2, 0), jnp.where(even, 0, rows - 2)
    return pair_at, cross_at, pair_from, cross_from


def stats_kernel(x_ref, *refs):
    vectors, (line_ref, kept_ref, params_ref, sems) = refs[:4], refs[4:]
    frames, rows, _, channels = x_ref.shape
    copies = [pltpu.make_async_copy(x_ref.at[f], kept_ref.at[f], sems.at[f]) for f in range(frames)]
    copies += [
        pltpu.make_async_copy(vector, params_ref.at[pl.ds(i, 1)], sems.at[frames + i])
        for i, vector in enumerate(vectors)
    ]
    for copy in copies:
        copy.start()
    for copy in copies:
        copy.wait()
    reads = [functools.partial(lambda f, r: kept_ref[f, r], f, r) for f in range(frames) for r in range(rows)]
    line_ref[...] = jnp.broadcast_to(local_moments(reads, channels), line_ref.shape)


def edges_kernel(members, lines_ref, x_ref, prev_ref, line_ref, pair_ref, cross_ref):
    rows = x_ref.shape[1]
    _, _, pair_from, cross_from = places(rows)
    for out_ref, at in ((pair_ref, pair_from), (cross_ref, cross_from)):
        out_ref[0:2] = prev_ref[:, pl.ds(at, 2)]
        out_ref[2:4] = x_ref[:, pl.ds(at, 2)]
    line_ref[...] = jnp.broadcast_to(merged_lines(lines_ref[...], members), line_ref.shape)


def merge_kernel(members, lines_ref, line_ref):
    line_ref[...] = jnp.broadcast_to(merged_lines(lines_ref[...], members), line_ref.shape)


def scaling(lines_ref, params_ref, norm, members):
    channels = params_ref.shape[1]
    devices = lax.axis_size("tm") * lax.axis_size("band")
    line = merged_lines(lines_ref[...], members * lax.axis_size("band"))
    centre, inverse = channel_moments(line, members * devices, channels)
    gain, shift = params_ref[2 * norm : 2 * norm + 1], params_ref[2 * norm + 1 : 2 * norm + 2]
    return centre, 0.5 * inverse * gain, 0.5 * shift


def at_ends():
    band = lax.axis_index("band")
    return lax.axis_index("tm") == 0, band == 0, band == lax.axis_size("band") - 1


def first_kernel(members, x_ref, prev_ref, pair_ref, cross_ref, lines_ref, params_ref, weight_ref,
                 hidden_ref, line_ref, act_ref, held_ref, weight_sems):
    frames, rows, cols, channels = x_ref.shape
    weights = [pltpu.make_async_copy(weight_ref.at[t], held_ref.at[t], weight_sems.at[t]) for t in range(9)]
    for copy in weights:
        copy.start()
    leading, top, bottom = at_ends()
    even = lax.rem(lax.axis_index("band"), 2) == 0
    norm = scaling(lines_ref, params_ref, 0, members)

    def row_of(f, r):
        inner = prev_ref if f < 2 else x_ref
        if 2 <= r < rows + 2:
            return inner[f % 2, r - 2]
        if r < 2:
            outer = jnp.where(even, cross_ref[f, r], pair_ref[f, r])
            return jnp.where(top, inner[f % 2, 0], outer) if r == 1 else outer
        outer = jnp.where(even, pair_ref[f, r - rows - 2], cross_ref[f, r - rows - 2])
        return jnp.where(bottom, inner[f % 2, rows - 1], outer) if r == rows + 2 else outer

    def activate(f):
        for r in range(rows + 4):
            x = jnp.where(leading, row_of(2, r), row_of(f, r)) if f < 2 else row_of(f, r)
            act_ref[f, r] = activated(x, *norm)

    for f in range(2 + frames):
        activate(f)
    for copy in weights:
        copy.wait()
    for f in range(frames):
        hidden_ref[f] = convolved(act_ref, held_ref, f, rows + 2).astype(jnp.bfloat16)
    reads = [functools.partial(lambda f, r: hidden_ref[f, r + 1], f, r) for f in range(frames) for r in range(rows)]
    line_ref[...] = jnp.broadcast_to(local_moments(reads, channels), line_ref.shape)


def second_kernel(members, hidden_ref, prev_ref, lines_ref, params_ref, x_ref, weight_ref, out_ref,
                  act_ref, made_ref, out_sems):
    frames, rows, cols, channels = x_ref.shape
    leading, top, bottom = at_ends()
    norm = scaling(lines_ref, params_ref, 1, members)

    def row_of(f, r):
        ref = prev_ref if f < 2 else hidden_ref
        if r == 0:
            return jnp.where(top, ref[f % 2, 1], ref[f % 2, 0])
        if r == rows + 1:
            return jnp.where(bottom, ref[f % 2, rows], ref[f % 2, rows + 1])
        return ref[f % 2, r]

    def activate(f):
        for r in range(rows + 2):
            x = jnp.where(leading, row_of(2, r), row_of(f, r)) if f < 2 else row_of(f, r)
            act_ref[f, r] = activated(x, *norm)

    for f in range(2 + frames):
        activate(f)
    outs = []
    for f in range(frames):
        made_ref[f] = (x_ref[f].astype(jnp.float32) + convolved(act_ref, weight_ref, f, rows)).astype(jnp.bfloat16)
        outs.append(pltpu.make_async_copy(made_ref.at[f], out_ref.at[f], out_sems.at[f]))
        outs[-1].start()
    for copy in outs:
        copy.wait()


def local(
    features, first_gain, first_shift, first_weight, second_gain, second_shift, second_weight
):
    frames, rows, cols, channels = features.shape
    outputs = first_weight.shape[-1]
    tm, band = lax.axis_size("tm"), lax.axis_size("band")
    members = frames * rows * cols * (channels // GROUPS)
    vmem = pl.BlockSpec(memory_space=pltpu.VMEM)
    hbm = pl.BlockSpec(memory_space=pltpu.HBM)
    params = pltpu.CompilerParams(vmem_limit_bytes=VMEM_LIMIT)
    small = pltpu.CompilerParams(vmem_limit_bytes=4 * 1024 * 1024)
    line = lambda count: jax.ShapeDtypeStruct((count, LANES), jnp.float32)
    block = lambda f, r: jax.ShapeDtypeStruct((f, r, cols, channels), jnp.bfloat16)
    held = lambda f, r: pltpu.VMEM((f, r, cols, channels), jnp.bfloat16)
    dmas = lambda count: pltpu.SemaphoreType.DMA((count,))
    taps = lambda weight: weight.reshape(9, 3, channels, outputs)
    stay = lambda value: pltpu.with_memory_space_constraint(value, pltpu.HBM)
    spread_over = lambda lines, axis: lax.all_to_all(lines, axis, 0, 0, tiled=True)
    vectors = [v.reshape(1, channels) for v in (first_gain, first_shift, second_gain, second_shift)]

    prev = next_frames(features)
    lines, kept, vectors = pl.pallas_call(
        stats_kernel,
        out_shape=[line(band), block(frames, rows), jax.ShapeDtypeStruct((8, channels), jnp.float32)],
        in_specs=[hbm] * 5,
        out_specs=[vmem] * 3,
        scratch_shapes=[dmas(frames + 4)],
        compiler_params=small,
        name="moments",
    )(stay(features), *[stay(v) for v in vectors])
    lines = spread_over(lines, "band")
    lines, pair, cross = pl.pallas_call(
        functools.partial(edges_kernel, members),
        out_shape=[line(tm), block(frames + 2, 2), block(frames + 2, 2)],
        in_specs=[vmem] * 3,
        out_specs=[vmem] * 3,
        compiler_params=small,
        name="edges",
    )(lines, kept, prev)
    pair = swapped(pair, "band", 0)
    cross = swapped(cross, "band", 1)
    lines = spread_over(lines, "tm")

    hidden, lines = pl.pallas_call(
        functools.partial(first_kernel, members),
        out_shape=[block(frames, rows + 2), line(band)],
        in_specs=[vmem] * 6 + [hbm],
        out_specs=[vmem, vmem],
        scratch_shapes=[held(frames + 2, rows + 4), pltpu.VMEM((9, 3, channels, outputs), jnp.bfloat16), dmas(9)],
        compiler_params=params,
        name="first_conv",
    )(kept, prev, pair, cross, lines, vectors, stay(taps(first_weight)))

    prev = next_frames(hidden)
    lines = spread_over(lines, "band")
    lines = pl.pallas_call(
        functools.partial(merge_kernel, members),
        out_shape=line(tm),
        in_specs=[vmem],
        out_specs=vmem,
        compiler_params=small,
        name="merge",
    )(lines)
    lines = spread_over(lines, "tm")

    return pl.pallas_call(
        functools.partial(second_kernel, members),
        out_shape=block(frames, rows),
        in_specs=[vmem] * 6,
        out_specs=hbm,
        scratch_shapes=[held(frames + 2, rows + 2), held(frames, rows), dmas(frames)],
        compiler_params=params,
        name="second_conv",
    )(hidden, prev, lines, vectors, kept, taps(second_weight))


def solution(mesh):
    in_specs = (P("tm", "band", None, None), P(), P(), P(), P(), P(), P())
    out_specs = P("tm", "band", None, None)
    return jax.shard_map(local, mesh=mesh, in_specs=in_specs, out_specs=out_specs, check_vma=False)
```

time: 85.8 us -> 78.2 us (0.911)
  blocking collectives: 28.1 us -> 53.3 us
  starting transfers between devices: 33.9 us -> 9.32 us
  local copies, waits for them, and re-layouts: 6.46 us -> 0.01 us
  waiting for transfers between devices: 1.91 us -> 0.01 us
    all_to_all x1 -> x4, blocking collectives: 28.1 us -> 53.3 us  [local(): lax.all_to_all(lines, axis, 0, 0, tiled=True)]
    all_to_all x1 -> x0, starting transfers between devices: 14.8 us -> none  [local(): lines = lax.all_to_all(lines, AXES, 0, 0, tiled=True)]
    ppermute x6 -> x4, starting transfers between devices: 19.1 us -> 9.32 us  [the longest x2 6.54 us: next_frames(): return lax.ppermute(value, 'tm', [(i, i + 1) for i in range(count - 1)])]
    unnamed x18 -> x2, local copies, waits for them, and re-layouts: 5.47 us -> 0.01 us
    ppermute x6 -> x4, waiting for transfers between devices: 1.91 us -> 0.01 us  [the longest x2 0.01 us: next_frames(): return lax.ppermute(value, 'tm', [(i, i + 1) for i in range(count - 1)])]
    slice x1 -> x0, local copies, waits for them, and re-layouts: 0.99 us -> none  [local(): top_rows = features[:, :2]]
    pallas_call x3 -> x5, Pallas kernels: 14.6 us -> 15.2 us  [the longest x1 8.26 us: local(): pl.pallas_call(functools.partial(first_kernel, members), out_shape=[block...]
  transfers between devices with their start and end apart: 7 -> 4, of which waited for: 1 -> 0; matrix products, arithmetic and copies ran while one was open for 1% -> 0% of each run, Pallas kernels for 2% -> 3%
where the time goes in v2:
time: 78.2 us; the launch traced here: 77.9 us
  blocking collectives  53.3 us (68%)
  Pallas kernels  15.2 us (19%)
  starting transfers between devices  9.32 us (12%)
    all_to_all x4, blocking collectives, local(): lax.all_to_all(lines, axis, 0, 0, tiled=True)  53.3 us
    pallas_call x1, Pallas kernels, local(): pl.pallas_call(functools.partial(first_kernel, members), out_shape=[block...  8.26 us
    ppermute x2, starting transfers between devices, next_frames(): return lax.ppermute(value, 'tm', [(i, i + 1) for i in range(count - 1)])  6.54 us
    pallas_call x1, Pallas kernels, local(): pl.pallas_call(functools.partial(second_kernel, members), out_shape=block...  4.88 us
    ppermute x2, starting transfers between devices, swapped(): return lax.ppermute(value, axis, pairs)  2.78 us
    pallas_call x1, Pallas kernels, local(): pl.pallas_call(stats_kernel, out_shape=[line(band), block(frames, rows),...  1.87 us
  transfers between devices with their start and end apart: 4, of which 0 were waited for; matrix products, arithmetic and copies ran while one was open for 0% of the time, Pallas kernels for 3%

profile of v2, /device:TPU:1, one launch (start us, length us, event | category | flops | bytes accessed | tf_op | source)
XLA Modules:
  0.0 77.9 jit_solution(10985701360429620587)
XLA Ops:
  0.0 0.0 copy-start
  0.0 4.3 %collective-permute-start = (bf16[2,8,64,256]{3,2,1,0:T(8,128)(2,1)}, bf16[2,8,64,256]{3,2,1,0:T(8,128)(2,1)S(1)}, u32[]{:S(2)}, u32[]{:S(2)}) collective-permute-start(bf16[2,8,64,256]{3,2,1,0:T(8,128)(2,1)} %x_ref.1), channel_id=1, source_target_pairs={{0,16},{16,32},{32,48},{48,64},{64,80},{80,96},{96,112},{112,128},... | collective-permute-start | bytes 1572872 | tf_op jit(solution)/shard_map/ppermute | solution.py:19
  4.3 1.9 %moments.1 = (f32[16,128]{1,0:T(8,128)S(1)}, bf16[2,8,64,256]{3,2,1,0:T(8,128)(2,1)S(1)}, f32[8,256]{1,0:T(8,128)S(1)}) custom-call(bf16[2,8,64,256]{3,2,1,0:T(8,128)(2,1)} %x_ref.1, f32[1,256]{1,0:T(1,128)} %bitcast.32, f32[1,256]{1,0:T(1,128)} %bitcast.33, f32[1,256]{1,0:T(1,128)} %bitcast.34, f32[1,256]{1,0:T(1,128)} %bitcast.35), custom_call_target="tpu_custom_call" | custom-call | tf_op jit(solution)/shard_map/moments/pallas_call | solution.py:256
  6.2 16.2 %all_to_all.44 = f32[16,1,128]{2,1,0:T(1,128)S(1)} all-to-all(f32[16,1,128]{2,1,0:T(1,128)S(1)} %bitcast.30), channel_id=1, replica_groups=mesh['tm'=16,'band'=16] {'band'}, dimensions={0} | all-to-all | bytes 16384 | tf_op jit(solution)/shard_map/all_to_all | solution.py:252
  22.4 0.0 collective-permute-done.prev_ref
  22.5 0.1 edges.1
  22.5 0.7 collective-permute-start.1
  23.3 2.1 %collective-permute-start.2 = (bf16[4,2,64,256]{3,2,1,0:T(8,128)(2,1)S(1)}, bf16[4,2,64,256]{3,2,1,0:T(8,128)(2,1)S(1)}, u32[]{:S(2)}, u32[]{:S(2)}) collective-permute-start(bf16[4,2,64,256]{3,2,1,0:T(8,128)(2,1)S(1)} %get-tuple-element.16), channel_id=1, source_target_pairs={{1,2},{2,1},{3,4},{4,3},{5,6},{6,5},{7,8},{8,7},{9,10},{10,9},{11,... | collective-permute-start | bytes 786440 | tf_op jit(solution)/shard_map/ppermute | solution.py:27
  25.3 12.6 %all_to_all.45 = f32[16,1,128]{2,1,0:T(1,128)S(1)} all-to-all(f32[16,1,128]{2,1,0:T(1,128)S(1)} %bitcast.28), channel_id=1, replica_groups=mesh['tm'=16,'band'=16] {'tm'}, dimensions={0} | all-to-all | bytes 16384 | tf_op jit(solution)/shard_map/all_to_all | solution.py:252
  38.0 0.0 collective-permute-done.1.pair_ref
  38.0 0.0 collective-permute-done.2.cross_ref
  38.0 8.3 %first_conv.1 = (bf16[2,10,64,256]{3,2,1,0:T(8,128)(2,1)S(1)}, f32[16,128]{1,0:T(8,128)S(1)}) custom-call(bf16[2,8,64,256]{3,2,1,0:T(8,128)(2,1)S(1)} %get-tuple-element.13.x_ref, bf16[2,8,64,256]{3,2,1,0:T(8,128)(2,1)S(1)} %collective-permute-done.prev_ref, bf16[4,2,64,256]{3,2,1,0:T(8,128)(2,1)S(1)} %collective-permute-done.1.pair_ref, ...), custom_call_target="tpu_custom_call" | custom-call | tf_op jit(solution)/shard_map/first_conv/pallas_call | solution.py:278
  46.3 2.2 %collective-permute-start.3 = (bf16[2,10,64,256]{3,2,1,0:T(8,128)(2,1)S(1)}, bf16[2,10,64,256]{3,2,1,0:T(8,128)(2,1)S(1)}, u32[]{:S(2)}, u32[]{:S(2)}) collective-permute-start(bf16[2,10,64,256]{3,2,1,0:T(8,128)(2,1)S(1)} %get-tuple-element.19.hidden_ref), channel_id=1, source_target_pairs={{0,16},{16,32},{32,48},{48,64},{64,80},{80,96},{96,112},{112,128},... | collective-permute-start | bytes 1966088 | tf_op jit(solution)/shard_map/ppermute | solution.py:19
  48.5 13.0 %all_to_all.46 = f32[16,1,128]{2,1,0:T(1,128)S(1)} all-to-all(f32[16,1,128]{2,1,0:T(1,128)S(1)} %bitcast.29), channel_id=1, replica_groups=mesh['tm'=16,'band'=16] {'band'}, dimensions={0} | all-to-all | bytes 16384 | tf_op jit(solution)/shard_map/all_to_all | solution.py:252
  61.5 0.1 merge.1
  61.6 11.4 %all_to_all.47 = f32[16,1,128]{2,1,0:T(1,128)S(1)} all-to-all(f32[16,1,128]{2,1,0:T(1,128)S(1)} %bitcast.27), channel_id=1, replica_groups=mesh['tm'=16,'band'=16] {'tm'}, dimensions={0} | all-to-all | bytes 16384 | tf_op jit(solution)/shard_map/all_to_all | solution.py:252
  73.0 0.0 collective-permute-done.3.prev_ref
  73.0 0.0 copy-done
  73.0 4.9 %second_conv.1 = bf16[2,8,64,256]{3,2,1,0:T(8,128)(2,1)} custom-call(bf16[2,10,64,256]{3,2,1,0:T(8,128)(2,1)S(1)} %get-tuple-element.19.hidden_ref, bf16[2,10,64,256]{3,2,1,0:T(8,128)(2,1)S(1)} %collective-permute-done.3.prev_ref, f32[16,128]{1,0:T(8,128)S(1)} %bitcast.24, f32[8,256]{1,0:T(8,128)S(1)} %get-tuple-element.18.params_ref, ...), custom_call_target="tpu_custom_call" | custom-call | tf_op jit(solution)/shard_map/second_conv/pallas_call | solution.py:300
Async XLA Ops:
  0.0 73.0 %copy-start = (bf16[3,3,3,256,256]{4,3,2,1,0:T(8,128)(2,1)S(1)}, bf16[3,3,3,256,256]{4,3,2,1,0:T(8,128)(2,1)}, u32[]{:S(2)}) copy-start(bf16[3,3,3,256,256]{4,3,2,1,0:T(8,128)(2,1)} %param.13) | copy-start | bytes 10616836
  0.0 22.4 %collective-permute-start = (bf16[2,8,64,256]{3,2,1,0:T(8,128)(2,1)}, bf16[2,8,64,256]{3,2,1,0:T(8,128)(2,1)S(1)}, u32[]{:S(2)}, u32[]{:S(2)}) collective-permute-start(bf16[2,8,64,256]{3,2,1,0:T(8,128)(2,1)} %x_ref.1), channel_id=1, source_target_pairs={{0,16},{16,32},{32,48},{48,64},{64,80},{80,96},{96,112},{112,128},... | collective-permute-start | bytes 1572872 | tf_op jit(solution)/shard_map/ppermute | solution.py:19
  22.5 15.4 %collective-permute-start.1 = (bf16[4,2,64,256]{3,2,1,0:T(8,128)(2,1)S(1)}, bf16[4,2,64,256]{3,2,1,0:T(8,128)(2,1)S(1)}, u32[]{:S(2)}, u32[]{:S(2)}) collective-permute-start(bf16[4,2,64,256]{3,2,1,0:T(8,128)(2,1)S(1)} %get-tuple-element.15), channel_id=1, source_target_pairs={{0,1},{1,0},{2,3},{3,2},{4,5},{5,4},{6,7},{7,6},{8,9},{9,8},{10,11... | collective-permute-start | bytes 786440 | tf_op jit(solution)/shard_map/ppermute | solution.py:27
  23.3 14.7 %collective-permute-start.2 = (bf16[4,2,64,256]{3,2,1,0:T(8,128)(2,1)S(1)}, bf16[4,2,64,256]{3,2,1,0:T(8,128)(2,1)S(1)}, u32[]{:S(2)}, u32[]{:S(2)}) collective-permute-start(bf16[4,2,64,256]{3,2,1,0:T(8,128)(2,1)S(1)} %get-tuple-element.16), channel_id=1, source_target_pairs={{1,2},{2,1},{3,4},{4,3},{5,6},{6,5},{7,8},{8,7},{9,10},{10,9},{11,... | collective-permute-start | bytes 786440 | tf_op jit(solution)/shard_map/ppermute | solution.py:27
  46.3 26.8 %collective-permute-start.3 = (bf16[2,10,64,256]{3,2,1,0:T(8,128)(2,1)S(1)}, bf16[2,10,64,256]{3,2,1,0:T(8,128)(2,1)S(1)}, u32[]{:S(2)}, u32[]{:S(2)}) collective-permute-start(bf16[2,10,64,256]{3,2,1,0:T(8,128)(2,1)S(1)} %get-tuple-element.19.hidden_ref), channel_id=1, source_target_pairs={{0,16},{16,32},{32,48},{48,64},{64,80},{80,96},{96,112},{112,128},... | collective-permute-start | bytes 1966088 | tf_op jit(solution)/shard_map/ppermute | solution.py:19

commit v3 on v2

--- a/solution.py
+++ b/solution.py
@@ -92,26 +92,21 @@
     return (half + half * jnp.tanh(half)).astype(jnp.bfloat16)
 
 
-def convolved(act_ref, weight_ref, frame, row_count):
+def convolved(act_ref, weight_of, frame, first_row, row_count):
     cols, channels = act_ref.shape[2:]
-    outputs = weight_ref.shape[-1]
     window = jnp.concatenate(
         [
-            act_ref[frame + i, j : j + row_count].reshape(row_count * cols, channels)
+            act_ref[frame + i, first_row + j : first_row + j + row_count].reshape(row_count * cols, channels)
             for i in range(3)
             for j in range(3)
         ],
         axis=-1,
     )
     left, middle, right = (
-        jnp.dot(
-            window,
-            weight_ref[:, k].reshape(9 * channels, outputs),
-            preferred_element_type=jnp.float32,
-        ).reshape(row_count, cols, outputs)
+        jnp.dot(window, weight_of(k), preferred_element_type=jnp.float32).reshape(row_count, cols, -1)
         for k in range(3)
     )
-    column = lax.broadcasted_iota(jnp.int32, (row_count, cols, outputs), 1)
+    column = lax.broadcasted_iota(jnp.int32, left.shape, 1)
     left = jnp.where(column == 0, left, pltpu.roll(left, 1, 1))
     right = jnp.where(column == cols - 1, right, pltpu.roll(right, cols - 1, 1))
     return left + middle + right
@@ -168,11 +163,8 @@
 
 
 def first_kernel(members, x_ref, prev_ref, pair_ref, cross_ref, lines_ref, params_ref, weight_ref,
-                 hidden_ref, line_ref, act_ref, held_ref, weight_sems):
+                 hidden_ref, line_ref, act_ref):
     frames, rows, cols, channels = x_ref.shape
-    weights = [pltpu.make_async_copy(weight_ref.at[t], held_ref.at[t], weight_sems.at[t]) for t in range(9)]
-    for copy in weights:
-        copy.start()
     leading, top, bottom = at_ends()
     even = lax.rem(lax.axis_index("band"), 2) == 0
     norm = scaling(lines_ref, params_ref, 0, members)
@@ -194,12 +186,15 @@
 
     for f in range(2 + frames):
         activate(f)
-    for copy in weights:
-        copy.wait()
+    weight_of = lambda k: weight_ref[:, k].reshape(9 * channels, -1)
     for f in range(frames):
-        hidden_ref[f] = convolved(act_ref, held_ref, f, rows + 2).astype(jnp.bfloat16)
+        hidden_ref[f] = convolved(act_ref, weight_of, f, 0, rows + 2).astype(jnp.bfloat16)
     reads = [functools.partial(lambda f, r: hidden_ref[f, r + 1], f, r) for f in range(frames) for r in range(rows)]
     line_ref[...] = jnp.broadcast_to(local_moments(reads, channels), line_ref.shape)
+
+
+def pieces(frames, rows):
+    return [(f, 0, rows) for f in range(frames - 1)] + [(frames - 1, 0, rows // 2), (frames - 1, rows // 2, rows // 2)]
 
 
 def second_kernel(members, hidden_ref, prev_ref, lines_ref, params_ref, x_ref, weight_ref, out_ref,
@@ -223,10 +218,13 @@
 
     for f in range(2 + frames):
         activate(f)
+    weight_of = lambda k: weight_ref[:, k].reshape(9 * channels, -1)
     outs = []
-    for f in range(frames):
-        made_ref[f] = (x_ref[f].astype(jnp.float32) + convolved(act_ref, weight_ref, f, rows)).astype(jnp.bfloat16)
-        outs.append(pltpu.make_async_copy(made_ref.at[f], out_ref.at[f], out_sems.at[f]))
+    for f, first, count in pieces(frames, rows):
+        at = f, pl.ds(first, count)
+        summed = x_ref[at].astype(jnp.float32) + convolved(act_ref, weight_of, f, first, count)
+        made_ref[at] = summed.astype(jnp.bfloat16)
+        outs.append(pltpu.make_async_copy(made_ref.at[at], out_ref.at[at], out_sems.at[len(outs)]))
         outs[-1].start()
     for copy in outs:
         copy.wait()
@@ -269,6 +267,7 @@
         in_specs=[vmem] * 3,
         out_specs=[vmem] * 3,
         compiler_params=small,
+        cost_estimate=pl.CostEstimate(flops=4 * 10**9, bytes_accessed=0, transcendentals=0),
         name="edges",
     )(lines, kept, prev)
     pair = swapped(pair, "band", 0)
@@ -278,12 +277,12 @@
     hidden, lines = pl.pallas_call(
         functools.partial(first_kernel, members),
         out_shape=[block(frames, rows + 2), line(band)],
-        in_specs=[vmem] * 6 + [hbm],
+        in_specs=[vmem] * 7,
         out_specs=[vmem, vmem],
-        scratch_shapes=[held(frames + 2, rows + 4), pltpu.VMEM((9, 3, channels, outputs), jnp.bfloat16), dmas(9)],
+        scratch_shapes=[held(frames + 2, rows + 4)],
         compiler_params=params,
         name="first_conv",
-    )(kept, prev, pair, cross, lines, vectors, stay(taps(first_weight)))
+    )(kept, prev, pair, cross, lines, vectors, taps(first_weight))
 
     prev = next_frames(hidden)
     lines = spread_over(lines, "band")
@@ -302,7 +301,7 @@
         out_shape=block(frames, rows),
         in_specs=[vmem] * 6,
         out_specs=hbm,
-        scratch_shapes=[held(frames + 2, rows + 2), held(frames, rows), dmas(frames)],
+        scratch_shapes=[held(frames + 2, rows + 2), held(frames, rows), dmas(frames + 1)],
         compiler_params=params,
         name="second_conv",
     )(hidden, prev, lines, vectors, kept, taps(second_weight))

time: 78.2 us -> 75.8 us (0.969)
  Pallas kernels: 15.2 us -> 12.7 us
    pallas_call x1, Pallas kernels: 8.26 us -> 5.72 us  [local(): pl.pallas_call(functools.partial(first_kernel, members), out_shape=[block...]
where the time goes in v3:
time: 75.8 us; the launch traced here: 75.5 us
  blocking collectives  53.3 us (70%)
  Pallas kernels  12.7 us (17%)
  starting transfers between devices  9.35 us (12%)
    all_to_all x4, blocking collectives, local(): lax.all_to_all(lines, axis, 0, 0, tiled=True)  53.3 us
    ppermute x2, starting transfers between devices, next_frames(): return lax.ppermute(value, 'tm', [(i, i + 1) for i in range(count - 1)])  6.3 us
    pallas_call x1, Pallas kernels, local(): pl.pallas_call(functools.partial(first_kernel, members), out_shape=[block...  5.72 us
    pallas_call x1, Pallas kernels, local(): pl.pallas_call(functools.partial(second_kernel, members), out_shape=block...  4.95 us
    ppermute x2, starting transfers between devices, swapped(): return lax.ppermute(value, axis, pairs)  3.05 us
    pallas_call x1, Pallas kernels, local(): pl.pallas_call(stats_kernel, out_shape=[line(band), block(frames, rows),...  1.87 us
  transfers between devices with their start and end apart: 4, of which 0 were waited for; matrix products, arithmetic and copies ran while one was open for 0% of the time, Pallas kernels for 3%

profile of v3, /device:TPU:1, one launch (start us, length us, event | category | flops | bytes accessed | tf_op | source)
XLA Modules:
  0.0 75.5 jit_solution(11361980075250764279)
XLA Ops:
  0.0 4.0 %collective-permute-start = (bf16[2,8,64,256]{3,2,1,0:T(8,128)(2,1)}, bf16[2,8,64,256]{3,2,1,0:T(8,128)(2,1)S(1)}, u32[]{:S(2)}, u32[]{:S(2)}) collective-permute-start(bf16[2,8,64,256]{3,2,1,0:T(8,128)(2,1)} %x_ref.1), channel_id=1, source_target_pairs={{0,16},{16,32},{32,48},{48,64},{64,80},{80,96},{96,112},{112,128},... | collective-permute-start | bytes 1572872 | tf_op jit(solution)/shard_map/ppermute | solution.py:19
  4.1 1.9 %moments.1 = (f32[16,128]{1,0:T(8,128)S(1)}, bf16[2,8,64,256]{3,2,1,0:T(8,128)(2,1)S(1)}, f32[8,256]{1,0:T(8,128)S(1)}) custom-call(bf16[2,8,64,256]{3,2,1,0:T(8,128)(2,1)} %x_ref.1, f32[1,256]{1,0:T(1,128)} %bitcast.32, f32[1,256]{1,0:T(1,128)} %bitcast.33, f32[1,256]{1,0:T(1,128)} %bitcast.34, f32[1,256]{1,0:T(1,128)} %bitcast.35), custom_call_target="tpu_custom_call" | custom-call | tf_op jit(solution)/shard_map/moments/pallas_call | solution.py:254
  5.9 16.2 %all_to_all.44 = f32[16,1,128]{2,1,0:T(1,128)S(1)} all-to-all(f32[16,1,128]{2,1,0:T(1,128)S(1)} %bitcast.31), channel_id=1, replica_groups=mesh['tm'=16,'band'=16] {'band'}, dimensions={0} | all-to-all | bytes 16384 | tf_op jit(solution)/shard_map/all_to_all | solution.py:250
  22.2 0.0 collective-permute-done.prev_ref
  22.2 0.0 copy-start
  22.2 0.1 edges.1
  22.3 0.0 copy-start.1
  22.3 0.7 collective-permute-start.1
  23.0 2.3 %collective-permute-start.2 = (bf16[4,2,64,256]{3,2,1,0:T(8,128)(2,1)S(1)}, bf16[4,2,64,256]{3,2,1,0:T(8,128)(2,1)S(1)}, u32[]{:S(2)}, u32[]{:S(2)}) collective-permute-start(bf16[4,2,64,256]{3,2,1,0:T(8,128)(2,1)S(1)} %get-tuple-element.16), channel_id=1, source_target_pairs={{1,2},{2,1},{3,4},{4,3},{5,6},{6,5},{7,8},{8,7},{9,10},{10,9},{11,... | collective-permute-start | bytes 786440 | tf_op jit(solution)/shard_map/ppermute | solution.py:27
  25.3 12.6 %all_to_all.45 = f32[16,1,128]{2,1,0:T(1,128)S(1)} all-to-all(f32[16,1,128]{2,1,0:T(1,128)S(1)} %bitcast.28), channel_id=1, replica_groups=mesh['tm'=16,'band'=16] {'tm'}, dimensions={0} | all-to-all | bytes 16384 | tf_op jit(solution)/shard_map/all_to_all | solution.py:250
  38.0 0.0 collective-permute-done.1.pair_ref
  38.0 0.0 collective-permute-done.2.cross_ref
  38.0 0.0 copy-done
  38.0 5.7 %first_conv.1 = (bf16[2,10,64,256]{3,2,1,0:T(8,128)(2,1)S(1)}, f32[16,128]{1,0:T(8,128)S(1)}) custom-call(bf16[2,8,64,256]{3,2,1,0:T(8,128)(2,1)S(1)} %get-tuple-element.13.x_ref, bf16[2,8,64,256]{3,2,1,0:T(8,128)(2,1)S(1)} %collective-permute-done.prev_ref, bf16[4,2,64,256]{3,2,1,0:T(8,128)(2,1)S(1)} %collective-permute-done.1.pair_ref, ...), custom_call_target="tpu_custom_call" | custom-call | tf_op jit(solution)/shard_map/first_conv/pallas_call | solution.py:277
  43.7 2.2 %collective-permute-start.3 = (bf16[2,10,64,256]{3,2,1,0:T(8,128)(2,1)S(1)}, bf16[2,10,64,256]{3,2,1,0:T(8,128)(2,1)S(1)}, u32[]{:S(2)}, u32[]{:S(2)}) collective-permute-start(bf16[2,10,64,256]{3,2,1,0:T(8,128)(2,1)S(1)} %get-tuple-element.19.hidden_ref), channel_id=1, source_target_pairs={{0,16},{16,32},{32,48},{48,64},{64,80},{80,96},{96,112},{112,128},... | collective-permute-start | bytes 1966088 | tf_op jit(solution)/shard_map/ppermute | solution.py:19
  46.0 13.0 %all_to_all.46 = f32[16,1,128]{2,1,0:T(1,128)S(1)} all-to-all(f32[16,1,128]{2,1,0:T(1,128)S(1)} %bitcast.29), channel_id=1, replica_groups=mesh['tm'=16,'band'=16] {'band'}, dimensions={0} | all-to-all | bytes 16384 | tf_op jit(solution)/shard_map/all_to_all | solution.py:250
  59.0 0.1 merge.1
  59.1 11.4 %all_to_all.47 = f32[16,1,128]{2,1,0:T(1,128)S(1)} all-to-all(f32[16,1,128]{2,1,0:T(1,128)S(1)} %bitcast.27), channel_id=1, replica_groups=mesh['tm'=16,'band'=16] {'tm'}, dimensions={0} | all-to-all | bytes 16384 | tf_op jit(solution)/shard_map/all_to_all | solution.py:250
  70.5 0.0 collective-permute-done.3.prev_ref
  70.5 0.0 copy-done.1
  70.5 5.0 %second_conv.1 = bf16[2,8,64,256]{3,2,1,0:T(8,128)(2,1)} custom-call(bf16[2,10,64,256]{3,2,1,0:T(8,128)(2,1)S(1)} %get-tuple-element.19.hidden_ref, bf16[2,10,64,256]{3,2,1,0:T(8,128)(2,1)S(1)} %collective-permute-done.3.prev_ref, f32[16,128]{1,0:T(8,128)S(1)} %bitcast.25, f32[8,256]{1,0:T(8,128)S(1)} %get-tuple-element.18.params_ref, ...), custom_call_target="tpu_custom_call" | custom-call | tf_op jit(solution)/shard_map/second_conv/pallas_call | solution.py:299
Async XLA Ops:
  0.0 22.2 %collective-permute-start = (bf16[2,8,64,256]{3,2,1,0:T(8,128)(2,1)}, bf16[2,8,64,256]{3,2,1,0:T(8,128)(2,1)S(1)}, u32[]{:S(2)}, u32[]{:S(2)}) collective-permute-start(bf16[2,8,64,256]{3,2,1,0:T(8,128)(2,1)} %x_ref.1), channel_id=1, source_target_pairs={{0,16},{16,32},{32,48},{48,64},{64,80},{80,96},{96,112},{112,128},... | collective-permute-start | bytes 1572872 | tf_op jit(solution)/shard_map/ppermute | solution.py:19
  22.2 15.8 %copy-start = (bf16[3,3,3,256,256]{4,3,2,1,0:T(8,128)(2,1)S(1)}, bf16[3,3,3,256,256]{4,3,2,1,0:T(8,128)(2,1)}, u32[]{:S(2)}) copy-start(bf16[3,3,3,256,256]{4,3,2,1,0:T(8,128)(2,1)} %param.10) | copy-start | bytes 10616836
  22.3 48.2 %copy-start.1 = (bf16[3,3,3,256,256]{4,3,2,1,0:T(8,128)(2,1)S(1)}, bf16[3,3,3,256,256]{4,3,2,1,0:T(8,128)(2,1)}, u32[]{:S(2)}) copy-start(bf16[3,3,3,256,256]{4,3,2,1,0:T(8,128)(2,1)} %param.13) | copy-start | bytes 10616836
  22.3 15.7 %collective-permute-start.1 = (bf16[4,2,64,256]{3,2,1,0:T(8,128)(2,1)S(1)}, bf16[4,2,64,256]{3,2,1,0:T(8,128)(2,1)S(1)}, u32[]{:S(2)}, u32[]{:S(2)}) collective-permute-start(bf16[4,2,64,256]{3,2,1,0:T(8,128)(2,1)S(1)} %get-tuple-element.15), channel_id=1, source_target_pairs={{0,1},{1,0},{2,3},{3,2},{4,5},{5,4},{6,7},{7,6},{8,9},{9,8},{10,11... | collective-permute-start | bytes 786440 | tf_op jit(solution)/shard_map/ppermute | solution.py:27
  23.0 15.0 %collective-permute-start.2 = (bf16[4,2,64,256]{3,2,1,0:T(8,128)(2,1)S(1)}, bf16[4,2,64,256]{3,2,1,0:T(8,128)(2,1)S(1)}, u32[]{:S(2)}, u32[]{:S(2)}) collective-permute-start(bf16[4,2,64,256]{3,2,1,0:T(8,128)(2,1)S(1)} %get-tuple-element.16), channel_id=1, source_target_pairs={{1,2},{2,1},{3,4},{4,3},{5,6},{6,5},{7,8},{8,7},{9,10},{10,9},{11,... | collective-permute-start | bytes 786440 | tf_op jit(solution)/shard_map/ppermute | solution.py:27
  43.7 26.8 %collective-permute-start.3 = (bf16[2,10,64,256]{3,2,1,0:T(8,128)(2,1)S(1)}, bf16[2,10,64,256]{3,2,1,0:T(8,128)(2,1)S(1)}, u32[]{:S(2)}, u32[]{:S(2)}) collective-permute-start(bf16[2,10,64,256]{3,2,1,0:T(8,128)(2,1)S(1)} %get-tuple-element.19.hidden_ref), channel_id=1, source_target_pairs={{0,16},{16,32},{32,48},{48,64},{64,80},{80,96},{96,112},{112,128},... | collective-permute-start | bytes 1966088 | tf_op jit(solution)/shard_map/ppermute | solution.py:19

commit v4 on v3

--- a/solution.py
+++ b/solution.py
@@ -89,27 +89,45 @@
 
 def activated(x, centre, scale, offset):
     half = (x.astype(jnp.float32) - centre) * scale + offset
-    return (half + half * jnp.tanh(half)).astype(jnp.bfloat16)
-
-
-def convolved(act_ref, weight_of, frame, first_row, row_count):
+    return half + half * jnp.tanh(half)
+
+
+def mixed_frames(act_ref, row, frames):
+    first, second, third, fourth = frames
+    for part, value in enumerate((first - third, second + third, third - second, second - fourth)):
+        act_ref[part, row] = value.astype(jnp.bfloat16)
+
+
+def mix_weight(weight_ref, mixed_ref):
+    for t in range(9):
+        first, middle, last = (weight_ref[3 * i + t // 3, t % 3].astype(jnp.float32) for i in range(3))
+        ends = 0.5 * (first + last)
+        middle = 0.5 * middle
+        mixed_ref[0, t // 3, t % 3] = (ends + middle).astype(jnp.bfloat16)
+        mixed_ref[1, t // 3, t % 3] = (ends - middle).astype(jnp.bfloat16)
+
+
+def convolved(act_ref, weight_ref, mixed_ref, row_count):
     cols, channels = act_ref.shape[2:]
-    window = jnp.concatenate(
-        [
-            act_ref[frame + i, first_row + j : first_row + j + row_count].reshape(row_count * cols, channels)
-            for i in range(3)
-            for j in range(3)
-        ],
-        axis=-1,
-    )
-    left, middle, right = (
-        jnp.dot(window, weight_of(k), preferred_element_type=jnp.float32).reshape(row_count, cols, -1)
-        for k in range(3)
-    )
-    column = lax.broadcasted_iota(jnp.int32, left.shape, 1)
-    left = jnp.where(column == 0, left, pltpu.roll(left, 1, 1))
-    right = jnp.where(column == cols - 1, right, pltpu.roll(right, cols - 1, 1))
-    return left + middle + right
+    windows = [
+        jnp.concatenate([act_ref[part, j : j + row_count].reshape(row_count * cols, channels) for j in range(3)], axis=-1)
+        for part in range(4)
+    ]
+    early = late = None
+    for k in range(3):
+        taps = weight_ref[0:3, k], mixed_ref[0, :, k], mixed_ref[1, :, k], weight_ref[6:9, k]
+        first, second, third, fourth = (
+            jnp.dot(window, tap.reshape(3 * channels, -1), preferred_element_type=jnp.float32).reshape(row_count, cols, -1)
+            for window, tap in zip(windows, taps)
+        )
+        pair = first + second + third, second - third - fourth
+        if k != 1:
+            column = lax.broadcasted_iota(jnp.int32, first.shape, 1)
+            edge, by = (0, 1) if k == 0 else (cols - 1, cols - 1)
+            pair = [jnp.where(column == edge, value, pltpu.roll(value, by, 1)) for value in pair]
+        early = pair[0] if early is None else early + pair[0]
+        late = pair[1] if late is None else late + pair[1]
+    return early, late
 
 
 def places(rows):
@@ -163,7 +181,7 @@
 
 
 def first_kernel(members, x_ref, prev_ref, pair_ref, cross_ref, lines_ref, params_ref, weight_ref,
-                 hidden_ref, line_ref, act_ref):
+                 hidden_ref, line_ref, act_ref, mixed_ref):
     frames, rows, cols, channels = x_ref.shape
     leading, top, bottom = at_ends()
     even = lax.rem(lax.axis_index("band"), 2) == 0
@@ -179,26 +197,19 @@
         outer = jnp.where(even, pair_ref[f, r - rows - 2], cross_ref[f, r - rows - 2])
         return jnp.where(bottom, inner[f % 2, rows - 1], outer) if r == rows + 2 else outer
 
-    def activate(f):
-        for r in range(rows + 4):
-            x = jnp.where(leading, row_of(2, r), row_of(f, r)) if f < 2 else row_of(f, r)
-            act_ref[f, r] = activated(x, *norm)
-
-    for f in range(2 + frames):
-        activate(f)
-    weight_of = lambda k: weight_ref[:, k].reshape(9 * channels, -1)
-    for f in range(frames):
-        hidden_ref[f] = convolved(act_ref, weight_of, f, 0, rows + 2).astype(jnp.bfloat16)
+    for r in range(rows + 4):
+        own = [row_of(f, r) for f in (2, 3)]
+        before = [jnp.where(leading, own[0], row_of(f, r)) for f in (0, 1)]
+        mixed_frames(act_ref, r, [activated(x, *norm) for x in before + own])
+    mix_weight(weight_ref, mixed_ref)
+    for f, value in enumerate(convolved(act_ref, weight_ref, mixed_ref, rows + 2)):
+        hidden_ref[f] = value.astype(jnp.bfloat16)
     reads = [functools.partial(lambda f, r: hidden_ref[f, r + 1], f, r) for f in range(frames) for r in range(rows)]
     line_ref[...] = jnp.broadcast_to(local_moments(reads, channels), line_ref.shape)
 
 
-def pieces(frames, rows):
-    return [(f, 0, rows) for f in range(frames - 1)] + [(frames - 1, 0, rows // 2), (frames - 1, rows // 2, rows // 2)]
-
-
 def second_kernel(members, hidden_ref, prev_ref, lines_ref, params_ref, x_ref, weight_ref, out_ref,
-                  act_ref, made_ref, out_sems):
+                  act_ref, mixed_ref, made_ref, out_sems):
     frames, rows, cols, channels = x_ref.shape
     leading, top, bottom = at_ends()
     norm = scaling(lines_ref, params_ref, 1, members)
@@ -211,20 +222,15 @@
             return jnp.where(bottom, ref[f % 2, rows], ref[f % 2, rows + 1])
         return ref[f % 2, r]
 
-    def activate(f):
-        for r in range(rows + 2):
-            x = jnp.where(leading, row_of(2, r), row_of(f, r)) if f < 2 else row_of(f, r)
-            act_ref[f, r] = activated(x, *norm)
-
-    for f in range(2 + frames):
-        activate(f)
-    weight_of = lambda k: weight_ref[:, k].reshape(9 * channels, -1)
+    for r in range(rows + 2):
+        own = [row_of(f, r) for f in (2, 3)]
+        before = [jnp.where(leading, own[0], row_of(f, r)) for f in (0, 1)]
+        mixed_frames(act_ref, r, [activated(x, *norm) for x in before + own])
+    mix_weight(weight_ref, mixed_ref)
     outs = []
-    for f, first, count in pieces(frames, rows):
-        at = f, pl.ds(first, count)
-        summed = x_ref[at].astype(jnp.float32) + convolved(act_ref, weight_of, f, first, count)
-        made_ref[at] = summed.astype(jnp.bfloat16)
-        outs.append(pltpu.make_async_copy(made_ref.at[at], out_ref.at[at], out_sems.at[len(outs)]))
+    for f, value in enumerate(convolved(act_ref, weight_ref, mixed_ref, rows)):
+        made_ref[f] = (x_ref[f].astype(jnp.float32) + value).astype(jnp.bfloat16)
+        outs.append(pltpu.make_async_copy(made_ref.at[f], out_ref.at[f], out_sems.at[f]))
         outs[-1].start()
     for copy in outs:
         copy.wait()
@@ -246,6 +252,7 @@
     held = lambda f, r: pltpu.VMEM((f, r, cols, channels), jnp.bfloat16)
     dmas = lambda count: pltpu.SemaphoreType.DMA((count,))
     taps = lambda weight: weight.reshape(9, 3, channels, outputs)
+    mixed = pltpu.VMEM((2, 3, 3, channels, outputs), jnp.bfloat16)
     stay = lambda value: pltpu.with_memory_space_constraint(value, pltpu.HBM)
     spread_over = lambda lines, axis: lax.all_to_all(lines, axis, 0, 0, tiled=True)
     vectors = [v.reshape(1, channels) for v in (first_gain, first_shift, second_gain, second_shift)]
@@ -279,7 +286,7 @@
         out_shape=[block(frames, rows + 2), line(band)],
         in_specs=[vmem] * 7,
         out_specs=[vmem, vmem],
-        scratch_shapes=[held(frames + 2, rows + 4)],
+        scratch_shapes=[held(4, rows + 4), mixed],
         compiler_params=params,
         name="first_conv",
     )(kept, prev, pair, cross, lines, vectors, taps(first_weight))
@@ -301,7 +308,7 @@
         out_shape=block(frames, rows),
         in_specs=[vmem] * 6,
         out_specs=hbm,
-        scratch_shapes=[held(frames + 2, rows + 2), held(frames, rows), dmas(frames + 1)],
+        scratch_shapes=[held(4, rows + 2), mixed, held(frames, rows), dmas(frames)],
         compiler_params=params,
         name="second_conv",
     )(hidden, prev, lines, vectors, kept, taps(second_weight))

time: 75.8 us -> 74.4 us (0.982)
  Pallas kernels: 12.7 us -> 11.3 us
    pallas_call x1, Pallas kernels: 5.72 us -> 4.91 us  [local(): pl.pallas_call(functools.partial(first_kernel, members), out_shape=[block...]
where the time goes in v4:
time: 74.4 us; the launch traced here: 74.1 us
  blocking collectives  53.3 us (72%)
  Pallas kernels  11.3 us (15%)
  starting transfers between devices  9.34 us (13%)
    all_to_all x4, blocking collectives, local(): lax.all_to_all(lines, axis, 0, 0, tiled=True)  53.3 us
    ppermute x2, starting transfers between devices, next_frames(): return lax.ppermute(value, 'tm', [(i, i + 1) for i in range(count - 1)])  6.29 us
    pallas_call x1, Pallas kernels, local(): pl.pallas_call(functools.partial(first_kernel, members), out_shape=[block...  4.91 us
    pallas_call x1, Pallas kernels, local(): pl.pallas_call(functools.partial(second_kernel, members), out_shape=block...  4.38 us
    ppermute x2, starting transfers between devices, swapped(): return lax.ppermute(value, axis, pairs)  3.05 us
    pallas_call x1, Pallas kernels, local(): pl.pallas_call(stats_kernel, out_shape=[line(band), block(frames, rows),...  1.87 us
  transfers between devices with their start and end apart: 4, of which 0 were waited for; matrix products, arithmetic and copies ran while one was open for 0% of the time, Pallas kernels for 3%

profile of v4, /device:TPU:1, one launch (start us, length us, event | category | flops | bytes accessed | tf_op | source)
XLA Modules:
  0.0 74.1 jit_solution(13509777470343876462)
XLA Ops:
  0.0 4.0 %collective-permute-start = (bf16[2,8,64,256]{3,2,1,0:T(8,128)(2,1)}, bf16[2,8,64,256]{3,2,1,0:T(8,128)(2,1)S(1)}, u32[]{:S(2)}, u32[]{:S(2)}) collective-permute-start(bf16[2,8,64,256]{3,2,1,0:T(8,128)(2,1)} %x_ref.1), channel_id=1, source_target_pairs={{0,16},{16,32},{32,48},{48,64},{64,80},{80,96},{96,112},{112,128},... | collective-permute-start | bytes 1572872 | tf_op jit(solution)/shard_map/ppermute | solution.py:19
  4.1 1.9 %moments.1 = (f32[16,128]{1,0:T(8,128)S(1)}, bf16[2,8,64,256]{3,2,1,0:T(8,128)(2,1)S(1)}, f32[8,256]{1,0:T(8,128)S(1)}) custom-call(bf16[2,8,64,256]{3,2,1,0:T(8,128)(2,1)} %x_ref.1, f32[1,256]{1,0:T(1,128)} %bitcast.32, f32[1,256]{1,0:T(1,128)} %bitcast.33, f32[1,256]{1,0:T(1,128)} %bitcast.34, f32[1,256]{1,0:T(1,128)} %bitcast.35), custom_call_target="tpu_custom_call" | custom-call | tf_op jit(solution)/shard_map/moments/pallas_call | solution.py:261
  5.9 16.2 %all_to_all.44 = f32[16,1,128]{2,1,0:T(1,128)S(1)} all-to-all(f32[16,1,128]{2,1,0:T(1,128)S(1)} %bitcast.31), channel_id=1, replica_groups=mesh['tm'=16,'band'=16] {'band'}, dimensions={0} | all-to-all | bytes 16384 | tf_op jit(solution)/shard_map/all_to_all | solution.py:257
  22.2 0.0 collective-permute-done.prev_ref
  22.2 0.0 copy-start
  22.2 0.1 edges.1
  22.3 0.0 copy-start.1
  22.3 0.7 collective-permute-start.1
  23.0 2.3 %collective-permute-start.2 = (bf16[4,2,64,256]{3,2,1,0:T(8,128)(2,1)S(1)}, bf16[4,2,64,256]{3,2,1,0:T(8,128)(2,1)S(1)}, u32[]{:S(2)}, u32[]{:S(2)}) collective-permute-start(bf16[4,2,64,256]{3,2,1,0:T(8,128)(2,1)S(1)} %get-tuple-element.16), channel_id=1, source_target_pairs={{1,2},{2,1},{3,4},{4,3},{5,6},{6,5},{7,8},{8,7},{9,10},{10,9},{11,... | collective-permute-start | bytes 786440 | tf_op jit(solution)/shard_map/ppermute | solution.py:27
  25.3 12.6 %all_to_all.45 = f32[16,1,128]{2,1,0:T(1,128)S(1)} all-to-all(f32[16,1,128]{2,1,0:T(1,128)S(1)} %bitcast.28), channel_id=1, replica_groups=mesh['tm'=16,'band'=16] {'tm'}, dimensions={0} | all-to-all | bytes 16384 | tf_op jit(solution)/shard_map/all_to_all | solution.py:257
  38.0 0.0 collective-permute-done.1.pair_ref
  38.0 0.0 collective-permute-done.2.cross_ref
  38.0 0.0 copy-done
  38.0 4.9 %first_conv.1 = (bf16[2,10,64,256]{3,2,1,0:T(8,128)(2,1)S(1)}, f32[16,128]{1,0:T(8,128)S(1)}) custom-call(bf16[2,8,64,256]{3,2,1,0:T(8,128)(2,1)S(1)} %get-tuple-element.13.x_ref, bf16[2,8,64,256]{3,2,1,0:T(8,128)(2,1)S(1)} %collective-permute-done.prev_ref, bf16[4,2,64,256]{3,2,1,0:T(8,128)(2,1)S(1)} %collective-permute-done.1.pair_ref, ...), custom_call_target="tpu_custom_call" | custom-call | tf_op jit(solution)/shard_map/first_conv/pallas_call | solution.py:284
  42.9 2.2 %collective-permute-start.3 = (bf16[2,10,64,256]{3,2,1,0:T(8,128)(2,1)S(1)}, bf16[2,10,64,256]{3,2,1,0:T(8,128)(2,1)S(1)}, u32[]{:S(2)}, u32[]{:S(2)}) collective-permute-start(bf16[2,10,64,256]{3,2,1,0:T(8,128)(2,1)S(1)} %get-tuple-element.19.hidden_ref), channel_id=1, source_target_pairs={{0,16},{16,32},{32,48},{48,64},{64,80},{80,96},{96,112},{112,128},... | collective-permute-start | bytes 1966088 | tf_op jit(solution)/shard_map/ppermute | solution.py:19
  45.2 13.0 %all_to_all.46 = f32[16,1,128]{2,1,0:T(1,128)S(1)} all-to-all(f32[16,1,128]{2,1,0:T(1,128)S(1)} %bitcast.29), channel_id=1, replica_groups=mesh['tm'=16,'band'=16] {'band'}, dimensions={0} | all-to-all | bytes 16384 | tf_op jit(solution)/shard_map/all_to_all | solution.py:257
  58.2 0.1 merge.1
  58.3 11.4 %all_to_all.47 = f32[16,1,128]{2,1,0:T(1,128)S(1)} all-to-all(f32[16,1,128]{2,1,0:T(1,128)S(1)} %bitcast.27), channel_id=1, replica_groups=mesh['tm'=16,'band'=16] {'tm'}, dimensions={0} | all-to-all | bytes 16384 | tf_op jit(solution)/shard_map/all_to_all | solution.py:257
  69.7 0.0 collective-permute-done.3.prev_ref
  69.7 0.0 copy-done.1
  69.7 4.4 %second_conv.1 = bf16[2,8,64,256]{3,2,1,0:T(8,128)(2,1)} custom-call(bf16[2,10,64,256]{3,2,1,0:T(8,128)(2,1)S(1)} %get-tuple-element.19.hidden_ref, bf16[2,10,64,256]{3,2,1,0:T(8,128)(2,1)S(1)} %collective-permute-done.3.prev_ref, f32[16,128]{1,0:T(8,128)S(1)} %bitcast.25, f32[8,256]{1,0:T(8,128)S(1)} %get-tuple-element.18.params_ref, ...), custom_call_target="tpu_custom_call" | custom-call | tf_op jit(solution)/shard_map/second_conv/pallas_call | solution.py:306
Async XLA Ops:
  0.0 22.2 %collective-permute-start = (bf16[2,8,64,256]{3,2,1,0:T(8,128)(2,1)}, bf16[2,8,64,256]{3,2,1,0:T(8,128)(2,1)S(1)}, u32[]{:S(2)}, u32[]{:S(2)}) collective-permute-start(bf16[2,8,64,256]{3,2,1,0:T(8,128)(2,1)} %x_ref.1), channel_id=1, source_target_pairs={{0,16},{16,32},{32,48},{48,64},{64,80},{80,96},{96,112},{112,128},... | collective-permute-start | bytes 1572872 | tf_op jit(solution)/shard_map/ppermute | solution.py:19
  22.2 15.8 %copy-start = (bf16[3,3,3,256,256]{4,3,2,1,0:T(8,128)(2,1)S(1)}, bf16[3,3,3,256,256]{4,3,2,1,0:T(8,128)(2,1)}, u32[]{:S(2)}) copy-start(bf16[3,3,3,256,256]{4,3,2,1,0:T(8,128)(2,1)} %param.10) | copy-start | bytes 10616836
  22.3 47.4 %copy-start.1 = (bf16[3,3,3,256,256]{4,3,2,1,0:T(8,128)(2,1)S(1)}, bf16[3,3,3,256,256]{4,3,2,1,0:T(8,128)(2,1)}, u32[]{:S(2)}) copy-start(bf16[3,3,3,256,256]{4,3,2,1,0:T(8,128)(2,1)} %param.13) | copy-start | bytes 10616836
  22.3 15.7 %collective-permute-start.1 = (bf16[4,2,64,256]{3,2,1,0:T(8,128)(2,1)S(1)}, bf16[4,2,64,256]{3,2,1,0:T(8,128)(2,1)S(1)}, u32[]{:S(2)}, u32[]{:S(2)}) collective-permute-start(bf16[4,2,64,256]{3,2,1,0:T(8,128)(2,1)S(1)} %get-tuple-element.15), channel_id=1, source_target_pairs={{0,1},{1,0},{2,3},{3,2},{4,5},{5,4},{6,7},{7,6},{8,9},{9,8},{10,11... | collective-permute-start | bytes 786440 | tf_op jit(solution)/shard_map/ppermute | solution.py:27
  23.0 15.0 %collective-permute-start.2 = (bf16[4,2,64,256]{3,2,1,0:T(8,128)(2,1)S(1)}, bf16[4,2,64,256]{3,2,1,0:T(8,128)(2,1)S(1)}, u32[]{:S(2)}, u32[]{:S(2)}) collective-permute-start(bf16[4,2,64,256]{3,2,1,0:T(8,128)(2,1)S(1)} %get-tuple-element.16), channel_id=1, source_target_pairs={{1,2},{2,1},{3,4},{4,3},{5,6},{6,5},{7,8},{8,7},{9,10},{10,9},{11,... | collective-permute-start | bytes 786440 | tf_op jit(solution)/shard_map/ppermute | solution.py:27
  42.9 26.8 %collective-permute-start.3 = (bf16[2,10,64,256]{3,2,1,0:T(8,128)(2,1)S(1)}, bf16[2,10,64,256]{3,2,1,0:T(8,128)(2,1)S(1)}, u32[]{:S(2)}, u32[]{:S(2)}) collective-permute-start(bf16[2,10,64,256]{3,2,1,0:T(8,128)(2,1)S(1)} %get-tuple-element.19.hidden_ref), channel_id=1, source_target_pairs={{0,16},{16,32},{32,48},{48,64},{64,80},{80,96},{96,112},{112,128},... | collective-permute-start | bytes 1966088 | tf_op jit(solution)/shard_map/ppermute | solution.py:19

commit v5 on v4

--- a/solution.py
+++ b/solution.py
@@ -11,7 +11,6 @@
 EPSILON = 1e-06
 LANES = 128
 VMEM_LIMIT = 32 * 1024 * 1024
-HIGHEST = lax.Precision.HIGHEST
 
 
 def next_frames(value):
@@ -30,11 +29,18 @@
 def indicator(rows, cols, fn):
     r = lax.broadcasted_iota(jnp.int32, (rows, cols), 0)
     c = lax.broadcasted_iota(jnp.int32, (rows, cols), 1)
-    return jnp.where(fn(r, c), 1.0, 0.0).astype(jnp.float32)
-
-
-def exact_dot(a, b):
-    return jnp.dot(a, b, precision=HIGHEST, preferred_element_type=jnp.float32)
+    return jnp.where(fn(r, c), 1.0, 0.0).astype(jnp.bfloat16)
+
+
+def picked(line, pick):
+    parts = []
+    for _ in range(3):
+        parts.append(line.astype(jnp.bfloat16).astype(jnp.float32))
+        line = line - parts[-1]
+    row = lax.broadcasted_iota(jnp.int32, (16, line.shape[1]), 0)
+    stacked = jnp.where(row == 0, parts[0], jnp.where(row == 1, parts[1], jnp.where(row == 2, parts[2], 0.0)))
+    product = jnp.dot(stacked.astype(jnp.bfloat16), pick, preferred_element_type=jnp.float32)
+    return jnp.sum(product, axis=0, keepdims=True)
 
 
 def folded(block):
@@ -44,25 +50,22 @@
 
 def local_moments(rows, channels):
     size = channels // GROUPS
+    same = indicator(channels, channels, lambda r, c: r // size == c // size)
+    first = indicator(channels, LANES, lambda r, c: r // size == c)
+    second = indicator(channels, LANES, lambda r, c: r // size + GROUPS == c)
     total = folded(rows[0]().astype(jnp.float32))
     for row in rows[1:]:
         total = total + folded(row().astype(jnp.float32))
     positions = len(rows) * rows[0]().shape[0]
-    channel_mean = jnp.sum(total, axis=0, keepdims=True) * (1.0 / positions)
-    channel_mean = jnp.broadcast_to(channel_mean, (8, channels))
-    same = indicator(channels, channels, lambda r, c: r // size == c // size)
-    group_mean = exact_dot(channel_mean, same) * (1.0 / size)
-    centre = group_mean[:1]
+    centre = jnp.sum(total, axis=0, keepdims=True) * (1.0 / positions)
     spread = None
     for row in rows:
         off = row().astype(jnp.float32) - centre
         part = folded(off * off)
         spread = part if spread is None else spread + part
-    first = indicator(channels, LANES, lambda r, c: r // size == c)
-    second = indicator(channels, LANES, lambda r, c: r // size + GROUPS == c)
-    spread = jnp.broadcast_to(jnp.sum(spread, axis=0, keepdims=True), (8, channels))
-    line = exact_dot(channel_mean, first) * (1.0 / size) + exact_dot(spread, second)
-    return line[:1]
+    apart = centre - picked(centre, same) * (1.0 / size)
+    spread = jnp.sum(spread, axis=0, keepdims=True) + positions * apart * apart
+    return picked(centre, first) * (1.0 / size) + picked(spread, second)
 
 
 def merged_lines(lines, members):
@@ -79,11 +82,9 @@
 
 def channel_moments(line, members, channels):
     size = channels // GROUPS
-    pick_first = indicator(LANES, channels, lambda r, c: c // size == r)
-    pick_second = indicator(LANES, channels, lambda r, c: c // size + GROUPS == r)
-    line = jnp.broadcast_to(line, (8, LANES))
-    centre = exact_dot(line, pick_first)[:1]
-    variance = exact_dot(line, pick_second)[:1] * (1.0 / members)
+    pick = indicator(LANES, 2 * channels, lambda r, c: c // size == r)
+    wide = picked(line, pick)
+    centre, variance = wide[:, :channels], wide[:, channels:] * (1.0 / members)
     return centre, lax.rsqrt(variance + EPSILON)
 
 
@@ -162,6 +163,11 @@
     line_ref[...] = jnp.broadcast_to(merged_lines(lines_ref[...], members), line_ref.shape)
 
 
+def ring_merge_kernel(members, a_ref, b_ref, c_ref, d_ref, block_ref, line_ref, sent_ref):
+    lines = jnp.concatenate([r[0:1] for r in (a_ref, b_ref, c_ref, d_ref)], axis=0)
+    line_ref[...] = jnp.broadcast_to(merged_lines(lines, members), line_ref.shape)
+
+
 def merge_kernel(members, lines_ref, line_ref):
     line_ref[...] = jnp.broadcast_to(merged_lines(lines_ref[...], members), line_ref.shape)
 
@@ -169,7 +175,7 @@
 def scaling(lines_ref, params_ref, norm, members):
     channels = params_ref.shape[1]
     devices = lax.axis_size("tm") * lax.axis_size("band")
-    line = merged_lines(lines_ref[...], members * lax.axis_size("band"))
+    line = merged_lines(lines_ref[...], members * devices // lines_ref.shape[0])
     centre, inverse = channel_moments(line, members * devices, channels)
     gain, shift = params_ref[2 * norm : 2 * norm + 1], params_ref[2 * norm + 1 : 2 * norm + 2]
     return centre, 0.5 * inverse * gain, 0.5 * shift
@@ -245,6 +251,7 @@
     members = frames * rows * cols * (channels // GROUPS)
     vmem = pl.BlockSpec(memory_space=pltpu.VMEM)
     hbm = pl.BlockSpec(memory_space=pltpu.HBM)
+    anywhere = pl.BlockSpec(memory_space=pl.ANY)
     params = pltpu.CompilerParams(vmem_limit_bytes=VMEM_LIMIT)
     small = pltpu.CompilerParams(vmem_limit_bytes=4 * 1024 * 1024)
     line = lambda count: jax.ShapeDtypeStruct((count, LANES), jnp.float32)
@@ -283,7 +290,7 @@
 
     hidden, lines = pl.pallas_call(
         functools.partial(first_kernel, members),
-        out_shape=[block(frames, rows + 2), line(band)],
+        out_shape=[block(frames, rows + 2), line(8)],
         in_specs=[vmem] * 7,
         out_specs=[vmem, vmem],
         scratch_shapes=[held(4, rows + 4), mixed],
@@ -291,17 +298,21 @@
         name="first_conv",
     )(kept, prev, pair, cross, lines, vectors, taps(first_weight))
 
-    prev = next_frames(hidden)
-    lines = spread_over(lines, "band")
-    lines = pl.pallas_call(
-        functools.partial(merge_kernel, members),
-        out_shape=line(tm),
-        in_specs=[vmem],
-        out_specs=vmem,
+    xz = [[(4 * x + y) * band + b for x in range(4) for b in range(band)] for y in range(4)]
+    def rot(v, by):
+        return lax.ppermute(v, "tm", [(i, i - i % 4 + (i + by) % 4) for i in range(tm)])
+    got = [rot(lines, by) for by in (2, 1, 3)]
+    lines, hidden = pl.pallas_call(
+        functools.partial(ring_merge_kernel, members),
+        out_shape=[line(64), block(frames, rows + 2)],
+        in_specs=[vmem] * 4 + [anywhere],
+        out_specs=[vmem, anywhere],
+        input_output_aliases={4: 1},
         compiler_params=small,
         name="merge",
-    )(lines)
-    lines = spread_over(lines, "tm")
+    )(lines, *got, hidden)
+    prev = next_frames(hidden)
+    lines = lax.all_to_all(lines, ("tm", "band"), 0, 0, tiled=True, axis_index_groups=xz)
 
     return pl.pallas_call(
         functools.partial(second_kernel, members),

time: 74.4 us -> 72.7 us (0.977)
  blocking collectives: 53.3 us -> 47 us
  waiting for transfers between devices: 0.01 us -> 3.05 us
  starting transfers between devices: 9.34 us -> 11.7 us
  Pallas kernels: 11.3 us -> 10.5 us
    all_to_all x4 -> x2, blocking collectives: 53.3 us -> 28.9 us  [local(): lax.all_to_all(lines, axis, 0, 0, tiled=True)]
    all_to_all x0 -> x1, blocking collectives: none -> 18.1 us  [local(): lax.all_to_all(lines, ('tm', 'band'), 0, 0, tiled=True, axis_index_groups...]
    ppermute x0 -> x3, waiting for transfers between devices: none -> 3.04 us  [rot(): lax.ppermute(v, 'tm', [(i, i - i % 4 + (i + by) % 4) for i in range(tm)])]
    ppermute x0 -> x3, starting transfers between devices: none -> 2.39 us  [rot(): lax.ppermute(v, 'tm', [(i, i - i % 4 + (i + by) % 4) for i in range(tm)])]
  transfers between devices with their start and end apart: 4 -> 7, of which waited for: 0 -> 3; matrix products, arithmetic and copies ran while one was open for 0% -> 0% of each run, Pallas kernels for 3% -> 2%
where the time goes in v5:
time: 72.7 us; the launch traced here: 72.5 us
  blocking collectives  47 us (65%)
  starting transfers between devices  11.7 us (16%)
  Pallas kernels  10.5 us (14%)
  waiting for transfers between devices  3.05 us (4%)
    all_to_all x2, blocking collectives, local(): lax.all_to_all(lines, axis, 0, 0, tiled=True)  28.9 us
    all_to_all x1, blocking collectives, local(): lax.all_to_all(lines, ('tm', 'band'), 0, 0, tiled=True, axis_index_groups...  18.1 us
    ppermute x2, starting transfers between devices, next_frames(): return lax.ppermute(value, 'tm', [(i, i + 1) for i in range(count - 1)])  6.27 us
    pallas_call x1, Pallas kernels, local(): pl.pallas_call(functools.partial(first_kernel, members), out_shape=[block...  4.49 us
    pallas_call x1, Pallas kernels, local(): pl.pallas_call(functools.partial(second_kernel, members), out_shape=block...  4.25 us
    ppermute x2, starting transfers between devices, swapped(): return lax.ppermute(value, axis, pairs)  3.05 us
    ppermute x3, waiting for transfers between devices, rot(): lax.ppermute(v, 'tm', [(i, i - i % 4 + (i + by) % 4) for i in range(tm)])  3.04 us
    ppermute x3, starting transfers between devices, rot(): lax.ppermute(v, 'tm', [(i, i - i % 4 + (i + by) % 4) for i in range(tm)])  2.39 us
  transfers between devices with their start and end apart: 7, of which 3 were waited for; matrix products, arithmetic and copies ran while one was open for 0% of the time, Pallas kernels for 2%

profile of v5, /device:TPU:1, one launch (start us, length us, event | category | flops | bytes accessed | tf_op | source)
XLA Modules:
  0.0 72.5 jit_solution(18301664374982711803)
XLA Ops:
  0.0 4.0 %collective-permute-start = (bf16[2,8,64,256]{3,2,1,0:T(8,128)(2,1)}, bf16[2,8,64,256]{3,2,1,0:T(8,128)(2,1)S(1)}, u32[]{:S(2)}, u32[]{:S(2)}) collective-permute-start(bf16[2,8,64,256]{3,2,1,0:T(8,128)(2,1)} %x_ref.1), channel_id=1, source_target_pairs={{0,16},{16,32},{32,48},{48,64},{64,80},{80,96},{96,112},{112,128},... | collective-permute-start | bytes 1572872 | tf_op jit(solution)/shard_map/ppermute | solution.py:18
  4.1 1.5 %moments.1 = (f32[16,128]{1,0:T(8,128)S(1)}, bf16[2,8,64,256]{3,2,1,0:T(8,128)(2,1)S(1)}, f32[8,256]{1,0:T(8,128)S(1)}) custom-call(bf16[2,8,64,256]{3,2,1,0:T(8,128)(2,1)} %x_ref.1, f32[1,256]{1,0:T(1,128)} %bitcast.26, f32[1,256]{1,0:T(1,128)} %bitcast.27, f32[1,256]{1,0:T(1,128)} %bitcast.28, f32[1,256]{1,0:T(1,128)} %bitcast.29), custom_call_target="tpu_custom_call" | custom-call | tf_op jit(solution)/shard_map/moments/pallas_call | solution.py:268
  5.6 16.2 %all_to_all.33 = f32[16,1,128]{2,1,0:T(1,128)S(1)} all-to-all(f32[16,1,128]{2,1,0:T(1,128)S(1)} %bitcast.25), channel_id=1, replica_groups=mesh['tm'=16,'band'=16] {'band'}, dimensions={0} | all-to-all | bytes 16384 | tf_op jit(solution)/shard_map/all_to_all | solution.py:264
  21.8 0.0 collective-permute-done.prev_ref
  21.8 0.0 copy-start
  21.8 0.1 edges.1
  21.9 0.0 copy-start.1
  21.9 0.7 collective-permute-start.1
  22.7 2.3 %collective-permute-start.2 = (bf16[4,2,64,256]{3,2,1,0:T(8,128)(2,1)S(1)}, bf16[4,2,64,256]{3,2,1,0:T(8,128)(2,1)S(1)}, u32[]{:S(2)}, u32[]{:S(2)}) collective-permute-start(bf16[4,2,64,256]{3,2,1,0:T(8,128)(2,1)S(1)} %get-tuple-element.18), channel_id=1, source_target_pairs={{1,2},{2,1},{3,4},{4,3},{5,6},{6,5},{7,8},{8,7},{9,10},{10,9},{11,... | collective-permute-start | bytes 786440 | tf_op jit(solution)/shard_map/ppermute | solution.py:26
  25.0 12.6 %all_to_all.34 = f32[16,1,128]{2,1,0:T(1,128)S(1)} all-to-all(f32[16,1,128]{2,1,0:T(1,128)S(1)} %bitcast.23), channel_id=1, replica_groups=mesh['tm'=16,'band'=16] {'tm'}, dimensions={0} | all-to-all | bytes 16384 | tf_op jit(solution)/shard_map/all_to_all | solution.py:264
  37.6 0.0 collective-permute-done.1.pair_ref
  37.6 0.0 collective-permute-done.2.cross_ref
  37.7 0.0 copy-done
  37.7 4.5 %first_conv.1 = (bf16[2,10,64,256]{3,2,1,0:T(8,128)(2,1)S(1)}, f32[8,128]{1,0:T(8,128)S(1)}) custom-call(bf16[2,8,64,256]{3,2,1,0:T(8,128)(2,1)S(1)} %get-tuple-element.15.x_ref, bf16[2,8,64,256]{3,2,1,0:T(8,128)(2,1)S(1)} %collective-permute-done.prev_ref, bf16[4,2,64,256]{3,2,1,0:T(8,128)(2,1)S(1)} %collective-permute-done.1.pair_ref, ...), custom_call_target="tpu_custom_call" | custom-call | tf_op jit(solution)/shard_map/first_conv/pallas_call | solution.py:291
  42.2 0.9 %collective-permute-start.5 = (f32[8,128]{1,0:T(8,128)S(1)}, f32[8,128]{1,0:T(8,128)S(1)}, u32[]{:S(2)}, u32[]{:S(2)}) collective-permute-start(f32[8,128]{1,0:T(8,128)S(1)} %get-tuple-element.21.a_ref), channel_id=1, source_target_pairs={{0,48},{16,0},{32,16},{48,32},{64,112},{80,64},{96,80},{112,96},{1... | collective-permute-start | bytes 12296 | tf_op jit(solution)/shard_map/ppermute | solution.py:303
  43.1 0.6 collective-permute-start.4
  43.6 0.9 %collective-permute-start.3 = (f32[8,128]{1,0:T(8,128)S(1)}, f32[8,128]{1,0:T(8,128)S(1)}, u32[]{:S(2)}, u32[]{:S(2)}) collective-permute-start(f32[8,128]{1,0:T(8,128)S(1)} %get-tuple-element.21.a_ref), channel_id=1, source_target_pairs={{0,32},{16,48},{32,0},{48,16},{64,96},{80,112},{96,64},{112,80},{1... | collective-permute-start | bytes 12296 | tf_op jit(solution)/shard_map/ppermute | solution.py:303
  44.5 0.1 collective-permute-done.5.d_ref
  44.6 2.1 %collective-permute-done.4.c_ref = f32[8,128]{1,0:T(8,128)S(1)} collective-permute-done((f32[8,128]{1,0:T(8,128)S(1)}, f32[8,128]{1,0:T(8,128)S(1)}, u32[]{:S(2)}, u32[]{:S(2)}) %collective-permute-start.4) | collective-permute-done | bytes 4128 | tf_op jit(solution)/shard_map/ppermute | solution.py:303
  46.7 0.9 %collective-permute-done.3.b_ref = f32[8,128]{1,0:T(8,128)S(1)} collective-permute-done((f32[8,128]{1,0:T(8,128)S(1)}, f32[8,128]{1,0:T(8,128)S(1)}, u32[]{:S(2)}, u32[]{:S(2)}) %collective-permute-start.3) | collective-permute-done | bytes 4128 | tf_op jit(solution)/shard_map/ppermute | solution.py:303
  47.6 0.1 merge.1
  47.7 2.2 %collective-permute-start.6 = (bf16[2,10,64,256]{3,2,1,0:T(8,128)(2,1)S(1)}, bf16[2,10,64,256]{3,2,1,0:T(8,128)(2,1)S(1)}, u32[]{:S(2)}, u32[]{:S(2)}) collective-permute-start(bf16[2,10,64,256]{3,2,1,0:T(8,128)(2,1)S(1)} %get-tuple-element.23.hidden_ref), channel_id=1, source_target_pairs={{0,16},{16,32},{32,48},{48,64},{64,80},{80,96},{96,112},{112,128},... | collective-permute-start | bytes 1966088 | tf_op jit(solution)/shard_map/ppermute | solution.py:18
  49.9 18.1 %all_to_all.35 = f32[64,1,128]{2,1,0:T(1,128)S(1)} all-to-all(f32[64,1,128]{2,1,0:T(1,128)S(1)} %bitcast.22), channel_id=1, replica_groups={{0,1,2,3,4,5,6,7,8,9,10,11,12,13,14,15,64,65,66,67,68,69,70,71,72,73,74..., dimensions={0} | all-to-all | bytes 65536 | tf_op jit(solution)/shard_map/all_to_all | solution.py:315
  68.0 0.0 collective-permute-done.6.prev_ref
  68.0 0.0 copy-done.1
  68.0 4.3 %second_conv.1 = bf16[2,8,64,256]{3,2,1,0:T(8,128)(2,1)} custom-call(bf16[2,10,64,256]{3,2,1,0:T(8,128)(2,1)S(1)} %get-tuple-element.23.hidden_ref, bf16[2,10,64,256]{3,2,1,0:T(8,128)(2,1)S(1)} %collective-permute-done.6.prev_ref, f32[64,128]{1,0:T(8,128)S(1)} %bitcast.20, f32[8,256]{1,0:T(8,128)S(1)} %get-tuple-element.20.params_ref, ...), custom_call_target="tpu_custom_call" | custom-call | tf_op jit(solution)/shard_map/second_conv/pallas_call | solution.py:317
Async XLA Ops:
  0.0 21.8 %collective-permute-start = (bf16[2,8,64,256]{3,2,1,0:T(8,128)(2,1)}, bf16[2,8,64,256]{3,2,1,0:T(8,128)(2,1)S(1)}, u32[]{:S(2)}, u32[]{:S(2)}) collective-permute-start(bf16[2,8,64,256]{3,2,1,0:T(8,128)(2,1)} %x_ref.1), channel_id=1, source_target_pairs={{0,16},{16,32},{32,48},{48,64},{64,80},{80,96},{96,112},{112,128},... | collective-permute-start | bytes 1572872 | tf_op jit(solution)/shard_map/ppermute | solution.py:18
  21.8 15.8 %copy-start = (bf16[3,3,3,256,256]{4,3,2,1,0:T(8,128)(2,1)S(1)}, bf16[3,3,3,256,256]{4,3,2,1,0:T(8,128)(2,1)}, u32[]{:S(2)}) copy-start(bf16[3,3,3,256,256]{4,3,2,1,0:T(8,128)(2,1)} %param.10) | copy-start | bytes 10616836
  21.9 46.1 %copy-start.1 = (bf16[3,3,3,256,256]{4,3,2,1,0:T(8,128)(2,1)S(1)}, bf16[3,3,3,256,256]{4,3,2,1,0:T(8,128)(2,1)}, u32[]{:S(2)}) copy-start(bf16[3,3,3,256,256]{4,3,2,1,0:T(8,128)(2,1)} %param.13) | copy-start | bytes 10616836
  21.9 15.7 %collective-permute-start.1 = (bf16[4,2,64,256]{3,2,1,0:T(8,128)(2,1)S(1)}, bf16[4,2,64,256]{3,2,1,0:T(8,128)(2,1)S(1)}, u32[]{:S(2)}, u32[]{:S(2)}) collective-permute-start(bf16[4,2,64,256]{3,2,1,0:T(8,128)(2,1)S(1)} %get-tuple-element.17), channel_id=1, source_target_pairs={{0,1},{1,0},{2,3},{3,2},{4,5},{5,4},{6,7},{7,6},{8,9},{9,8},{10,11... | collective-permute-start | bytes 786440 | tf_op jit(solution)/shard_map/ppermute | solution.py:26
  22.7 15.0 %collective-permute-start.2 = (bf16[4,2,64,256]{3,2,1,0:T(8,128)(2,1)S(1)}, bf16[4,2,64,256]{3,2,1,0:T(8,128)(2,1)S(1)}, u32[]{:S(2)}, u32[]{:S(2)}) collective-permute-start(bf16[4,2,64,256]{3,2,1,0:T(8,128)(2,1)S(1)} %get-tuple-element.18), channel_id=1, source_target_pairs={{1,2},{2,1},{3,4},{4,3},{5,6},{6,5},{7,8},{8,7},{9,10},{10,9},{11,... | collective-permute-start | bytes 786440 | tf_op jit(solution)/shard_map/ppermute | solution.py:26
  42.2 2.5 %collective-permute-start.5 = (f32[8,128]{1,0:T(8,128)S(1)}, f32[8,128]{1,0:T(8,128)S(1)}, u32[]{:S(2)}, u32[]{:S(2)}) collective-permute-start(f32[8,128]{1,0:T(8,128)S(1)} %get-tuple-element.21.a_ref), channel_id=1, source_target_pairs={{0,48},{16,0},{32,16},{48,32},{64,112},{80,64},{96,80},{112,96},{1... | collective-permute-start | bytes 12296 | tf_op jit(solution)/shard_map/ppermute | solution.py:303
  43.1 3.7 %collective-permute-start.4 = (f32[8,128]{1,0:T(8,128)S(1)}, f32[8,128]{1,0:T(8,128)S(1)}, u32[]{:S(2)}, u32[]{:S(2)}) collective-permute-start(f32[8,128]{1,0:T(8,128)S(1)} %get-tuple-element.21.a_ref), channel_id=1, source_target_pairs={{0,16},{16,32},{32,48},{48,0},{64,80},{80,96},{96,112},{112,64},{1... | collective-permute-start | bytes 12296 | tf_op jit(solution)/shard_map/ppermute | solution.py:303
  43.6 4.0 %collective-permute-start.3 = (f32[8,128]{1,0:T(8,128)S(1)}, f32[8,128]{1,0:T(8,128)S(1)}, u32[]{:S(2)}, u32[]{:S(2)}) collective-permute-start(f32[8,128]{1,0:T(8,128)S(1)} %get-tuple-element.21.a_ref), channel_id=1, source_target_pairs={{0,32},{16,48},{32,0},{48,16},{64,96},{80,112},{96,64},{112,80},{1... | collective-permute-start | bytes 12296 | tf_op jit(solution)/shard_map/ppermute | solution.py:303
  47.7 20.4 %collective-permute-start.6 = (bf16[2,10,64,256]{3,2,1,0:T(8,128)(2,1)S(1)}, bf16[2,10,64,256]{3,2,1,0:T(8,128)(2,1)S(1)}, u32[]{:S(2)}, u32[]{:S(2)}) collective-permute-start(bf16[2,10,64,256]{3,2,1,0:T(8,128)(2,1)S(1)} %get-tuple-element.23.hidden_ref), channel_id=1, source_target_pairs={{0,16},{16,32},{32,48},{48,64},{64,80},{80,96},{96,112},{112,128},... | collective-permute-start | bytes 1966088 | tf_op jit(solution)/shard_map/ppermute | solution.py:18

commit v6 on v5

--- a/solution.py
+++ b/solution.py
@@ -163,7 +163,7 @@
     line_ref[...] = jnp.broadcast_to(merged_lines(lines_ref[...], members), line_ref.shape)
 
 
-def ring_merge_kernel(members, a_ref, b_ref, c_ref, d_ref, block_ref, line_ref, sent_ref):
+def ring_merge_kernel(members, a_ref, b_ref, c_ref, d_ref, line_ref):
     lines = jnp.concatenate([r[0:1] for r in (a_ref, b_ref, c_ref, d_ref)], axis=0)
     line_ref[...] = jnp.broadcast_to(merged_lines(lines, members), line_ref.shape)
 
@@ -302,15 +302,15 @@
     def rot(v, by):
         return lax.ppermute(v, "tm", [(i, i - i % 4 + (i + by) % 4) for i in range(tm)])
     got = [rot(lines, by) for by in (2, 1, 3)]
-    lines, hidden = pl.pallas_call(
+    lines = pl.pallas_call(
         functools.partial(ring_merge_kernel, members),
-        out_shape=[line(64), block(frames, rows + 2)],
-        in_specs=[vmem] * 4 + [anywhere],
-        out_specs=[vmem, anywhere],
-        input_output_aliases={4: 1},
+        out_shape=line(64),
+        in_specs=[vmem] * 4,
+        out_specs=vmem,
         compiler_params=small,
+        cost_estimate=pl.CostEstimate(flops=20 * 10**9, bytes_accessed=0, transcendentals=0),
         name="merge",
-    )(lines, *got, hidden)
+    )(lines, *got)
     prev = next_frames(hidden)
     lines = lax.all_to_all(lines, ("tm", "band"), 0, 0, tiled=True, axis_index_groups=xz)
 

time: 72.7 us -> 70.5 us (0.970)
  waiting for transfers between devices: 3.05 us -> 0.02 us
  starting transfers between devices: 11.7 us -> 13.4 us
  blocking collectives: 47 us -> 46 us
    ppermute x3, waiting for transfers between devices: 3.04 us -> 0.01 us  [rot(): lax.ppermute(v, 'tm', [(i, i - i % 4 + (i + by) % 4) for i in range(tm)])]
    ppermute x2, starting transfers between devices: 6.27 us -> 8.01 us  [next_frames(): return lax.ppermute(value, 'tm', [(i, i + 1) for i in range(count - 1)])]
    all_to_all x1, blocking collectives: 18.1 us -> 17.1 us  [local(): lax.all_to_all(lines, ('tm', 'band'), 0, 0, tiled=True, axis_index_groups...]
  transfers between devices with their start and end apart: 7 -> 7, of which waited for: 3 -> 0; matrix products, arithmetic and copies ran while one was open for 0% -> 0% of each run, Pallas kernels for 2% -> 2%
where the time goes in v6:
time: 70.5 us; the launch traced here: 70.2 us
  blocking collectives  46 us (65%)
  starting transfers between devices  13.4 us (19%)
  Pallas kernels  10.5 us (15%)
    all_to_all x2, blocking collectives, local(): lax.all_to_all(lines, axis, 0, 0, tiled=True)  28.9 us
    all_to_all x1, blocking collectives, local(): lax.all_to_all(lines, ('tm', 'band'), 0, 0, tiled=True, axis_index_groups...  17.1 us
    ppermute x2, starting transfers between devices, next_frames(): return lax.ppermute(value, 'tm', [(i, i + 1) for i in range(count - 1)])  8.01 us
    pallas_call x1, Pallas kernels, local(): pl.pallas_call(functools.partial(first_kernel, members), out_shape=[block...  4.51 us
    pallas_call x1, Pallas kernels, local(): pl.pallas_call(functools.partial(second_kernel, members), out_shape=block...  4.31 us
    ppermute x2, starting transfers between devices, swapped(): return lax.ppermute(value, axis, pairs)  3.04 us
    ppermute x3, starting transfers between devices, rot(): lax.ppermute(v, 'tm', [(i, i - i % 4 + (i + by) % 4) for i in range(tm)])  2.39 us
    pallas_call x1, Pallas kernels, local(): pl.pallas_call(stats_kernel, out_shape=[line(band), block(frames, rows),...  1.52 us
  transfers between devices with their start and end apart: 7, of which 0 were waited for; matrix products, arithmetic and copies ran while one was open for 0% of the time, Pallas kernels for 2%

profile of v6, /device:TPU:1, one launch (start us, length us, event | category | flops | bytes accessed | tf_op | source)
XLA Modules:
  0.0 70.2 jit_solution(16531110138924501249)
XLA Ops:
  0.0 4.0 %collective-permute-start = (bf16[2,8,64,256]{3,2,1,0:T(8,128)(2,1)}, bf16[2,8,64,256]{3,2,1,0:T(8,128)(2,1)S(1)}, u32[]{:S(2)}, u32[]{:S(2)}) collective-permute-start(bf16[2,8,64,256]{3,2,1,0:T(8,128)(2,1)} %x_ref.1), channel_id=1, source_target_pairs={{0,16},{16,32},{32,48},{48,64},{64,80},{80,96},{96,112},{112,128},... | collective-permute-start | bytes 1572872 | tf_op jit(solution)/shard_map/ppermute | solution.py:18
  4.1 1.5 %moments.1 = (f32[16,128]{1,0:T(8,128)S(1)}, bf16[2,8,64,256]{3,2,1,0:T(8,128)(2,1)S(1)}, f32[8,256]{1,0:T(8,128)S(1)}) custom-call(bf16[2,8,64,256]{3,2,1,0:T(8,128)(2,1)} %x_ref.1, f32[1,256]{1,0:T(1,128)} %bitcast.26, f32[1,256]{1,0:T(1,128)} %bitcast.27, f32[1,256]{1,0:T(1,128)} %bitcast.28, f32[1,256]{1,0:T(1,128)} %bitcast.29), custom_call_target="tpu_custom_call" | custom-call | tf_op jit(solution)/shard_map/moments/pallas_call | solution.py:268
  5.6 16.2 %all_to_all.33 = f32[16,1,128]{2,1,0:T(1,128)S(1)} all-to-all(f32[16,1,128]{2,1,0:T(1,128)S(1)} %bitcast.25), channel_id=1, replica_groups=mesh['tm'=16,'band'=16] {'band'}, dimensions={0} | all-to-all | bytes 16384 | tf_op jit(solution)/shard_map/all_to_all | solution.py:264
  21.8 0.0 collective-permute-done.prev_ref
  21.8 0.0 copy-start
  21.8 0.1 edges.1
  21.9 0.7 %collective-permute-start.1 = (bf16[4,2,64,256]{3,2,1,0:T(8,128)(2,1)S(1)}, bf16[4,2,64,256]{3,2,1,0:T(8,128)(2,1)S(1)}, u32[]{:S(2)}, u32[]{:S(2)}) collective-permute-start(bf16[4,2,64,256]{3,2,1,0:T(8,128)(2,1)S(1)} %get-tuple-element.15), channel_id=1, source_target_pairs={{0,1},{1,0},{2,3},{3,2},{4,5},{5,4},{6,7},{7,6},{8,9},{9,8},{10,11... | collective-permute-start | bytes 786440 | tf_op jit(solution)/shard_map/ppermute | solution.py:26
  22.6 2.3 %collective-permute-start.2 = (bf16[4,2,64,256]{3,2,1,0:T(8,128)(2,1)S(1)}, bf16[4,2,64,256]{3,2,1,0:T(8,128)(2,1)S(1)}, u32[]{:S(2)}, u32[]{:S(2)}) collective-permute-start(bf16[4,2,64,256]{3,2,1,0:T(8,128)(2,1)S(1)} %get-tuple-element.16), channel_id=1, source_target_pairs={{1,2},{2,1},{3,4},{4,3},{5,6},{6,5},{7,8},{8,7},{9,10},{10,9},{11,... | collective-permute-start | bytes 786440 | tf_op jit(solution)/shard_map/ppermute | solution.py:26
  25.0 12.6 %all_to_all.34 = f32[16,1,128]{2,1,0:T(1,128)S(1)} all-to-all(f32[16,1,128]{2,1,0:T(1,128)S(1)} %bitcast.23), channel_id=1, replica_groups=mesh['tm'=16,'band'=16] {'tm'}, dimensions={0} | all-to-all | bytes 16384 | tf_op jit(solution)/shard_map/all_to_all | solution.py:264
  37.6 0.0 collective-permute-done.1.pair_ref
  37.6 0.0 collective-permute-done.2.cross_ref
  37.6 0.0 copy-done
  37.6 4.5 %first_conv.1 = (bf16[2,10,64,256]{3,2,1,0:T(8,128)(2,1)S(1)}, f32[8,128]{1,0:T(8,128)S(1)}) custom-call(bf16[2,8,64,256]{3,2,1,0:T(8,128)(2,1)S(1)} %get-tuple-element.13.x_ref, bf16[2,8,64,256]{3,2,1,0:T(8,128)(2,1)S(1)} %collective-permute-done.prev_ref, bf16[4,2,64,256]{3,2,1,0:T(8,128)(2,1)S(1)} %collective-permute-done.1.pair_ref, ...), custom_call_target="tpu_custom_call" | custom-call | tf_op jit(solution)/shard_map/first_conv/pallas_call | solution.py:291
  42.2 0.9 %collective-permute-start.6 = (f32[8,128]{1,0:T(8,128)S(1)}, f32[8,128]{1,0:T(8,128)S(1)}, u32[]{:S(2)}, u32[]{:S(2)}) collective-permute-start(f32[8,128]{1,0:T(8,128)S(1)} %get-tuple-element.20.a_ref), channel_id=1, source_target_pairs={{0,48},{16,0},{32,16},{48,32},{64,112},{80,64},{96,80},{112,96},{1... | collective-permute-start | bytes 12296 | tf_op jit(solution)/shard_map/ppermute | solution.py:303
  43.1 0.6 collective-permute-start.5
  43.6 0.9 %collective-permute-start.4 = (f32[8,128]{1,0:T(8,128)S(1)}, f32[8,128]{1,0:T(8,128)S(1)}, u32[]{:S(2)}, u32[]{:S(2)}) collective-permute-start(f32[8,128]{1,0:T(8,128)S(1)} %get-tuple-element.20.a_ref), channel_id=1, source_target_pairs={{0,32},{16,48},{32,0},{48,16},{64,96},{80,112},{96,64},{112,80},{1... | collective-permute-start | bytes 12296 | tf_op jit(solution)/shard_map/ppermute | solution.py:303
  44.5 0.0 copy-start.1
  44.5 4.0 %collective-permute-start.3 = (bf16[2,10,64,256]{3,2,1,0:T(8,128)(2,1)S(1)}, bf16[2,10,64,256]{3,2,1,0:T(8,128)(2,1)S(1)}, u32[]{:S(2)}, u32[]{:S(2)}) collective-permute-start(bf16[2,10,64,256]{3,2,1,0:T(8,128)(2,1)S(1)} %get-tuple-element.19.hidden_ref), channel_id=1, source_target_pairs={{0,16},{16,32},{32,48},{48,64},{64,80},{80,96},{96,112},{112,128},... | collective-permute-start | bytes 1966088 | tf_op jit(solution)/shard_map/ppermute | solution.py:18
  48.5 0.0 collective-permute-done.6.d_ref
  48.5 0.0 collective-permute-done.5.c_ref
  48.5 0.0 collective-permute-done.4.b_ref
  48.6 0.1 merge.1
  48.6 17.1 %all_to_all.35 = f32[64,1,128]{2,1,0:T(1,128)S(1)} all-to-all(f32[64,1,128]{2,1,0:T(1,128)S(1)} %bitcast.22), channel_id=1, replica_groups={{0,1,2,3,4,5,6,7,8,9,10,11,12,13,14,15,64,65,66,67,68,69,70,71,72,73,74..., dimensions={0} | all-to-all | bytes 65536 | tf_op jit(solution)/shard_map/all_to_all | solution.py:315
  65.8 0.0 collective-permute-done.3.prev_ref
  65.8 0.0 copy-done.1
  65.8 4.3 %second_conv.1 = bf16[2,8,64,256]{3,2,1,0:T(8,128)(2,1)} custom-call(bf16[2,10,64,256]{3,2,1,0:T(8,128)(2,1)S(1)} %get-tuple-element.19.hidden_ref, bf16[2,10,64,256]{3,2,1,0:T(8,128)(2,1)S(1)} %collective-permute-done.3.prev_ref, f32[64,128]{1,0:T(8,128)S(1)} %bitcast.20, f32[8,256]{1,0:T(8,128)S(1)} %get-tuple-element.18.params_ref, ...), custom_call_target="tpu_custom_call" | custom-call | tf_op jit(solution)/shard_map/second_conv/pallas_call | solution.py:317
Async XLA Ops:
  0.0 21.8 %collective-permute-start = (bf16[2,8,64,256]{3,2,1,0:T(8,128)(2,1)}, bf16[2,8,64,256]{3,2,1,0:T(8,128)(2,1)S(1)}, u32[]{:S(2)}, u32[]{:S(2)}) collective-permute-start(bf16[2,8,64,256]{3,2,1,0:T(8,128)(2,1)} %x_ref.1), channel_id=1, source_target_pairs={{0,16},{16,32},{32,48},{48,64},{64,80},{80,96},{96,112},{112,128},... | collective-permute-start | bytes 1572872 | tf_op jit(solution)/shard_map/ppermute | solution.py:18
  21.8 15.8 %copy-start = (bf16[3,3,3,256,256]{4,3,2,1,0:T(8,128)(2,1)S(1)}, bf16[3,3,3,256,256]{4,3,2,1,0:T(8,128)(2,1)}, u32[]{:S(2)}) copy-start(bf16[3,3,3,256,256]{4,3,2,1,0:T(8,128)(2,1)} %param.10) | copy-start | bytes 10616836
  21.9 15.7 %collective-permute-start.1 = (bf16[4,2,64,256]{3,2,1,0:T(8,128)(2,1)S(1)}, bf16[4,2,64,256]{3,2,1,0:T(8,128)(2,1)S(1)}, u32[]{:S(2)}, u32[]{:S(2)}) collective-permute-start(bf16[4,2,64,256]{3,2,1,0:T(8,128)(2,1)S(1)} %get-tuple-element.15), channel_id=1, source_target_pairs={{0,1},{1,0},{2,3},{3,2},{4,5},{5,4},{6,7},{7,6},{8,9},{9,8},{10,11... | collective-permute-start | bytes 786440 | tf_op jit(solution)/shard_map/ppermute | solution.py:26
  22.6 15.0 %collective-permute-start.2 = (bf16[4,2,64,256]{3,2,1,0:T(8,128)(2,1)S(1)}, bf16[4,2,64,256]{3,2,1,0:T(8,128)(2,1)S(1)}, u32[]{:S(2)}, u32[]{:S(2)}) collective-permute-start(bf16[4,2,64,256]{3,2,1,0:T(8,128)(2,1)S(1)} %get-tuple-element.16), channel_id=1, source_target_pairs={{1,2},{2,1},{3,4},{4,3},{5,6},{6,5},{7,8},{8,7},{9,10},{10,9},{11,... | collective-permute-start | bytes 786440 | tf_op jit(solution)/shard_map/ppermute | solution.py:26
  42.2 6.4 %collective-permute-start.6 = (f32[8,128]{1,0:T(8,128)S(1)}, f32[8,128]{1,0:T(8,128)S(1)}, u32[]{:S(2)}, u32[]{:S(2)}) collective-permute-start(f32[8,128]{1,0:T(8,128)S(1)} %get-tuple-element.20.a_ref), channel_id=1, source_target_pairs={{0,48},{16,0},{32,16},{48,32},{64,112},{80,64},{96,80},{112,96},{1... | collective-permute-start | bytes 12296 | tf_op jit(solution)/shard_map/ppermute | solution.py:303
  43.1 5.5 %collective-permute-start.5 = (f32[8,128]{1,0:T(8,128)S(1)}, f32[8,128]{1,0:T(8,128)S(1)}, u32[]{:S(2)}, u32[]{:S(2)}) collective-permute-start(f32[8,128]{1,0:T(8,128)S(1)} %get-tuple-element.20.a_ref), channel_id=1, source_target_pairs={{0,16},{16,32},{32,48},{48,0},{64,80},{80,96},{96,112},{112,64},{1... | collective-permute-start | bytes 12296 | tf_op jit(solution)/shard_map/ppermute | solution.py:303
  43.6 4.9 %collective-permute-start.4 = (f32[8,128]{1,0:T(8,128)S(1)}, f32[8,128]{1,0:T(8,128)S(1)}, u32[]{:S(2)}, u32[]{:S(2)}) collective-permute-start(f32[8,128]{1,0:T(8,128)S(1)} %get-tuple-element.20.a_ref), channel_id=1, source_target_pairs={{0,32},{16,48},{32,0},{48,16},{64,96},{80,112},{96,64},{112,80},{1... | collective-permute-start | bytes 12296 | tf_op jit(solution)/shard_map/ppermute | solution.py:303
  44.5 21.2 %copy-start.1 = (bf16[3,3,3,256,256]{4,3,2,1,0:T(8,128)(2,1)S(1)}, bf16[3,3,3,256,256]{4,3,2,1,0:T(8,128)(2,1)}, u32[]{:S(2)}) copy-start(bf16[3,3,3,256,256]{4,3,2,1,0:T(8,128)(2,1)} %param.13) | copy-start | bytes 10616836
  44.5 21.2 %collective-permute-start.3 = (bf16[2,10,64,256]{3,2,1,0:T(8,128)(2,1)S(1)}, bf16[2,10,64,256]{3,2,1,0:T(8,128)(2,1)S(1)}, u32[]{:S(2)}, u32[]{:S(2)}) collective-permute-start(bf16[2,10,64,256]{3,2,1,0:T(8,128)(2,1)S(1)} %get-tuple-element.19.hidden_ref), channel_id=1, source_target_pairs={{0,16},{16,32},{32,48},{48,64},{64,80},{80,96},{96,112},{112,128},... | collective-permute-start | bytes 1966088 | tf_op jit(solution)/shard_map/ppermute | solution.py:18

commit v7 on v6

--- a/solution.py
+++ b/solution.py
@@ -108,10 +108,19 @@
         mixed_ref[1, t // 3, t % 3] = (ends - middle).astype(jnp.bfloat16)
 
 
-def convolved(act_ref, weight_ref, mixed_ref, row_count):
+def convolved(act_ref, weight_ref, mixed_ref, pieces):
     cols, channels = act_ref.shape[2:]
+    row_count = sum(count for _, count in pieces)
     windows = [
-        jnp.concatenate([act_ref[part, j : j + row_count].reshape(row_count * cols, channels) for j in range(3)], axis=-1)
+        jnp.concatenate(
+            [
+                jnp.concatenate(
+                    [act_ref[part, first + j : first + j + count].reshape(count * cols, channels) for first, count in pieces]
+                )
+                for j in range(3)
+            ],
+            axis=-1,
+        )
         for part in range(4)
     ]
     early = late = None
@@ -154,18 +163,16 @@
     line_ref[...] = jnp.broadcast_to(local_moments(reads, channels), line_ref.shape)
 
 
-def edges_kernel(members, lines_ref, x_ref, prev_ref, line_ref, pair_ref, cross_ref):
-    rows = x_ref.shape[1]
-    _, _, pair_from, cross_from = places(rows)
+def edges_kernel(x_ref, prev_ref, after_ref, cross_ref, pair_ref):
+    _, _, pair_from, cross_from = places(x_ref.shape[1])
     for out_ref, at in ((pair_ref, pair_from), (cross_ref, cross_from)):
         out_ref[0:2] = prev_ref[:, pl.ds(at, 2)]
         out_ref[2:4] = x_ref[:, pl.ds(at, 2)]
-    line_ref[...] = jnp.broadcast_to(merged_lines(lines_ref[...], members), line_ref.shape)
-
-
-def ring_merge_kernel(members, a_ref, b_ref, c_ref, d_ref, line_ref):
+
+
+def ring_merge_kernel(members, a_ref, b_ref, c_ref, d_ref, *refs):
     lines = jnp.concatenate([r[0:1] for r in (a_ref, b_ref, c_ref, d_ref)], axis=0)
-    line_ref[...] = jnp.broadcast_to(merged_lines(lines, members), line_ref.shape)
+    refs[-1][...] = jnp.broadcast_to(merged_lines(lines, members), refs[-1].shape)
 
 
 def merge_kernel(members, lines_ref, line_ref):
@@ -175,7 +182,7 @@
 def scaling(lines_ref, params_ref, norm, members):
     channels = params_ref.shape[1]
     devices = lax.axis_size("tm") * lax.axis_size("band")
-    line = merged_lines(lines_ref[...], members * devices // lines_ref.shape[0])
+    line = merged_lines(lines_ref[...], members * devices // lines_ref.shape[0]) if norm else lines_ref[0:1]
     centre, inverse = channel_moments(line, members * devices, channels)
     gain, shift = params_ref[2 * norm : 2 * norm + 1], params_ref[2 * norm + 1 : 2 * norm + 2]
     return centre, 0.5 * inverse * gain, 0.5 * shift
@@ -186,30 +193,46 @@
     return lax.axis_index("tm") == 0, band == 0, band == lax.axis_size("band") - 1
 
 
-def first_kernel(members, x_ref, prev_ref, pair_ref, cross_ref, lines_ref, params_ref, weight_ref,
-                 hidden_ref, line_ref, act_ref, mixed_ref):
-    frames, rows, cols, channels = x_ref.shape
+def first_rows(act_ref, out_ref, weight_ref, mixed_ref, pieces):
+    for f, value in enumerate(convolved(act_ref, weight_ref, mixed_ref, pieces)):
+        done = 0
+        for first, count in pieces:
+            out_ref[f, first : first + count] = value[done : done + count].astype(jnp.bfloat16)
+            done += count
+
+
+def inner_kernel(members, x_ref, prev_ref, lines_ref, params_ref, weight_ref, hidden_ref, act_ref, mixed_ref):
+    rows = x_ref.shape[1]
+    leading, _, _ = at_ends()
+    norm = scaling(lines_ref, params_ref, 0, members)
+    for r in range(rows):
+        own = [x_ref[f, r] for f in range(2)]
+        before = [jnp.where(leading, own[0], prev_ref[f, r]) for f in range(2)]
+        mixed_frames(act_ref, r + 2, [activated(x, *norm) for x in before + own])
+    mix_weight(weight_ref, mixed_ref)
+    first_rows(act_ref, hidden_ref, weight_ref, mixed_ref, [(2, rows - 2)])
+
+
+def outer_kernel(members, x_ref, prev_ref, cross_ref, pair_ref, lines_ref, params_ref, weight_ref, mixed_ref, _, __,
+                 hidden_ref, act_ref, line_ref):
+    frames, rows, _, channels = x_ref.shape
     leading, top, bottom = at_ends()
     even = lax.rem(lax.axis_index("band"), 2) == 0
     norm = scaling(lines_ref, params_ref, 0, members)
 
     def row_of(f, r):
         inner = prev_ref if f < 2 else x_ref
-        if 2 <= r < rows + 2:
-            return inner[f % 2, r - 2]
         if r < 2:
             outer = jnp.where(even, cross_ref[f, r], pair_ref[f, r])
             return jnp.where(top, inner[f % 2, 0], outer) if r == 1 else outer
         outer = jnp.where(even, pair_ref[f, r - rows - 2], cross_ref[f, r - rows - 2])
         return jnp.where(bottom, inner[f % 2, rows - 1], outer) if r == rows + 2 else outer
 
-    for r in range(rows + 4):
+    for r in (0, 1, rows + 2, rows + 3):
         own = [row_of(f, r) for f in (2, 3)]
         before = [jnp.where(leading, own[0], row_of(f, r)) for f in (0, 1)]
         mixed_frames(act_ref, r, [activated(x, *norm) for x in before + own])
-    mix_weight(weight_ref, mixed_ref)
-    for f, value in enumerate(convolved(act_ref, weight_ref, mixed_ref, rows + 2)):
-        hidden_ref[f] = value.astype(jnp.bfloat16)
+    first_rows(act_ref, hidden_ref, weight_ref, mixed_ref, [(0, 2), (rows, 2)])
     reads = [functools.partial(lambda f, r: hidden_ref[f, r + 1], f, r) for f in range(frames) for r in range(rows)]
     line_ref[...] = jnp.broadcast_to(local_moments(reads, channels), line_ref.shape)
 
@@ -234,7 +257,7 @@
         mixed_frames(act_ref, r, [activated(x, *norm) for x in before + own])
     mix_weight(weight_ref, mixed_ref)
     outs = []
-    for f, value in enumerate(convolved(act_ref, weight_ref, mixed_ref, rows)):
+    for f, value in enumerate(convolved(act_ref, weight_ref, mixed_ref, [(0, rows)])):
         made_ref[f] = (x_ref[f].astype(jnp.float32) + value).astype(jnp.bfloat16)
         outs.append(pltpu.make_async_copy(made_ref.at[f], out_ref.at[f], out_sems.at[f]))
         outs[-1].start()
@@ -261,58 +284,79 @@
     taps = lambda weight: weight.reshape(9, 3, channels, outputs)
     mixed = pltpu.VMEM((2, 3, 3, channels, outputs), jnp.bfloat16)
     stay = lambda value: pltpu.with_memory_space_constraint(value, pltpu.HBM)
-    spread_over = lambda lines, axis: lax.all_to_all(lines, axis, 0, 0, tiled=True)
     vectors = [v.reshape(1, channels) for v in (first_gain, first_shift, second_gain, second_shift)]
 
     prev = next_frames(features)
     lines, kept, vectors = pl.pallas_call(
         stats_kernel,
-        out_shape=[line(band), block(frames, rows), jax.ShapeDtypeStruct((8, channels), jnp.float32)],
+        out_shape=[line(64), block(frames, rows), jax.ShapeDtypeStruct((8, channels), jnp.float32)],
         in_specs=[hbm] * 5,
         out_specs=[vmem] * 3,
         scratch_shapes=[dmas(frames + 4)],
         compiler_params=small,
         name="moments",
     )(stay(features), *[stay(v) for v in vectors])
-    lines = spread_over(lines, "band")
-    lines, pair, cross = pl.pallas_call(
-        functools.partial(edges_kernel, members),
-        out_shape=[line(tm), block(frames + 2, 2), block(frames + 2, 2)],
+    others = [[(4 * x + y) * band + b for x in range(4) for b in range(band)] for y in range(4)]
+    over_others = lambda lines: lax.all_to_all(lines, ("tm", "band"), 0, 0, tiled=True, axis_index_groups=others)
+    around = lambda line, by: lax.ppermute(line, "tm", [(i, i - i % 4 + (i + by) % 4) for i in range(tm)])
+
+    def over_y(lines, members, count, *ready):
+        return pl.pallas_call(
+            functools.partial(ring_merge_kernel, members),
+            out_shape=line(count),
+            in_specs=[vmem] * (4 + len(ready)),
+            out_specs=vmem,
+            compiler_params=small,
+            cost_estimate=pl.CostEstimate(flops=20 * 10**9, bytes_accessed=0, transcendentals=0),
+            name="merge_y",
+        )(lines, *[around(lines, by) for by in (2, 1, 3)], *ready)
+
+    lines = pl.pallas_call(
+        functools.partial(merge_kernel, members),
+        out_shape=line(8),
+        in_specs=[vmem],
+        out_specs=vmem,
+        compiler_params=small,
+        name="merge",
+    )(over_others(lines))
+    cross, pair = pl.pallas_call(
+        edges_kernel,
+        out_shape=[block(frames + 2, 2), block(frames + 2, 2)],
         in_specs=[vmem] * 3,
-        out_specs=[vmem] * 3,
+        out_specs=[vmem] * 2,
         compiler_params=small,
         cost_estimate=pl.CostEstimate(flops=4 * 10**9, bytes_accessed=0, transcendentals=0),
         name="edges",
-    )(lines, kept, prev)
+    )(kept, prev, lines)
+    cross = swapped(cross, "band", 1)
     pair = swapped(pair, "band", 0)
-    cross = swapped(cross, "band", 1)
-    lines = spread_over(lines, "tm")
-
-    hidden, lines = pl.pallas_call(
-        functools.partial(first_kernel, members),
-        out_shape=[block(frames, rows + 2), line(8)],
-        in_specs=[vmem] * 7,
-        out_specs=[vmem, vmem],
-        scratch_shapes=[held(4, rows + 4), mixed],
+    first_weight = taps(first_weight)
+    lines = over_y(lines, 64 * members, 8, first_weight)
+
+    hidden, act, mixed_weight = pl.pallas_call(
+        functools.partial(inner_kernel, members),
+        out_shape=[
+            block(frames, rows + 2),
+            block(4, rows + 4),
+            jax.ShapeDtypeStruct((2, 3, 3, channels, outputs), jnp.bfloat16),
+        ],
+        in_specs=[vmem] * 5,
+        out_specs=[vmem] * 3,
         compiler_params=params,
-        name="first_conv",
-    )(kept, prev, pair, cross, lines, vectors, taps(first_weight))
-
-    xz = [[(4 * x + y) * band + b for x in range(4) for b in range(band)] for y in range(4)]
-    def rot(v, by):
-        return lax.ppermute(v, "tm", [(i, i - i % 4 + (i + by) % 4) for i in range(tm)])
-    got = [rot(lines, by) for by in (2, 1, 3)]
-    lines = pl.pallas_call(
-        functools.partial(ring_merge_kernel, members),
-        out_shape=line(64),
-        in_specs=[vmem] * 4,
-        out_specs=vmem,
-        compiler_params=small,
-        cost_estimate=pl.CostEstimate(flops=20 * 10**9, bytes_accessed=0, transcendentals=0),
-        name="merge",
-    )(lines, *got)
+        name="first_conv_inner",
+    )(kept, prev, lines, vectors, first_weight)
+    hidden, _, lines = pl.pallas_call(
+        functools.partial(outer_kernel, members),
+        out_shape=[block(frames, rows + 2), block(4, rows + 4), line(8)],
+        in_specs=[vmem] * 10,
+        out_specs=[vmem] * 3,
+        input_output_aliases={8: 0, 9: 1},
+        compiler_params=params,
+        name="first_conv_outer",
+    )(kept, prev, cross, pair, lines, vectors, first_weight, mixed_weight, hidden, act)
+
     prev = next_frames(hidden)
-    lines = lax.all_to_all(lines, ("tm", "band"), 0, 0, tiled=True, axis_index_groups=xz)
+    lines = over_others(over_y(lines, members, 64))
 
     return pl.pallas_call(
         functools.partial(second_kernel, members),

time: 70.5 us -> 69 us (0.979)
  blocking collectives: 46 us -> 38 us
  starting transfers between devices: 13.4 us -> 18.4 us
  waiting for transfers between devices: 0.02 us -> 1.07 us
    all_to_all x2 -> x0, blocking collectives: 28.9 us -> none  [local(): lax.all_to_all(lines, axis, 0, 0, tiled=True)]
    all_to_all x1 -> x2, blocking collectives: 17.1 us -> 38 us  [local(): lax.all_to_all(lines, ('tm', 'band'), 0, 0, tiled=True, axis_index_groups...]
    ppermute x3 -> x6, starting transfers between devices: 2.39 us -> 7.07 us  [local(): lax.ppermute(line, 'tm', [(i, i - i % 4 + (i + by) % 4) for i in range(tm)])]
    ppermute x2, waiting for transfers between devices: 0.01 us -> 1.05 us  [swapped(): return lax.ppermute(value, axis, pairs)]
    ppermute x2, starting transfers between devices: 3.04 us -> 4 us  [swapped(): return lax.ppermute(value, axis, pairs)]
    pallas_call x4 -> x7, Pallas kernels: 6.22 us -> 6.76 us  [the longest x1 2.75 us: local(): pl.pallas_call(functools.partial(inner_kernel, members), out_shape=[block...]
  transfers between devices with their start and end apart: 7 -> 10, of which waited for: 0 -> 1; matrix products, arithmetic and copies ran while one was open for 0% -> 0% of each run, Pallas kernels for 2% -> 7%
where the time goes in v7:
time: 69 us; the launch traced here: 68.8 us
  blocking collectives  38 us (55%)
  starting transfers between devices  18.4 us (27%)
  Pallas kernels  11 us (16%)
  waiting for transfers between devices  1.07 us (2%)
    all_to_all x2, blocking collectives, local(): lax.all_to_all(lines, ('tm', 'band'), 0, 0, tiled=True, axis_index_groups...  38 us
    ppermute x2, starting transfers between devices, next_frames(): return lax.ppermute(value, 'tm', [(i, i + 1) for i in range(count - 1)])  7.33 us
    ppermute x6, starting transfers between devices, local(): lax.ppermute(line, 'tm', [(i, i - i % 4 + (i + by) % 4) for i in range(tm)])  7.07 us
    pallas_call x1, Pallas kernels, local(): pl.pallas_call(functools.partial(second_kernel, members), out_shape=block...  4.27 us
    ppermute x2, starting transfers between devices, swapped(): return lax.ppermute(value, axis, pairs)  4 us
    pallas_call x1, Pallas kernels, local(): pl.pallas_call(functools.partial(inner_kernel, members), out_shape=[block...  2.75 us
    pallas_call x1, Pallas kernels, local(): pl.pallas_call(functools.partial(outer_kernel, members), out_shape=[block...  2.15 us
    pallas_call x1, Pallas kernels, local(): pl.pallas_call(stats_kernel, out_shape=[line(64), block(frames, rows), ja...  1.53 us
  transfers between devices with their start and end apart: 10, of which 1 were waited for; matrix products, arithmetic and copies ran while one was open for 0% of the time, Pallas kernels for 7%

profile of v7, /device:TPU:1, one launch (start us, length us, event | category | flops | bytes accessed | tf_op | source)
XLA Modules:
  0.0 68.8 jit_solution(14861422703559856137)
XLA Ops:
  0.0 4.0 %collective-permute-start = (bf16[2,8,64,256]{3,2,1,0:T(8,128)(2,1)}, bf16[2,8,64,256]{3,2,1,0:T(8,128)(2,1)S(1)}, u32[]{:S(2)}, u32[]{:S(2)}) collective-permute-start(bf16[2,8,64,256]{3,2,1,0:T(8,128)(2,1)} %x_ref.1), channel_id=1, source_target_pairs={{0,16},{16,32},{32,48},{48,64},{64,80},{80,96},{96,112},{112,128},... | collective-permute-start | bytes 1572872 | tf_op jit(solution)/shard_map/ppermute | solution.py:18
  4.1 1.5 %moments.1 = (f32[64,128]{1,0:T(8,128)S(1)}, bf16[2,8,64,256]{3,2,1,0:T(8,128)(2,1)S(1)}, f32[8,256]{1,0:T(8,128)S(1)}) custom-call(bf16[2,8,64,256]{3,2,1,0:T(8,128)(2,1)} %x_ref.1, f32[1,256]{1,0:T(1,128)} %bitcast.22, f32[1,256]{1,0:T(1,128)} %bitcast.23, f32[1,256]{1,0:T(1,128)} %bitcast.24, f32[1,256]{1,0:T(1,128)} %bitcast.25), custom_call_target="tpu_custom_call" | custom-call | tf_op jit(solution)/shard_map/moments/pallas_call | solution.py:290
  5.6 21.5 %all_to_all.22 = f32[64,1,128]{2,1,0:T(1,128)S(1)} all-to-all(f32[64,1,128]{2,1,0:T(1,128)S(1)} %bitcast.21), channel_id=1, replica_groups={{0,1,2,3,4,5,6,7,8,9,10,11,12,13,14,15,64,65,66,67,68,69,70,71,72,73,74..., dimensions={0} | all-to-all | bytes 65536 | tf_op jit(solution)/shard_map/all_to_all | solution.py:300
  27.1 0.1 merge.1.after_ref.a_ref
  27.2 2.0 %collective-permute-start.5 = (f32[8,128]{1,0:T(8,128)S(1)}, f32[8,128]{1,0:T(8,128)S(1)}, u32[]{:S(2)}, u32[]{:S(2)}) collective-permute-start(f32[8,128]{1,0:T(8,128)S(1)} %merge.1.after_ref.a_ref), channel_id=1, source_target_pairs={{0,48},{16,0},{32,16},{48,32},{64,112},{80,64},{96,80},{112,96},{1... | collective-permute-start | bytes 12296 | tf_op jit(solution)/shard_map/ppermute | solution.py:301
  29.2 0.0 collective-permute-start.4
  29.2 2.1 %collective-permute-start.3 = (f32[8,128]{1,0:T(8,128)S(1)}, f32[8,128]{1,0:T(8,128)S(1)}, u32[]{:S(2)}, u32[]{:S(2)}) collective-permute-start(f32[8,128]{1,0:T(8,128)S(1)} %merge.1.after_ref.a_ref), channel_id=1, source_target_pairs={{0,32},{16,48},{32,0},{48,16},{64,96},{80,112},{96,64},{112,80},{1... | collective-permute-start | bytes 12296 | tf_op jit(solution)/shard_map/ppermute | solution.py:301
  31.3 0.0 collective-permute-done.prev_ref
  31.3 3.9 %collective-permute-start.1 = (bf16[4,2,64,256]{3,2,1,0:T(8,128)(2,1)S(1)}, bf16[4,2,64,256]{3,2,1,0:T(8,128)(2,1)S(1)}, u32[]{:S(2)}, u32[]{:S(2)}) collective-permute-start(bf16[4,2,64,256]{3,2,1,0:T(8,128)(2,1)S(1)} %get-tuple-element.17), channel_id=1, source_target_pairs={{1,2},{2,1},{3,4},{4,3},{5,6},{6,5},{7,8},{8,7},{9,10},{10,9},{11,... | collective-permute-start | bytes 786440 | tf_op jit(solution)/shard_map/ppermute | solution.py:26
  35.3 0.1 collective-permute-start.2
  35.4 0.0 collective-permute-done.5.d_ref
  35.4 0.0 collective-permute-done.4.c_ref
  35.4 0.0 collective-permute-done.3.b_ref
  35.4 0.0 copy-done
  35.4 0.1 merge_y.2.lines_ref
  35.5 2.7 %first_conv_inner.1 = (bf16[2,10,64,256]{3,2,1,0:T(8,128)(2,1)S(1)}, bf16[4,12,64,256]{3,2,1,0:T(8,128)(2,1)S(1)}, bf16[2,3,3,256,256]{4,3,2,1,0:T(8,128)(2,1)S(1)}) custom-call(bf16[2,8,64,256]{3,2,1,0:T(8,128)(2,1)S(1)} %get-tuple-element.15.x_ref, bf16[2,8,64,256]{3,2,1,0:T(8,128)(2,1)S(1)} %collective-permute-done.prev_ref, ...), custom_call_target="tpu_custom_call" | custom-call | tf_op jit(solution)/shard_map/first_conv_inner/pallas_call | solution.py:336
  38.2 1.0 %collective-permute-done.1.cross_ref = bf16[4,2,64,256]{3,2,1,0:T(8,128)(2,1)S(1)} collective-permute-done((bf16[4,2,64,256]{3,2,1,0:T(8,128)(2,1)S(1)}, bf16[4,2,64,256]{3,2,1,0:T(8,128)(2,1)S(1)}, u32[]{:S(2)}, u32[]{:S(2)}) %collective-permute-start.1) | collective-permute-done | bytes 262176 | tf_op jit(solution)/shard_map/ppermute | solution.py:26
  39.3 0.0 collective-permute-done.2.pair_ref
  39.3 2.1 %first_conv_outer.1 = (bf16[2,10,64,256]{3,2,1,0:T(8,128)(2,1)S(1)}, bf16[4,12,64,256]{3,2,1,0:T(8,128)(2,1)S(1)}, f32[8,128]{1,0:T(8,128)S(1)}) custom-call(bf16[2,8,64,256]{3,2,1,0:T(8,128)(2,1)S(1)} %get-tuple-element.15.x_ref, bf16[2,8,64,256]{3,2,1,0:T(8,128)(2,1)S(1)} %collective-permute-done.prev_ref, ...), custom_call_target="tpu_custom_call", output_to_operand_aliasing={{0}: (8, {}), {1}: (9, {})} | custom-call | tf_op jit(solution)/shard_map/first_conv_outer/pallas_call | solution.py:348
  41.4 1.1 %collective-permute-start.9 = (f32[8,128]{1,0:T(8,128)S(1)}, f32[8,128]{1,0:T(8,128)S(1)}, u32[]{:S(2)}, u32[]{:S(2)}) collective-permute-start(f32[8,128]{1,0:T(8,128)S(1)} %get-tuple-element.24.a_ref), channel_id=1, source_target_pairs={{0,48},{16,0},{32,16},{48,32},{64,112},{80,64},{96,80},{112,96},{1... | collective-permute-start | bytes 12296 | tf_op jit(solution)/shard_map/ppermute | solution.py:301
  42.5 0.4 collective-permute-start.8
  42.9 1.5 %collective-permute-start.7 = (f32[8,128]{1,0:T(8,128)S(1)}, f32[8,128]{1,0:T(8,128)S(1)}, u32[]{:S(2)}, u32[]{:S(2)}) collective-permute-start(f32[8,128]{1,0:T(8,128)S(1)} %get-tuple-element.24.a_ref), channel_id=1, source_target_pairs={{0,32},{16,48},{32,0},{48,16},{64,96},{80,112},{96,64},{112,80},{1... | collective-permute-start | bytes 12296 | tf_op jit(solution)/shard_map/ppermute | solution.py:301
  44.4 3.3 %collective-permute-start.6 = (bf16[2,10,64,256]{3,2,1,0:T(8,128)(2,1)S(1)}, bf16[2,10,64,256]{3,2,1,0:T(8,128)(2,1)S(1)}, u32[]{:S(2)}, u32[]{:S(2)}) collective-permute-start(bf16[2,10,64,256]{3,2,1,0:T(8,128)(2,1)S(1)} %get-tuple-element.23.hidden_ref), channel_id=1, source_target_pairs={{0,16},{16,32},{32,48},{48,64},{64,80},{80,96},{96,112},{112,128},... | collective-permute-start | bytes 1966088 | tf_op jit(solution)/shard_map/ppermute | solution.py:18
  47.7 0.0 collective-permute-done.9.d_ref
  47.7 0.0 collective-permute-done.8.c_ref
  47.7 0.0 collective-permute-done.7.b_ref
  47.7 0.0 copy-start.1
  47.8 0.1 merge_y.3
  47.9 16.5 %all_to_all.23 = f32[64,1,128]{2,1,0:T(1,128)S(1)} all-to-all(f32[64,1,128]{2,1,0:T(1,128)S(1)} %bitcast.20), channel_id=1, replica_groups={{0,1,2,3,4,5,6,7,8,9,10,11,12,13,14,15,64,65,66,67,68,69,70,71,72,73,74..., dimensions={0} | all-to-all | bytes 65536 | tf_op jit(solution)/shard_map/all_to_all | solution.py:300
  64.4 0.0 collective-permute-done.6.prev_ref
  64.4 0.0 copy-done.1
  64.4 4.3 %second_conv.1 = bf16[2,8,64,256]{3,2,1,0:T(8,128)(2,1)} custom-call(bf16[2,10,64,256]{3,2,1,0:T(8,128)(2,1)S(1)} %get-tuple-element.23.hidden_ref, bf16[2,10,64,256]{3,2,1,0:T(8,128)(2,1)S(1)} %collective-permute-done.6.prev_ref, f32[64,128]{1,0:T(8,128)S(1)} %bitcast.18, f32[8,256]{1,0:T(8,128)S(1)} %get-tuple-element.19.params_ref, ...), custom_call_target="tpu_custom_call" | custom-call | tf_op jit(solution)/shard_map/second_conv/pallas_call | solution.py:361
  (2 shorter events, 0.0 us)
Async XLA Ops:
  0.0 31.3 %collective-permute-start = (bf16[2,8,64,256]{3,2,1,0:T(8,128)(2,1)}, bf16[2,8,64,256]{3,2,1,0:T(8,128)(2,1)S(1)}, u32[]{:S(2)}, u32[]{:S(2)}) collective-permute-start(bf16[2,8,64,256]{3,2,1,0:T(8,128)(2,1)} %x_ref.1), channel_id=1, source_target_pairs={{0,16},{16,32},{32,48},{48,64},{64,80},{80,96},{96,112},{112,128},... | collective-permute-start | bytes 1572872 | tf_op jit(solution)/shard_map/ppermute | solution.py:18
  27.2 8.2 %collective-permute-start.5 = (f32[8,128]{1,0:T(8,128)S(1)}, f32[8,128]{1,0:T(8,128)S(1)}, u32[]{:S(2)}, u32[]{:S(2)}) collective-permute-start(f32[8,128]{1,0:T(8,128)S(1)} %merge.1.after_ref.a_ref), channel_id=1, source_target_pairs={{0,48},{16,0},{32,16},{48,32},{64,112},{80,64},{96,80},{112,96},{1... | collective-permute-start | bytes 12296 | tf_op jit(solution)/shard_map/ppermute | solution.py:301
  29.2 6.2 %collective-permute-start.4 = (f32[8,128]{1,0:T(8,128)S(1)}, f32[8,128]{1,0:T(8,128)S(1)}, u32[]{:S(2)}, u32[]{:S(2)}) collective-permute-start(f32[8,128]{1,0:T(8,128)S(1)} %merge.1.after_ref.a_ref), channel_id=1, source_target_pairs={{0,16},{16,32},{32,48},{48,0},{64,80},{80,96},{96,112},{112,64},{1... | collective-permute-start | bytes 12296 | tf_op jit(solution)/shard_map/ppermute | solution.py:301
  29.2 6.2 %collective-permute-start.3 = (f32[8,128]{1,0:T(8,128)S(1)}, f32[8,128]{1,0:T(8,128)S(1)}, u32[]{:S(2)}, u32[]{:S(2)}) collective-permute-start(f32[8,128]{1,0:T(8,128)S(1)} %merge.1.after_ref.a_ref), channel_id=1, source_target_pairs={{0,32},{16,48},{32,0},{48,16},{64,96},{80,112},{96,64},{112,80},{1... | collective-permute-start | bytes 12296 | tf_op jit(solution)/shard_map/ppermute | solution.py:301
  31.3 4.1 %copy-start = (bf16[3,3,3,256,256]{4,3,2,1,0:T(8,128)(2,1)S(1)}, bf16[3,3,3,256,256]{4,3,2,1,0:T(8,128)(2,1)}, u32[]{:S(2)}) copy-start(bf16[3,3,3,256,256]{4,3,2,1,0:T(8,128)(2,1)} %param.10) | copy-start | bytes 10616836
  31.3 8.0 %collective-permute-start.1 = (bf16[4,2,64,256]{3,2,1,0:T(8,128)(2,1)S(1)}, bf16[4,2,64,256]{3,2,1,0:T(8,128)(2,1)S(1)}, u32[]{:S(2)}, u32[]{:S(2)}) collective-permute-start(bf16[4,2,64,256]{3,2,1,0:T(8,128)(2,1)S(1)} %get-tuple-element.17), channel_id=1, source_target_pairs={{1,2},{2,1},{3,4},{4,3},{5,6},{6,5},{7,8},{8,7},{9,10},{10,9},{11,... | collective-permute-start | bytes 786440 | tf_op jit(solution)/shard_map/ppermute | solution.py:26
  35.3 4.0 %collective-permute-start.2 = (bf16[4,2,64,256]{3,2,1,0:T(8,128)(2,1)S(1)}, bf16[4,2,64,256]{3,2,1,0:T(8,128)(2,1)S(1)}, u32[]{:S(2)}, u32[]{:S(2)}) collective-permute-start(bf16[4,2,64,256]{3,2,1,0:T(8,128)(2,1)S(1)} %get-tuple-element.18), channel_id=1, source_target_pairs={{0,1},{1,0},{2,3},{3,2},{4,5},{5,4},{6,7},{7,6},{8,9},{9,8},{10,11... | collective-permute-start | bytes 786440 | tf_op jit(solution)/shard_map/ppermute | solution.py:26
  41.4 6.3 %collective-permute-start.9 = (f32[8,128]{1,0:T(8,128)S(1)}, f32[8,128]{1,0:T(8,128)S(1)}, u32[]{:S(2)}, u32[]{:S(2)}) collective-permute-start(f32[8,128]{1,0:T(8,128)S(1)} %get-tuple-element.24.a_ref), channel_id=1, source_target_pairs={{0,48},{16,0},{32,16},{48,32},{64,112},{80,64},{96,80},{112,96},{1... | collective-permute-start | bytes 12296 | tf_op jit(solution)/shard_map/ppermute | solution.py:301
  42.5 5.2 %collective-permute-start.8 = (f32[8,128]{1,0:T(8,128)S(1)}, f32[8,128]{1,0:T(8,128)S(1)}, u32[]{:S(2)}, u32[]{:S(2)}) collective-permute-start(f32[8,128]{1,0:T(8,128)S(1)} %get-tuple-element.24.a_ref), channel_id=1, source_target_pairs={{0,16},{16,32},{32,48},{48,0},{64,80},{80,96},{96,112},{112,64},{1... | collective-permute-start | bytes 12296 | tf_op jit(solution)/shard_map/ppermute | solution.py:301
  42.9 4.8 %collective-permute-start.7 = (f32[8,128]{1,0:T(8,128)S(1)}, f32[8,128]{1,0:T(8,128)S(1)}, u32[]{:S(2)}, u32[]{:S(2)}) collective-permute-start(f32[8,128]{1,0:T(8,128)S(1)} %get-tuple-element.24.a_ref), channel_id=1, source_target_pairs={{0,32},{16,48},{32,0},{48,16},{64,96},{80,112},{96,64},{112,80},{1... | collective-permute-start | bytes 12296 | tf_op jit(solution)/shard_map/ppermute | solution.py:301
  44.4 19.9 %collective-permute-start.6 = (bf16[2,10,64,256]{3,2,1,0:T(8,128)(2,1)S(1)}, bf16[2,10,64,256]{3,2,1,0:T(8,128)(2,1)S(1)}, u32[]{:S(2)}, u32[]{:S(2)}) collective-permute-start(bf16[2,10,64,256]{3,2,1,0:T(8,128)(2,1)S(1)} %get-tuple-element.23.hidden_ref), channel_id=1, source_target_pairs={{0,16},{16,32},{32,48},{48,64},{64,80},{80,96},{96,112},{112,128},... | collective-permute-start | bytes 1966088 | tf_op jit(solution)/shard_map/ppermute | solution.py:18
  47.7 16.6 %copy-start.1 = (bf16[3,3,3,256,256]{4,3,2,1,0:T(8,128)(2,1)S(1)}, bf16[3,3,3,256,256]{4,3,2,1,0:T(8,128)(2,1)}, u32[]{:S(2)}) copy-start(bf16[3,3,3,256,256]{4,3,2,1,0:T(8,128)(2,1)} %param.13) | copy-start | bytes 10616836

commit v8 on v7

--- a/solution.py
+++ b/solution.py
@@ -115,7 +115,7 @@
         jnp.concatenate(
             [
                 jnp.concatenate(
-                    [act_ref[part, first + j : first + j + count].reshape(count * cols, channels) for first, count in pieces]
+                    [act_ref[part, pl.ds(first + j, count)].reshape(count * cols, channels) for first, count in pieces]
                 )
                 for j in range(3)
             ],
@@ -197,42 +197,40 @@
     for f, value in enumerate(convolved(act_ref, weight_ref, mixed_ref, pieces)):
         done = 0
         for first, count in pieces:
-            out_ref[f, first : first + count] = value[done : done + count].astype(jnp.bfloat16)
+            out_ref[f, pl.ds(first, count)] = value[done : done + count].astype(jnp.bfloat16)
             done += count
 
 
-def inner_kernel(members, x_ref, prev_ref, lines_ref, params_ref, weight_ref, hidden_ref, act_ref, mixed_ref):
+def inner_kernel(members, x_ref, prev_ref, pair_ref, lines_ref, params_ref, weight_ref, hidden_ref, act_ref, mixed_ref):
     rows = x_ref.shape[1]
     leading, _, _ = at_ends()
+    pair_at, _, _, _ = places(rows)
     norm = scaling(lines_ref, params_ref, 0, members)
+
+    def row(at, before, own):
+        before = [jnp.where(leading, own[0], x) for x in before]
+        mixed_frames(act_ref, at, [activated(x, *norm) for x in before + own])
+
     for r in range(rows):
-        own = [x_ref[f, r] for f in range(2)]
-        before = [jnp.where(leading, own[0], prev_ref[f, r]) for f in range(2)]
-        mixed_frames(act_ref, r + 2, [activated(x, *norm) for x in before + own])
+        row(r + 2, [prev_ref[f, r] for f in range(2)], [x_ref[f, r] for f in range(2)])
+    for r in range(2):
+        row(pair_at + r, [pair_ref[f, r] for f in (0, 1)], [pair_ref[f, r] for f in (2, 3)])
     mix_weight(weight_ref, mixed_ref)
-    first_rows(act_ref, hidden_ref, weight_ref, mixed_ref, [(2, rows - 2)])
-
-
-def outer_kernel(members, x_ref, prev_ref, cross_ref, pair_ref, lines_ref, params_ref, weight_ref, mixed_ref, _, __,
+    first_rows(act_ref, hidden_ref, weight_ref, mixed_ref, [(2, rows - 2), (jnp.minimum(pair_at, rows), 2)])
+
+
+def outer_kernel(members, x_ref, prev_ref, cross_ref, lines_ref, params_ref, weight_ref, mixed_ref, _, __,
                  hidden_ref, act_ref, line_ref):
     frames, rows, _, channels = x_ref.shape
     leading, top, bottom = at_ends()
-    even = lax.rem(lax.axis_index("band"), 2) == 0
+    _, cross_at, _, _ = places(rows)
     norm = scaling(lines_ref, params_ref, 0, members)
-
-    def row_of(f, r):
-        inner = prev_ref if f < 2 else x_ref
-        if r < 2:
-            outer = jnp.where(even, cross_ref[f, r], pair_ref[f, r])
-            return jnp.where(top, inner[f % 2, 0], outer) if r == 1 else outer
-        outer = jnp.where(even, pair_ref[f, r - rows - 2], cross_ref[f, r - rows - 2])
-        return jnp.where(bottom, inner[f % 2, rows - 1], outer) if r == rows + 2 else outer
-
-    for r in (0, 1, rows + 2, rows + 3):
-        own = [row_of(f, r) for f in (2, 3)]
-        before = [jnp.where(leading, own[0], row_of(f, r)) for f in (0, 1)]
-        mixed_frames(act_ref, r, [activated(x, *norm) for x in before + own])
-    first_rows(act_ref, hidden_ref, weight_ref, mixed_ref, [(0, 2), (rows, 2)])
+    for r in range(2):
+        rim = [jnp.where(top, ref[f, 0], ref[f, rows - 1]) for ref in (prev_ref, x_ref) for f in range(2)]
+        values = [jnp.where(top | bottom, rim[f], cross_ref[f, r]) for f in range(4)]
+        before = [jnp.where(leading, values[2], x) for x in values[:2]]
+        mixed_frames(act_ref, cross_at + r, [activated(x, *norm) for x in before + values[2:]])
+    first_rows(act_ref, hidden_ref, weight_ref, mixed_ref, [(jnp.minimum(cross_at, rows), 2)])
     reads = [functools.partial(lambda f, r: hidden_ref[f, r + 1], f, r) for f in range(frames) for r in range(rows)]
     line_ref[...] = jnp.broadcast_to(local_moments(reads, channels), line_ref.shape)
 
@@ -331,7 +329,7 @@
     cross = swapped(cross, "band", 1)
     pair = swapped(pair, "band", 0)
     first_weight = taps(first_weight)
-    lines = over_y(lines, 64 * members, 8, first_weight)
+    lines = over_y(lines, 64 * members, 8, first_weight, pair)
 
     hidden, act, mixed_weight = pl.pallas_call(
         functools.partial(inner_kernel, members),
@@ -340,20 +338,20 @@
             block(4, rows + 4),
             jax.ShapeDtypeStruct((2, 3, 3, channels, outputs), jnp.bfloat16),
         ],
-        in_specs=[vmem] * 5,
+        in_specs=[vmem] * 6,
         out_specs=[vmem] * 3,
         compiler_params=params,
         name="first_conv_inner",
-    )(kept, prev, lines, vectors, first_weight)
+    )(kept, prev, pair, lines, vectors, first_weight)
     hidden, _, lines = pl.pallas_call(
         functools.partial(outer_kernel, members),
         out_shape=[block(frames, rows + 2), block(4, rows + 4), line(8)],
-        in_specs=[vmem] * 10,
+        in_specs=[vmem] * 9,
         out_specs=[vmem] * 3,
-        input_output_aliases={8: 0, 9: 1},
+        input_output_aliases={7: 0, 8: 1},
         compiler_params=params,
         name="first_conv_outer",
-    )(kept, prev, cross, pair, lines, vectors, first_weight, mixed_weight, hidden, act)
+    )(kept, prev, cross, lines, vectors, first_weight, mixed_weight, hidden, act)
 
     prev = next_frames(hidden)
     lines = over_others(over_y(lines, members, 64))

time: 69 us -> 68.3 us (0.990)
    pallas_call x1, Pallas kernels: 2.75 us -> 3.53 us  [local(): pl.pallas_call(functools.partial(inner_kernel, members), out_shape=[block...]
  transfers between devices with their start and end apart: 10 -> 10, of which waited for: 1 -> 1; matrix products, arithmetic and copies ran while one was open for 0% -> 0% of each run, Pallas kernels for 7% -> 8%
where the time goes in v8:
time: 68.3 us; the launch traced here: 68.1 us
  blocking collectives  37.4 us (55%)
  starting transfers between devices  18.2 us (27%)
  Pallas kernels  11.2 us (16%)
  waiting for transfers between devices  0.96 us (1%)
    all_to_all x2, blocking collectives, local(): lax.all_to_all(lines, ('tm', 'band'), 0, 0, tiled=True, axis_index_groups...  37.4 us
    ppermute x2, starting transfers between devices, next_frames(): return lax.ppermute(value, 'tm', [(i, i + 1) for i in range(count - 1)])  7.33 us
    ppermute x6, starting transfers between devices, local(): lax.ppermute(line, 'tm', [(i, i - i % 4 + (i + by) % 4) for i in range(tm)])  7.08 us
    pallas_call x1, Pallas kernels, local(): pl.pallas_call(functools.partial(second_kernel, members), out_shape=block...  4.27 us
    ppermute x2, starting transfers between devices, swapped(): return lax.ppermute(value, axis, pairs)  3.8 us
    pallas_call x1, Pallas kernels, local(): pl.pallas_call(functools.partial(inner_kernel, members), out_shape=[block...  3.53 us
    pallas_call x1, Pallas kernels, local(): pl.pallas_call(functools.partial(outer_kernel, members), out_shape=[block...  1.55 us
    pallas_call x1, Pallas kernels, local(): pl.pallas_call(stats_kernel, out_shape=[line(64), block(frames, rows), ja...  1.53 us
  transfers between devices with their start and end apart: 10, of which 1 were waited for; matrix products, arithmetic and copies ran while one was open for 0% of the time, Pallas kernels for 8%

profile of v8, /device:TPU:1, one launch (start us, length us, event | category | flops | bytes accessed | tf_op | source)
XLA Modules:
  0.0 68.1 jit_solution(5790389994820549820)
XLA Ops:
  0.0 4.0 %collective-permute-start = (bf16[2,8,64,256]{3,2,1,0:T(8,128)(2,1)}, bf16[2,8,64,256]{3,2,1,0:T(8,128)(2,1)S(1)}, u32[]{:S(2)}, u32[]{:S(2)}) collective-permute-start(bf16[2,8,64,256]{3,2,1,0:T(8,128)(2,1)} %x_ref.1), channel_id=1, source_target_pairs={{0,16},{16,32},{32,48},{48,64},{64,80},{80,96},{96,112},{112,128},... | collective-permute-start | bytes 1572872 | tf_op jit(solution)/shard_map/ppermute | solution.py:18
  4.1 1.5 %moments.1 = (f32[64,128]{1,0:T(8,128)S(1)}, bf16[2,8,64,256]{3,2,1,0:T(8,128)(2,1)S(1)}, f32[8,256]{1,0:T(8,128)S(1)}) custom-call(bf16[2,8,64,256]{3,2,1,0:T(8,128)(2,1)} %x_ref.1, f32[1,256]{1,0:T(1,128)} %bitcast.22, f32[1,256]{1,0:T(1,128)} %bitcast.23, f32[1,256]{1,0:T(1,128)} %bitcast.24, f32[1,256]{1,0:T(1,128)} %bitcast.25), custom_call_target="tpu_custom_call" | custom-call | tf_op jit(solution)/shard_map/moments/pallas_call | solution.py:288
  5.6 21.5 %all_to_all.22 = f32[64,1,128]{2,1,0:T(1,128)S(1)} all-to-all(f32[64,1,128]{2,1,0:T(1,128)S(1)} %bitcast.21), channel_id=1, replica_groups={{0,1,2,3,4,5,6,7,8,9,10,11,12,13,14,15,64,65,66,67,68,69,70,71,72,73,74..., dimensions={0} | all-to-all | bytes 65536 | tf_op jit(solution)/shard_map/all_to_all | solution.py:298
  27.1 0.1 merge.1.after_ref.a_ref
  27.2 0.0 collective-permute-done.prev_ref
  27.2 0.8 %collective-permute-start.5 = (bf16[4,2,64,256]{3,2,1,0:T(8,128)(2,1)S(1)}, bf16[4,2,64,256]{3,2,1,0:T(8,128)(2,1)S(1)}, u32[]{:S(2)}, u32[]{:S(2)}) collective-permute-start(bf16[4,2,64,256]{3,2,1,0:T(8,128)(2,1)S(1)} %get-tuple-element.18), channel_id=1, source_target_pairs={{0,1},{1,0},{2,3},{3,2},{4,5},{5,4},{6,7},{7,6},{8,9},{9,8},{10,11... | collective-permute-start | bytes 786440 | tf_op jit(solution)/shard_map/ppermute | solution.py:26
  28.0 2.0 %collective-permute-start.4 = (f32[8,128]{1,0:T(8,128)S(1)}, f32[8,128]{1,0:T(8,128)S(1)}, u32[]{:S(2)}, u32[]{:S(2)}) collective-permute-start(f32[8,128]{1,0:T(8,128)S(1)} %merge.1.after_ref.a_ref), channel_id=1, source_target_pairs={{0,48},{16,0},{32,16},{48,32},{64,112},{80,64},{96,80},{112,96},{1... | collective-permute-start | bytes 12296 | tf_op jit(solution)/shard_map/ppermute | solution.py:299
  30.0 0.0 collective-permute-start.3
  30.0 2.1 %collective-permute-start.2 = (f32[8,128]{1,0:T(8,128)S(1)}, f32[8,128]{1,0:T(8,128)S(1)}, u32[]{:S(2)}, u32[]{:S(2)}) collective-permute-start(f32[8,128]{1,0:T(8,128)S(1)} %merge.1.after_ref.a_ref), channel_id=1, source_target_pairs={{0,32},{16,48},{32,0},{48,16},{64,96},{80,112},{96,64},{112,80},{1... | collective-permute-start | bytes 12296 | tf_op jit(solution)/shard_map/ppermute | solution.py:299
  32.1 3.0 %collective-permute-start.1 = (bf16[4,2,64,256]{3,2,1,0:T(8,128)(2,1)S(1)}, bf16[4,2,64,256]{3,2,1,0:T(8,128)(2,1)S(1)}, u32[]{:S(2)}, u32[]{:S(2)}) collective-permute-start(bf16[4,2,64,256]{3,2,1,0:T(8,128)(2,1)S(1)} %get-tuple-element.17), channel_id=1, source_target_pairs={{1,2},{2,1},{3,4},{4,3},{5,6},{6,5},{7,8},{8,7},{9,10},{10,9},{11,... | collective-permute-start | bytes 786440 | tf_op jit(solution)/shard_map/ppermute | solution.py:26
  35.1 0.0 collective-permute-done.4.d_ref
  35.2 0.0 collective-permute-done.3.c_ref
  35.2 0.0 collective-permute-done.2.b_ref
  35.2 0.0 collective-permute-done.5.refs_1_.pair_ref
  35.2 0.0 copy-done
  35.2 0.1 merge_y.2.lines_ref
  35.3 3.5 %first_conv_inner.1 = (bf16[2,10,64,256]{3,2,1,0:T(8,128)(2,1)S(1)}, bf16[4,12,64,256]{3,2,1,0:T(8,128)(2,1)S(1)}, bf16[2,3,3,256,256]{4,3,2,1,0:T(8,128)(2,1)S(1)}) custom-call(bf16[2,8,64,256]{3,2,1,0:T(8,128)(2,1)S(1)} %get-tuple-element.15.x_ref, bf16[2,8,64,256]{3,2,1,0:T(8,128)(2,1)S(1)} %collective-permute-done.prev_ref, ...), custom_call_target="tpu_custom_call" | custom-call | tf_op jit(solution)/shard_map/first_conv_inner/pallas_call | solution.py:334
  38.8 0.9 %collective-permute-done.1.cross_ref = bf16[4,2,64,256]{3,2,1,0:T(8,128)(2,1)S(1)} collective-permute-done((bf16[4,2,64,256]{3,2,1,0:T(8,128)(2,1)S(1)}, bf16[4,2,64,256]{3,2,1,0:T(8,128)(2,1)S(1)}, u32[]{:S(2)}, u32[]{:S(2)}) %collective-permute-start.1) | collective-permute-done | bytes 262176 | tf_op jit(solution)/shard_map/ppermute | solution.py:26
  39.8 1.6 %first_conv_outer.1 = (bf16[2,10,64,256]{3,2,1,0:T(8,128)(2,1)S(1)}, bf16[4,12,64,256]{3,2,1,0:T(8,128)(2,1)S(1)}, f32[8,128]{1,0:T(8,128)S(1)}) custom-call(bf16[2,8,64,256]{3,2,1,0:T(8,128)(2,1)S(1)} %get-tuple-element.15.x_ref, bf16[2,8,64,256]{3,2,1,0:T(8,128)(2,1)S(1)} %collective-permute-done.prev_ref, ...), custom_call_target="tpu_custom_call", output_to_operand_aliasing={{0}: (7, {}), {1}: (8, {})} | custom-call | tf_op jit(solution)/shard_map/first_conv_outer/pallas_call | solution.py:346
  41.3 1.1 %collective-permute-start.9 = (f32[8,128]{1,0:T(8,128)S(1)}, f32[8,128]{1,0:T(8,128)S(1)}, u32[]{:S(2)}, u32[]{:S(2)}) collective-permute-start(f32[8,128]{1,0:T(8,128)S(1)} %get-tuple-element.24.a_ref), channel_id=1, source_target_pairs={{0,48},{16,0},{32,16},{48,32},{64,112},{80,64},{96,80},{112,96},{1... | collective-permute-start | bytes 12296 | tf_op jit(solution)/shard_map/ppermute | solution.py:299
  42.4 0.4 collective-permute-start.8
  42.8 1.5 %collective-permute-start.7 = (f32[8,128]{1,0:T(8,128)S(1)}, f32[8,128]{1,0:T(8,128)S(1)}, u32[]{:S(2)}, u32[]{:S(2)}) collective-permute-start(f32[8,128]{1,0:T(8,128)S(1)} %get-tuple-element.24.a_ref), channel_id=1, source_target_pairs={{0,32},{16,48},{32,0},{48,16},{64,96},{80,112},{96,64},{112,80},{1... | collective-permute-start | bytes 12296 | tf_op jit(solution)/shard_map/ppermute | solution.py:299
  44.3 3.3 %collective-permute-start.6 = (bf16[2,10,64,256]{3,2,1,0:T(8,128)(2,1)S(1)}, bf16[2,10,64,256]{3,2,1,0:T(8,128)(2,1)S(1)}, u32[]{:S(2)}, u32[]{:S(2)}) collective-permute-start(bf16[2,10,64,256]{3,2,1,0:T(8,128)(2,1)S(1)} %get-tuple-element.23.hidden_ref), channel_id=1, source_target_pairs={{0,16},{16,32},{32,48},{48,64},{64,80},{80,96},{96,112},{112,128},... | collective-permute-start | bytes 1966088 | tf_op jit(solution)/shard_map/ppermute | solution.py:18
  47.6 0.0 collective-permute-done.9.d_ref
  47.6 0.0 collective-permute-done.8.c_ref
  47.6 0.0 collective-permute-done.7.b_ref
  47.6 0.0 copy-start.1
  47.6 0.1 merge_y.3
  47.7 15.9 %all_to_all.23 = f32[64,1,128]{2,1,0:T(1,128)S(1)} all-to-all(f32[64,1,128]{2,1,0:T(1,128)S(1)} %bitcast.20), channel_id=1, replica_groups={{0,1,2,3,4,5,6,7,8,9,10,11,12,13,14,15,64,65,66,67,68,69,70,71,72,73,74..., dimensions={0} | all-to-all | bytes 65536 | tf_op jit(solution)/shard_map/all_to_all | solution.py:298
  63.7 0.0 collective-permute-done.6.prev_ref
  63.7 0.0 copy-done.1
  63.7 4.3 %second_conv.1 = bf16[2,8,64,256]{3,2,1,0:T(8,128)(2,1)} custom-call(bf16[2,10,64,256]{3,2,1,0:T(8,128)(2,1)S(1)} %get-tuple-element.23.hidden_ref, bf16[2,10,64,256]{3,2,1,0:T(8,128)(2,1)S(1)} %collective-permute-done.6.prev_ref, f32[64,128]{1,0:T(8,128)S(1)} %bitcast.18, f32[8,256]{1,0:T(8,128)S(1)} %get-tuple-element.19.params_ref, ...), custom_call_target="tpu_custom_call" | custom-call | tf_op jit(solution)/shard_map/second_conv/pallas_call | solution.py:359
  (2 shorter events, 0.0 us)
Async XLA Ops:
  0.0 27.2 %collective-permute-start = (bf16[2,8,64,256]{3,2,1,0:T(8,128)(2,1)}, bf16[2,8,64,256]{3,2,1,0:T(8,128)(2,1)S(1)}, u32[]{:S(2)}, u32[]{:S(2)}) collective-permute-start(bf16[2,8,64,256]{3,2,1,0:T(8,128)(2,1)} %x_ref.1), channel_id=1, source_target_pairs={{0,16},{16,32},{32,48},{48,64},{64,80},{80,96},{96,112},{112,128},... | collective-permute-start | bytes 1572872 | tf_op jit(solution)/shard_map/ppermute | solution.py:18
  27.2 8.0 %copy-start = (bf16[3,3,3,256,256]{4,3,2,1,0:T(8,128)(2,1)S(1)}, bf16[3,3,3,256,256]{4,3,2,1,0:T(8,128)(2,1)}, u32[]{:S(2)}) copy-start(bf16[3,3,3,256,256]{4,3,2,1,0:T(8,128)(2,1)} %param.10) | copy-start | bytes 10616836
  27.2 7.9 %collective-permute-start.5 = (bf16[4,2,64,256]{3,2,1,0:T(8,128)(2,1)S(1)}, bf16[4,2,64,256]{3,2,1,0:T(8,128)(2,1)S(1)}, u32[]{:S(2)}, u32[]{:S(2)}) collective-permute-start(bf16[4,2,64,256]{3,2,1,0:T(8,128)(2,1)S(1)} %get-tuple-element.18), channel_id=1, source_target_pairs={{0,1},{1,0},{2,3},{3,2},{4,5},{5,4},{6,7},{7,6},{8,9},{9,8},{10,11... | collective-permute-start | bytes 786440 | tf_op jit(solution)/shard_map/ppermute | solution.py:26
  28.0 7.2 %collective-permute-start.4 = (f32[8,128]{1,0:T(8,128)S(1)}, f32[8,128]{1,0:T(8,128)S(1)}, u32[]{:S(2)}, u32[]{:S(2)}) collective-permute-start(f32[8,128]{1,0:T(8,128)S(1)} %merge.1.after_ref.a_ref), channel_id=1, source_target_pairs={{0,48},{16,0},{32,16},{48,32},{64,112},{80,64},{96,80},{112,96},{1... | collective-permute-start | bytes 12296 | tf_op jit(solution)/shard_map/ppermute | solution.py:299
  30.0 5.1 %collective-permute-start.3 = (f32[8,128]{1,0:T(8,128)S(1)}, f32[8,128]{1,0:T(8,128)S(1)}, u32[]{:S(2)}, u32[]{:S(2)}) collective-permute-start(f32[8,128]{1,0:T(8,128)S(1)} %merge.1.after_ref.a_ref), channel_id=1, source_target_pairs={{0,16},{16,32},{32,48},{48,0},{64,80},{80,96},{96,112},{112,64},{1... | collective-permute-start | bytes 12296 | tf_op jit(solution)/shard_map/ppermute | solution.py:299
  30.0 5.1 %collective-permute-start.2 = (f32[8,128]{1,0:T(8,128)S(1)}, f32[8,128]{1,0:T(8,128)S(1)}, u32[]{:S(2)}, u32[]{:S(2)}) collective-permute-start(f32[8,128]{1,0:T(8,128)S(1)} %merge.1.after_ref.a_ref), channel_id=1, source_target_pairs={{0,32},{16,48},{32,0},{48,16},{64,96},{80,112},{96,64},{112,80},{1... | collective-permute-start | bytes 12296 | tf_op jit(solution)/shard_map/ppermute | solution.py:299
  32.1 7.7 %collective-permute-start.1 = (bf16[4,2,64,256]{3,2,1,0:T(8,128)(2,1)S(1)}, bf16[4,2,64,256]{3,2,1,0:T(8,128)(2,1)S(1)}, u32[]{:S(2)}, u32[]{:S(2)}) collective-permute-start(bf16[4,2,64,256]{3,2,1,0:T(8,128)(2,1)S(1)} %get-tuple-element.17), channel_id=1, source_target_pairs={{1,2},{2,1},{3,4},{4,3},{5,6},{6,5},{7,8},{8,7},{9,10},{10,9},{11,... | collective-permute-start | bytes 786440 | tf_op jit(solution)/shard_map/ppermute | solution.py:26
  41.3 6.3 %collective-permute-start.9 = (f32[8,128]{1,0:T(8,128)S(1)}, f32[8,128]{1,0:T(8,128)S(1)}, u32[]{:S(2)}, u32[]{:S(2)}) collective-permute-start(f32[8,128]{1,0:T(8,128)S(1)} %get-tuple-element.24.a_ref), channel_id=1, source_target_pairs={{0,48},{16,0},{32,16},{48,32},{64,112},{80,64},{96,80},{112,96},{1... | collective-permute-start | bytes 12296 | tf_op jit(solution)/shard_map/ppermute | solution.py:299
  42.4 5.2 %collective-permute-start.8 = (f32[8,128]{1,0:T(8,128)S(1)}, f32[8,128]{1,0:T(8,128)S(1)}, u32[]{:S(2)}, u32[]{:S(2)}) collective-permute-start(f32[8,128]{1,0:T(8,128)S(1)} %get-tuple-element.24.a_ref), channel_id=1, source_target_pairs={{0,16},{16,32},{32,48},{48,0},{64,80},{80,96},{96,112},{112,64},{1... | collective-permute-start | bytes 12296 | tf_op jit(solution)/shard_map/ppermute | solution.py:299
  42.8 4.8 %collective-permute-start.7 = (f32[8,128]{1,0:T(8,128)S(1)}, f32[8,128]{1,0:T(8,128)S(1)}, u32[]{:S(2)}, u32[]{:S(2)}) collective-permute-start(f32[8,128]{1,0:T(8,128)S(1)} %get-tuple-element.24.a_ref), channel_id=1, source_target_pairs={{0,32},{16,48},{32,0},{48,16},{64,96},{80,112},{96,64},{112,80},{1... | collective-permute-start | bytes 12296 | tf_op jit(solution)/shard_map/ppermute | solution.py:299
  44.3 19.4 %collective-permute-start.6 = (bf16[2,10,64,256]{3,2,1,0:T(8,128)(2,1)S(1)}, bf16[2,10,64,256]{3,2,1,0:T(8,128)(2,1)S(1)}, u32[]{:S(2)}, u32[]{:S(2)}) collective-permute-start(bf16[2,10,64,256]{3,2,1,0:T(8,128)(2,1)S(1)} %get-tuple-element.23.hidden_ref), channel_id=1, source_target_pairs={{0,16},{16,32},{32,48},{48,64},{64,80},{80,96},{96,112},{112,128},... | collective-permute-start | bytes 1966088 | tf_op jit(solution)/shard_map/ppermute | solution.py:18
  47.6 16.0 %copy-start.1 = (bf16[3,3,3,256,256]{4,3,2,1,0:T(8,128)(2,1)S(1)}, bf16[3,3,3,256,256]{4,3,2,1,0:T(8,128)(2,1)}, u32[]{:S(2)}) copy-start(bf16[3,3,3,256,256]{4,3,2,1,0:T(8,128)(2,1)} %param.13) | copy-start | bytes 10616836

commit v9 on v8

--- a/solution.py
+++ b/solution.py
@@ -284,7 +284,6 @@
     stay = lambda value: pltpu.with_memory_space_constraint(value, pltpu.HBM)
     vectors = [v.reshape(1, channels) for v in (first_gain, first_shift, second_gain, second_shift)]
 
-    prev = next_frames(features)
     lines, kept, vectors = pl.pallas_call(
         stats_kernel,
         out_shape=[line(64), block(frames, rows), jax.ShapeDtypeStruct((8, channels), jnp.float32)],
@@ -294,6 +293,7 @@
         compiler_params=small,
         name="moments",
     )(stay(features), *[stay(v) for v in vectors])
+    prev = next_frames(kept)
     others = [[(4 * x + y) * band + b for x in range(4) for b in range(band)] for y in range(4)]
     over_others = lambda lines: lax.all_to_all(lines, ("tm", "band"), 0, 0, tiled=True, axis_index_groups=others)
     around = lambda line, by: lax.ppermute(line, "tm", [(i, i - i % 4 + (i + by) % 4) for i in range(tm)])

time: 68.3 us -> 68.3 us (level)
  transfers between devices with their start and end apart: 10 -> 10, of which waited for: 1 -> 1; matrix products, arithmetic and copies ran while one was open for 0% -> 0% of each run, Pallas kernels for 8% -> 6%
where the time goes in v9:
time: 68.3 us; the launch traced here: 68.1 us
  blocking collectives  37.4 us (55%)
  starting transfers between devices  18.2 us (27%)
  Pallas kernels  11.2 us (16%)
  waiting for transfers between devices  0.96 us (1%)
    all_to_all x2, blocking collectives, local(): lax.all_to_all(lines, ('tm', 'band'), 0, 0, tiled=True, axis_index_groups...  37.4 us
    ppermute x2, starting transfers between devices, next_frames(): return lax.ppermute(value, 'tm', [(i, i + 1) for i in range(count - 1)])  7.35 us
    ppermute x6, starting transfers between devices, local(): lax.ppermute(line, 'tm', [(i, i - i % 4 + (i + by) % 4) for i in range(tm)])  7.08 us
    pallas_call x1, Pallas kernels, local(): pl.pallas_call(functools.partial(second_kernel, members), out_shape=block...  4.27 us
    ppermute x2, starting transfers between devices, swapped(): return lax.ppermute(value, axis, pairs)  3.8 us
    pallas_call x1, Pallas kernels, local(): pl.pallas_call(functools.partial(inner_kernel, members), out_shape=[block...  3.53 us
    pallas_call x1, Pallas kernels, local(): pl.pallas_call(functools.partial(outer_kernel, members), out_shape=[block...  1.55 us
    pallas_call x1, Pallas kernels, local(): pl.pallas_call(stats_kernel, out_shape=[line(64), block(frames, rows), ja...  1.52 us
  transfers between devices with their start and end apart: 10, of which 1 were waited for; matrix products, arithmetic and copies ran while one was open for 0% of the time, Pallas kernels for 6%

profile of v9, /device:TPU:1, one launch (start us, length us, event | category | flops | bytes accessed | tf_op | source)
XLA Modules:
  0.0 68.1 jit_solution(7801420336078234802)
XLA Ops:
  0.0 1.5 %moments.1 = (f32[64,128]{1,0:T(8,128)S(1)}, bf16[2,8,64,256]{3,2,1,0:T(8,128)(2,1)S(1)}, f32[8,256]{1,0:T(8,128)S(1)}) custom-call(bf16[2,8,64,256]{3,2,1,0:T(8,128)(2,1)} %x_ref.1, f32[1,256]{1,0:T(1,128)} %bitcast.22, f32[1,256]{1,0:T(1,128)} %bitcast.23, f32[1,256]{1,0:T(1,128)} %bitcast.24, f32[1,256]{1,0:T(1,128)} %bitcast.25), custom_call_target="tpu_custom_call" | custom-call | tf_op jit(solution)/shard_map/moments/pallas_call | solution.py:287
  1.5 4.1 %collective-permute-start = (bf16[2,8,64,256]{3,2,1,0:T(8,128)(2,1)S(1)}, bf16[2,8,64,256]{3,2,1,0:T(8,128)(2,1)S(1)}, u32[]{:S(2)}, u32[]{:S(2)}) collective-permute-start(bf16[2,8,64,256]{3,2,1,0:T(8,128)(2,1)S(1)} %get-tuple-element.15.x_ref), channel_id=1, source_target_pairs={{0,16},{16,32},{32,48},{48,64},{64,80},{80,96},{96,112},{112,128},... | collective-permute-start | bytes 1572872 | tf_op jit(solution)/shard_map/ppermute | solution.py:18
  5.6 21.5 %all_to_all.22 = f32[64,1,128]{2,1,0:T(1,128)S(1)} all-to-all(f32[64,1,128]{2,1,0:T(1,128)S(1)} %bitcast.20), channel_id=1, replica_groups={{0,1,2,3,4,5,6,7,8,9,10,11,12,13,14,15,64,65,66,67,68,69,70,71,72,73,74..., dimensions={0} | all-to-all | bytes 65536 | tf_op jit(solution)/shard_map/all_to_all | solution.py:298
  27.1 0.1 merge.1.after_ref.a_ref
  27.2 0.0 collective-permute-done.prev_ref
  27.2 0.8 %collective-permute-start.5 = (bf16[4,2,64,256]{3,2,1,0:T(8,128)(2,1)S(1)}, bf16[4,2,64,256]{3,2,1,0:T(8,128)(2,1)S(1)}, u32[]{:S(2)}, u32[]{:S(2)}) collective-permute-start(bf16[4,2,64,256]{3,2,1,0:T(8,128)(2,1)S(1)} %get-tuple-element.18), channel_id=1, source_target_pairs={{0,1},{1,0},{2,3},{3,2},{4,5},{5,4},{6,7},{7,6},{8,9},{9,8},{10,11... | collective-permute-start | bytes 786440 | tf_op jit(solution)/shard_map/ppermute | solution.py:26
  28.0 2.0 %collective-permute-start.4 = (f32[8,128]{1,0:T(8,128)S(1)}, f32[8,128]{1,0:T(8,128)S(1)}, u32[]{:S(2)}, u32[]{:S(2)}) collective-permute-start(f32[8,128]{1,0:T(8,128)S(1)} %merge.1.after_ref.a_ref), channel_id=1, source_target_pairs={{0,48},{16,0},{32,16},{48,32},{64,112},{80,64},{96,80},{112,96},{1... | collective-permute-start | bytes 12296 | tf_op jit(solution)/shard_map/ppermute | solution.py:299
  30.0 0.0 collective-permute-start.3
  30.0 2.1 %collective-permute-start.2 = (f32[8,128]{1,0:T(8,128)S(1)}, f32[8,128]{1,0:T(8,128)S(1)}, u32[]{:S(2)}, u32[]{:S(2)}) collective-permute-start(f32[8,128]{1,0:T(8,128)S(1)} %merge.1.after_ref.a_ref), channel_id=1, source_target_pairs={{0,32},{16,48},{32,0},{48,16},{64,96},{80,112},{96,64},{112,80},{1... | collective-permute-start | bytes 12296 | tf_op jit(solution)/shard_map/ppermute | solution.py:299
  32.1 3.0 %collective-permute-start.1 = (bf16[4,2,64,256]{3,2,1,0:T(8,128)(2,1)S(1)}, bf16[4,2,64,256]{3,2,1,0:T(8,128)(2,1)S(1)}, u32[]{:S(2)}, u32[]{:S(2)}) collective-permute-start(bf16[4,2,64,256]{3,2,1,0:T(8,128)(2,1)S(1)} %get-tuple-element.17), channel_id=1, source_target_pairs={{1,2},{2,1},{3,4},{4,3},{5,6},{6,5},{7,8},{8,7},{9,10},{10,9},{11,... | collective-permute-start | bytes 786440 | tf_op jit(solution)/shard_map/ppermute | solution.py:26
  35.2 0.0 collective-permute-done.4.d_ref
  35.2 0.0 collective-permute-done.3.c_ref
  35.2 0.0 collective-permute-done.2.b_ref
  35.2 0.0 collective-permute-done.5.refs_1_.pair_ref
  35.2 0.0 copy-done
  35.2 0.1 merge_y.2.lines_ref
  35.3 3.5 %first_conv_inner.1 = (bf16[2,10,64,256]{3,2,1,0:T(8,128)(2,1)S(1)}, bf16[4,12,64,256]{3,2,1,0:T(8,128)(2,1)S(1)}, bf16[2,3,3,256,256]{4,3,2,1,0:T(8,128)(2,1)S(1)}) custom-call(bf16[2,8,64,256]{3,2,1,0:T(8,128)(2,1)S(1)} %get-tuple-element.15.x_ref, bf16[2,8,64,256]{3,2,1,0:T(8,128)(2,1)S(1)} %collective-permute-done.prev_ref, ...), custom_call_target="tpu_custom_call" | custom-call | tf_op jit(solution)/shard_map/first_conv_inner/pallas_call | solution.py:334
  38.8 0.9 %collective-permute-done.1.cross_ref = bf16[4,2,64,256]{3,2,1,0:T(8,128)(2,1)S(1)} collective-permute-done((bf16[4,2,64,256]{3,2,1,0:T(8,128)(2,1)S(1)}, bf16[4,2,64,256]{3,2,1,0:T(8,128)(2,1)S(1)}, u32[]{:S(2)}, u32[]{:S(2)}) %collective-permute-start.1) | collective-permute-done | bytes 262176 | tf_op jit(solution)/shard_map/ppermute | solution.py:26
  39.8 1.5 %first_conv_outer.1 = (bf16[2,10,64,256]{3,2,1,0:T(8,128)(2,1)S(1)}, bf16[4,12,64,256]{3,2,1,0:T(8,128)(2,1)S(1)}, f32[8,128]{1,0:T(8,128)S(1)}) custom-call(bf16[2,8,64,256]{3,2,1,0:T(8,128)(2,1)S(1)} %get-tuple-element.15.x_ref, bf16[2,8,64,256]{3,2,1,0:T(8,128)(2,1)S(1)} %collective-permute-done.prev_ref, ...), custom_call_target="tpu_custom_call", output_to_operand_aliasing={{0}: (7, {}), {1}: (8, {})} | custom-call | tf_op jit(solution)/shard_map/first_conv_outer/pallas_call | solution.py:346
  41.3 1.1 %collective-permute-start.9 = (f32[8,128]{1,0:T(8,128)S(1)}, f32[8,128]{1,0:T(8,128)S(1)}, u32[]{:S(2)}, u32[]{:S(2)}) collective-permute-start(f32[8,128]{1,0:T(8,128)S(1)} %get-tuple-element.24.a_ref), channel_id=1, source_target_pairs={{0,48},{16,0},{32,16},{48,32},{64,112},{80,64},{96,80},{112,96},{1... | collective-permute-start | bytes 12296 | tf_op jit(solution)/shard_map/ppermute | solution.py:299
  42.4 0.4 collective-permute-start.8
  42.8 1.5 %collective-permute-start.7 = (f32[8,128]{1,0:T(8,128)S(1)}, f32[8,128]{1,0:T(8,128)S(1)}, u32[]{:S(2)}, u32[]{:S(2)}) collective-permute-start(f32[8,128]{1,0:T(8,128)S(1)} %get-tuple-element.24.a_ref), channel_id=1, source_target_pairs={{0,32},{16,48},{32,0},{48,16},{64,96},{80,112},{96,64},{112,80},{1... | collective-permute-start | bytes 12296 | tf_op jit(solution)/shard_map/ppermute | solution.py:299
  44.3 3.3 %collective-permute-start.6 = (bf16[2,10,64,256]{3,2,1,0:T(8,128)(2,1)S(1)}, bf16[2,10,64,256]{3,2,1,0:T(8,128)(2,1)S(1)}, u32[]{:S(2)}, u32[]{:S(2)}) collective-permute-start(bf16[2,10,64,256]{3,2,1,0:T(8,128)(2,1)S(1)} %get-tuple-element.23.hidden_ref), channel_id=1, source_target_pairs={{0,16},{16,32},{32,48},{48,64},{64,80},{80,96},{96,112},{112,128},... | collective-permute-start | bytes 1966088 | tf_op jit(solution)/shard_map/ppermute | solution.py:18
  47.6 0.0 collective-permute-done.9.d_ref
  47.6 0.0 collective-permute-done.8.c_ref
  47.6 0.0 collective-permute-done.7.b_ref
  47.6 0.0 copy-start.1
  47.6 0.1 merge_y.3
  47.7 15.9 %all_to_all.23 = f32[64,1,128]{2,1,0:T(1,128)S(1)} all-to-all(f32[64,1,128]{2,1,0:T(1,128)S(1)} %bitcast.21), channel_id=1, replica_groups={{0,1,2,3,4,5,6,7,8,9,10,11,12,13,14,15,64,65,66,67,68,69,70,71,72,73,74..., dimensions={0} | all-to-all | bytes 65536 | tf_op jit(solution)/shard_map/all_to_all | solution.py:298
  63.7 0.0 collective-permute-done.6.prev_ref
  63.7 0.0 copy-done.1
  63.7 4.3 %second_conv.1 = bf16[2,8,64,256]{3,2,1,0:T(8,128)(2,1)} custom-call(bf16[2,10,64,256]{3,2,1,0:T(8,128)(2,1)S(1)} %get-tuple-element.23.hidden_ref, bf16[2,10,64,256]{3,2,1,0:T(8,128)(2,1)S(1)} %collective-permute-done.6.prev_ref, f32[64,128]{1,0:T(8,128)S(1)} %bitcast.18, f32[8,256]{1,0:T(8,128)S(1)} %get-tuple-element.19.params_ref, ...), custom_call_target="tpu_custom_call" | custom-call | tf_op jit(solution)/shard_map/second_conv/pallas_call | solution.py:359
  (2 shorter events, 0.0 us)
Async XLA Ops:
  1.5 25.7 %collective-permute-start = (bf16[2,8,64,256]{3,2,1,0:T(8,128)(2,1)S(1)}, bf16[2,8,64,256]{3,2,1,0:T(8,128)(2,1)S(1)}, u32[]{:S(2)}, u32[]{:S(2)}) collective-permute-start(bf16[2,8,64,256]{3,2,1,0:T(8,128)(2,1)S(1)} %get-tuple-element.15.x_ref), channel_id=1, source_target_pairs={{0,16},{16,32},{32,48},{48,64},{64,80},{80,96},{96,112},{112,128},... | collective-permute-start | bytes 1572872 | tf_op jit(solution)/shard_map/ppermute | solution.py:18
  27.2 8.0 %copy-start = (bf16[3,3,3,256,256]{4,3,2,1,0:T(8,128)(2,1)S(1)}, bf16[3,3,3,256,256]{4,3,2,1,0:T(8,128)(2,1)}, u32[]{:S(2)}) copy-start(bf16[3,3,3,256,256]{4,3,2,1,0:T(8,128)(2,1)} %param.10) | copy-start | bytes 10616836
  27.2 7.9 %collective-permute-start.5 = (bf16[4,2,64,256]{3,2,1,0:T(8,128)(2,1)S(1)}, bf16[4,2,64,256]{3,2,1,0:T(8,128)(2,1)S(1)}, u32[]{:S(2)}, u32[]{:S(2)}) collective-permute-start(bf16[4,2,64,256]{3,2,1,0:T(8,128)(2,1)S(1)} %get-tuple-element.18), channel_id=1, source_target_pairs={{0,1},{1,0},{2,3},{3,2},{4,5},{5,4},{6,7},{7,6},{8,9},{9,8},{10,11... | collective-permute-start | bytes 786440 | tf_op jit(solution)/shard_map/ppermute | solution.py:26
  28.0 7.2 %collective-permute-start.4 = (f32[8,128]{1,0:T(8,128)S(1)}, f32[8,128]{1,0:T(8,128)S(1)}, u32[]{:S(2)}, u32[]{:S(2)}) collective-permute-start(f32[8,128]{1,0:T(8,128)S(1)} %merge.1.after_ref.a_ref), channel_id=1, source_target_pairs={{0,48},{16,0},{32,16},{48,32},{64,112},{80,64},{96,80},{112,96},{1... | collective-permute-start | bytes 12296 | tf_op jit(solution)/shard_map/ppermute | solution.py:299
  30.0 5.1 %collective-permute-start.3 = (f32[8,128]{1,0:T(8,128)S(1)}, f32[8,128]{1,0:T(8,128)S(1)}, u32[]{:S(2)}, u32[]{:S(2)}) collective-permute-start(f32[8,128]{1,0:T(8,128)S(1)} %merge.1.after_ref.a_ref), channel_id=1, source_target_pairs={{0,16},{16,32},{32,48},{48,0},{64,80},{80,96},{96,112},{112,64},{1... | collective-permute-start | bytes 12296 | tf_op jit(solution)/shard_map/ppermute | solution.py:299
  30.0 5.1 %collective-permute-start.2 = (f32[8,128]{1,0:T(8,128)S(1)}, f32[8,128]{1,0:T(8,128)S(1)}, u32[]{:S(2)}, u32[]{:S(2)}) collective-permute-start(f32[8,128]{1,0:T(8,128)S(1)} %merge.1.after_ref.a_ref), channel_id=1, source_target_pairs={{0,32},{16,48},{32,0},{48,16},{64,96},{80,112},{96,64},{112,80},{1... | collective-permute-start | bytes 12296 | tf_op jit(solution)/shard_map/ppermute | solution.py:299
  32.1 7.7 %collective-permute-start.1 = (bf16[4,2,64,256]{3,2,1,0:T(8,128)(2,1)S(1)}, bf16[4,2,64,256]{3,2,1,0:T(8,128)(2,1)S(1)}, u32[]{:S(2)}, u32[]{:S(2)}) collective-permute-start(bf16[4,2,64,256]{3,2,1,0:T(8,128)(2,1)S(1)} %get-tuple-element.17), channel_id=1, source_target_pairs={{1,2},{2,1},{3,4},{4,3},{5,6},{6,5},{7,8},{8,7},{9,10},{10,9},{11,... | collective-permute-start | bytes 786440 | tf_op jit(solution)/shard_map/ppermute | solution.py:26
  41.3 6.3 %collective-permute-start.9 = (f32[8,128]{1,0:T(8,128)S(1)}, f32[8,128]{1,0:T(8,128)S(1)}, u32[]{:S(2)}, u32[]{:S(2)}) collective-permute-start(f32[8,128]{1,0:T(8,128)S(1)} %get-tuple-element.24.a_ref), channel_id=1, source_target_pairs={{0,48},{16,0},{32,16},{48,32},{64,112},{80,64},{96,80},{112,96},{1... | collective-permute-start | bytes 12296 | tf_op jit(solution)/shard_map/ppermute | solution.py:299
  42.4 5.2 %collective-permute-start.8 = (f32[8,128]{1,0:T(8,128)S(1)}, f32[8,128]{1,0:T(8,128)S(1)}, u32[]{:S(2)}, u32[]{:S(2)}) collective-permute-start(f32[8,128]{1,0:T(8,128)S(1)} %get-tuple-element.24.a_ref), channel_id=1, source_target_pairs={{0,16},{16,32},{32,48},{48,0},{64,80},{80,96},{96,112},{112,64},{1... | collective-permute-start | bytes 12296 | tf_op jit(solution)/shard_map/ppermute | solution.py:299
  42.8 4.8 %collective-permute-start.7 = (f32[8,128]{1,0:T(8,128)S(1)}, f32[8,128]{1,0:T(8,128)S(1)}, u32[]{:S(2)}, u32[]{:S(2)}) collective-permute-start(f32[8,128]{1,0:T(8,128)S(1)} %get-tuple-element.24.a_ref), channel_id=1, source_target_pairs={{0,32},{16,48},{32,0},{48,16},{64,96},{80,112},{96,64},{112,80},{1... | collective-permute-start | bytes 12296 | tf_op jit(solution)/shard_map/ppermute | solution.py:299
  44.3 19.4 %collective-permute-start.6 = (bf16[2,10,64,256]{3,2,1,0:T(8,128)(2,1)S(1)}, bf16[2,10,64,256]{3,2,1,0:T(8,128)(2,1)S(1)}, u32[]{:S(2)}, u32[]{:S(2)}) collective-permute-start(bf16[2,10,64,256]{3,2,1,0:T(8,128)(2,1)S(1)} %get-tuple-element.23.hidden_ref), channel_id=1, source_target_pairs={{0,16},{16,32},{32,48},{48,64},{64,80},{80,96},{96,112},{112,128},... | collective-permute-start | bytes 1966088 | tf_op jit(solution)/shard_map/ppermute | solution.py:18
  47.6 16.0 %copy-start.1 = (bf16[3,3,3,256,256]{4,3,2,1,0:T(8,128)(2,1)S(1)}, bf16[3,3,3,256,256]{4,3,2,1,0:T(8,128)(2,1)}, u32[]{:S(2)}) copy-start(bf16[3,3,3,256,256]{4,3,2,1,0:T(8,128)(2,1)} %param.13) | copy-start | bytes 10616836

commit v10 on v8

--- a/solution.py
+++ b/solution.py
@@ -48,11 +48,7 @@
     return jnp.sum(block.reshape(cols // 8, 8, channels), axis=0)
 
 
-def local_moments(rows, channels):
-    size = channels // GROUPS
-    same = indicator(channels, channels, lambda r, c: r // size == c // size)
-    first = indicator(channels, LANES, lambda r, c: r // size == c)
-    second = indicator(channels, LANES, lambda r, c: r // size + GROUPS == c)
+def channel_sums(rows):
     total = folded(rows[0]().astype(jnp.float32))
     for row in rows[1:]:
         total = total + folded(row().astype(jnp.float32))
@@ -63,8 +59,17 @@
         off = row().astype(jnp.float32) - centre
         part = folded(off * off)
         spread = part if spread is None else spread + part
+    return centre, jnp.sum(spread, axis=0, keepdims=True), positions
+
+
+def group_line(centre, spread, positions):
+    channels = centre.shape[1]
+    size = channels // GROUPS
+    same = indicator(channels, channels, lambda r, c: r // size == c // size)
+    first = indicator(channels, LANES, lambda r, c: r // size == c)
+    second = indicator(channels, LANES, lambda r, c: r // size + GROUPS == c)
     apart = centre - picked(centre, same) * (1.0 / size)
-    spread = jnp.sum(spread, axis=0, keepdims=True) + positions * apart * apart
+    spread = spread + positions * apart * apart
     return picked(centre, first) * (1.0 / size) + picked(spread, second)
 
 
@@ -160,7 +165,7 @@
     for copy in copies:
         copy.wait()
     reads = [functools.partial(lambda f, r: kept_ref[f, r], f, r) for f in range(frames) for r in range(rows)]
-    line_ref[...] = jnp.broadcast_to(local_moments(reads, channels), line_ref.shape)
+    line_ref[...] = jnp.broadcast_to(group_line(*channel_sums(reads)), line_ref.shape)
 
 
 def edges_kernel(x_ref, prev_ref, after_ref, cross_ref, pair_ref):
@@ -201,7 +206,8 @@
             done += count
 
 
-def inner_kernel(members, x_ref, prev_ref, pair_ref, lines_ref, params_ref, weight_ref, hidden_ref, act_ref, mixed_ref):
+def inner_kernel(members, x_ref, prev_ref, pair_ref, lines_ref, params_ref, weight_ref, hidden_ref, act_ref, mixed_ref,
+                 sums_ref):
     rows = x_ref.shape[1]
     leading, _, _ = at_ends()
     pair_at, _, _, _ = places(rows)
@@ -217,22 +223,31 @@
         row(pair_at + r, [pair_ref[f, r] for f in (0, 1)], [pair_ref[f, r] for f in (2, 3)])
     mix_weight(weight_ref, mixed_ref)
     first_rows(act_ref, hidden_ref, weight_ref, mixed_ref, [(2, rows - 2), (jnp.minimum(pair_at, rows), 2)])
-
-
-def outer_kernel(members, x_ref, prev_ref, cross_ref, lines_ref, params_ref, weight_ref, mixed_ref, _, __,
-                 hidden_ref, act_ref, line_ref):
-    frames, rows, _, channels = x_ref.shape
+    near = jnp.where(pair_at == 0, 1, rows)
+    places_own = [(f, r) for f in range(2) for r in list(range(2, rows)) + [near]]
+    centre, spread, _ = channel_sums([functools.partial(lambda f, r: hidden_ref[f, r], *at) for at in places_own])
+    for i, value in enumerate((centre, spread) + norm):
+        sums_ref[i : i + 1] = value
+
+
+def outer_kernel(x_ref, prev_ref, cross_ref, sums_ref, weight_ref, mixed_ref, _, __, hidden_ref, act_ref, line_ref):
+    frames, rows, cols, _ = x_ref.shape
     leading, top, bottom = at_ends()
     _, cross_at, _, _ = places(rows)
-    norm = scaling(lines_ref, params_ref, 0, members)
+    first_centre, first_spread, *norm = [sums_ref[i : i + 1] for i in range(5)]
     for r in range(2):
         rim = [jnp.where(top, ref[f, 0], ref[f, rows - 1]) for ref in (prev_ref, x_ref) for f in range(2)]
         values = [jnp.where(top | bottom, rim[f], cross_ref[f, r]) for f in range(4)]
         before = [jnp.where(leading, values[2], x) for x in values[:2]]
         mixed_frames(act_ref, cross_at + r, [activated(x, *norm) for x in before + values[2:]])
     first_rows(act_ref, hidden_ref, weight_ref, mixed_ref, [(jnp.minimum(cross_at, rows), 2)])
-    reads = [functools.partial(lambda f, r: hidden_ref[f, r + 1], f, r) for f in range(frames) for r in range(rows)]
-    line_ref[...] = jnp.broadcast_to(local_moments(reads, channels), line_ref.shape)
+    near = jnp.where(cross_at == 0, 1, rows)
+    centre, spread, count = channel_sums([functools.partial(lambda f: hidden_ref[f, near], f) for f in range(frames)])
+    positions = frames * rows * cols
+    apart = centre - first_centre
+    share = count / positions
+    spread = first_spread + spread + (positions - count) * share * apart * apart
+    line_ref[...] = jnp.broadcast_to(group_line(first_centre + share * apart, spread, positions), line_ref.shape)
 
 
 def second_kernel(members, hidden_ref, prev_ref, lines_ref, params_ref, x_ref, weight_ref, out_ref,
@@ -331,27 +346,28 @@
     first_weight = taps(first_weight)
     lines = over_y(lines, 64 * members, 8, first_weight, pair)
 
-    hidden, act, mixed_weight = pl.pallas_call(
+    hidden, act, mixed_weight, sums = pl.pallas_call(
         functools.partial(inner_kernel, members),
         out_shape=[
             block(frames, rows + 2),
             block(4, rows + 4),
             jax.ShapeDtypeStruct((2, 3, 3, channels, outputs), jnp.bfloat16),
+            jax.ShapeDtypeStruct((8, channels), jnp.float32),
         ],
         in_specs=[vmem] * 6,
-        out_specs=[vmem] * 3,
+        out_specs=[vmem] * 4,
         compiler_params=params,
         name="first_conv_inner",
     )(kept, prev, pair, lines, vectors, first_weight)
     hidden, _, lines = pl.pallas_call(
-        functools.partial(outer_kernel, members),
+        outer_kernel,
         out_shape=[block(frames, rows + 2), block(4, rows + 4), line(8)],
-        in_specs=[vmem] * 9,
+        in_specs=[vmem] * 8,
         out_specs=[vmem] * 3,
-        input_output_aliases={7: 0, 8: 1},
+        input_output_aliases={6: 0, 7: 1},
         compiler_params=params,
         name="first_conv_outer",
-    )(kept, prev, cross, lines, vectors, first_weight, mixed_weight, hidden, act)
+    )(kept, prev, cross, sums, first_weight, mixed_weight, hidden, act)
 
     prev = next_frames(hidden)
     lines = over_others(over_y(lines, members, 64))

time: 68.3 us -> 68.2 us (level)
  no operation moved by 1% of the time
where the time goes in v10:
time: 68.2 us; the launch traced here: 68 us
  blocking collectives  37.4 us (55%)
  starting transfers between devices  18.2 us (27%)
  Pallas kernels  11.4 us (17%)
    all_to_all x2, blocking collectives, local(): lax.all_to_all(lines, ('tm', 'band'), 0, 0, tiled=True, axis_index_groups...  37.4 us
    ppermute x2, starting transfers between devices, next_frames(): return lax.ppermute(value, 'tm', [(i, i + 1) for i in range(count - 1)])  7.33 us
    ppermute x6, starting transfers between devices, local(): lax.ppermute(line, 'tm', [(i, i - i % 4 + (i + by) % 4) for i in range(tm)])  7.08 us
    pallas_call x1, Pallas kernels, local(): pl.pallas_call(functools.partial(second_kernel, members), out_shape=block...  4.31 us
    pallas_call x1, Pallas kernels, local(): pl.pallas_call(functools.partial(inner_kernel, members), out_shape=[block...  3.87 us
    ppermute x2, starting transfers between devices, swapped(): return lax.ppermute(value, axis, pairs)  3.8 us
    pallas_call x1, Pallas kernels, local(): pl.pallas_call(stats_kernel, out_shape=[line(64), block(frames, rows), ja...  1.53 us
  transfers between devices with their start and end apart: 10, of which 1 were waited for; matrix products, arithmetic and copies ran while one was open for 0% of the time, Pallas kernels for 8%

profile of v10, /device:TPU:1, one launch (start us, length us, event | category | flops | bytes accessed | tf_op | source)
XLA Modules:
  0.0 68.0 jit_solution(5897436747661930851)
XLA Ops:
  0.0 4.0 %collective-permute-start = (bf16[2,8,64,256]{3,2,1,0:T(8,128)(2,1)}, bf16[2,8,64,256]{3,2,1,0:T(8,128)(2,1)S(1)}, u32[]{:S(2)}, u32[]{:S(2)}) collective-permute-start(bf16[2,8,64,256]{3,2,1,0:T(8,128)(2,1)} %x_ref.1), channel_id=1, source_target_pairs={{0,16},{16,32},{32,48},{48,64},{64,80},{80,96},{96,112},{112,128},... | collective-permute-start | bytes 1572872 | tf_op jit(solution)/shard_map/ppermute | solution.py:18
  4.1 1.5 %moments.1 = (f32[64,128]{1,0:T(8,128)S(1)}, bf16[2,8,64,256]{3,2,1,0:T(8,128)(2,1)S(1)}, f32[8,256]{1,0:T(8,128)S(1)}) custom-call(bf16[2,8,64,256]{3,2,1,0:T(8,128)(2,1)} %x_ref.1, f32[1,256]{1,0:T(1,128)} %bitcast.22, f32[1,256]{1,0:T(1,128)} %bitcast.23, f32[1,256]{1,0:T(1,128)} %bitcast.24, f32[1,256]{1,0:T(1,128)} %bitcast.25), custom_call_target="tpu_custom_call" | custom-call | tf_op jit(solution)/shard_map/moments/pallas_call | solution.py:303
  5.6 21.5 %all_to_all.22 = f32[64,1,128]{2,1,0:T(1,128)S(1)} all-to-all(f32[64,1,128]{2,1,0:T(1,128)S(1)} %bitcast.21), channel_id=1, replica_groups={{0,1,2,3,4,5,6,7,8,9,10,11,12,13,14,15,64,65,66,67,68,69,70,71,72,73,74..., dimensions={0} | all-to-all | bytes 65536 | tf_op jit(solution)/shard_map/all_to_all | solution.py:313
  27.1 0.1 merge.1.after_ref.a_ref
  27.2 0.0 collective-permute-done.prev_ref
  27.2 0.8 %collective-permute-start.2 = (bf16[4,2,64,256]{3,2,1,0:T(8,128)(2,1)S(1)}, bf16[4,2,64,256]{3,2,1,0:T(8,128)(2,1)S(1)}, u32[]{:S(2)}, u32[]{:S(2)}) collective-permute-start(bf16[4,2,64,256]{3,2,1,0:T(8,128)(2,1)S(1)} %get-tuple-element.19), channel_id=1, source_target_pairs={{0,1},{1,0},{2,3},{3,2},{4,5},{5,4},{6,7},{7,6},{8,9},{9,8},{10,11... | collective-permute-start | bytes 786440 | tf_op jit(solution)/shard_map/ppermute | solution.py:26
  28.0 2.0 %collective-permute-start.5 = (f32[8,128]{1,0:T(8,128)S(1)}, f32[8,128]{1,0:T(8,128)S(1)}, u32[]{:S(2)}, u32[]{:S(2)}) collective-permute-start(f32[8,128]{1,0:T(8,128)S(1)} %merge.1.after_ref.a_ref), channel_id=1, source_target_pairs={{0,48},{16,0},{32,16},{48,32},{64,112},{80,64},{96,80},{112,96},{1... | collective-permute-start | bytes 12296 | tf_op jit(solution)/shard_map/ppermute | solution.py:314
  30.0 0.0 collective-permute-start.4
  30.0 2.1 %collective-permute-start.3 = (f32[8,128]{1,0:T(8,128)S(1)}, f32[8,128]{1,0:T(8,128)S(1)}, u32[]{:S(2)}, u32[]{:S(2)}) collective-permute-start(f32[8,128]{1,0:T(8,128)S(1)} %merge.1.after_ref.a_ref), channel_id=1, source_target_pairs={{0,32},{16,48},{32,0},{48,16},{64,96},{80,112},{96,64},{112,80},{1... | collective-permute-start | bytes 12296 | tf_op jit(solution)/shard_map/ppermute | solution.py:314
  32.1 3.0 %collective-permute-start.1 = (bf16[4,2,64,256]{3,2,1,0:T(8,128)(2,1)S(1)}, bf16[4,2,64,256]{3,2,1,0:T(8,128)(2,1)S(1)}, u32[]{:S(2)}, u32[]{:S(2)}) collective-permute-start(bf16[4,2,64,256]{3,2,1,0:T(8,128)(2,1)S(1)} %get-tuple-element.18), channel_id=1, source_target_pairs={{1,2},{2,1},{3,4},{4,3},{5,6},{6,5},{7,8},{8,7},{9,10},{10,9},{11,... | collective-permute-start | bytes 786440 | tf_op jit(solution)/shard_map/ppermute | solution.py:26
  35.1 0.0 collective-permute-done.5.d_ref
  35.2 0.0 collective-permute-done.4.c_ref
  35.2 0.0 collective-permute-done.3.b_ref
  35.2 0.0 collective-permute-done.2.refs_1_.pair_ref
  35.2 0.0 copy-done
  35.2 0.1 merge_y.2.lines_ref
  35.3 3.9 %first_conv_inner.1 = (bf16[2,10,64,256]{3,2,1,0:T(8,128)(2,1)S(1)}, bf16[4,12,64,256]{3,2,1,0:T(8,128)(2,1)S(1)}, bf16[2,3,3,256,256]{4,3,2,1,0:T(8,128)(2,1)S(1)}, f32[8,256]{1,0:T(8,128)S(1)}) custom-call(bf16[2,8,64,256]{3,2,1,0:T(8,128)(2,1)S(1)} %get-tuple-element.16.x_ref, bf16[2,8,64,256]{3,2,1,0:T(8,128)(2,1)S(1)} %collective-permute-done.prev_ref, ...), custom_call_target="tpu_custom_call" | custom-call | tf_op jit(solution)/shard_map/first_conv_inner/pallas_call | solution.py:349
  39.2 0.6 collective-permute-done.1.cross_ref
  39.8 1.4 %first_conv_outer.1 = (bf16[2,10,64,256]{3,2,1,0:T(8,128)(2,1)S(1)}, bf16[4,12,64,256]{3,2,1,0:T(8,128)(2,1)S(1)}, f32[8,128]{1,0:T(8,128)S(1)}) custom-call(bf16[2,8,64,256]{3,2,1,0:T(8,128)(2,1)S(1)} %get-tuple-element.16.x_ref, bf16[2,8,64,256]{3,2,1,0:T(8,128)(2,1)S(1)} %collective-permute-done.prev_ref, ...), custom_call_target="tpu_custom_call", output_to_operand_aliasing={{0}: (6, {}), {1}: (7, {})} | custom-call | tf_op jit(solution)/shard_map/first_conv_outer/pallas_call | solution.py:362
  41.1 1.1 %collective-permute-start.9 = (f32[8,128]{1,0:T(8,128)S(1)}, f32[8,128]{1,0:T(8,128)S(1)}, u32[]{:S(2)}, u32[]{:S(2)}) collective-permute-start(f32[8,128]{1,0:T(8,128)S(1)} %get-tuple-element.26.a_ref), channel_id=1, source_target_pairs={{0,48},{16,0},{32,16},{48,32},{64,112},{80,64},{96,80},{112,96},{1... | collective-permute-start | bytes 12296 | tf_op jit(solution)/shard_map/ppermute | solution.py:314
  42.2 0.4 collective-permute-start.8
  42.6 1.5 %collective-permute-start.7 = (f32[8,128]{1,0:T(8,128)S(1)}, f32[8,128]{1,0:T(8,128)S(1)}, u32[]{:S(2)}, u32[]{:S(2)}) collective-permute-start(f32[8,128]{1,0:T(8,128)S(1)} %get-tuple-element.26.a_ref), channel_id=1, source_target_pairs={{0,32},{16,48},{32,0},{48,16},{64,96},{80,112},{96,64},{112,80},{1... | collective-permute-start | bytes 12296 | tf_op jit(solution)/shard_map/ppermute | solution.py:314
  44.1 3.3 %collective-permute-start.6 = (bf16[2,10,64,256]{3,2,1,0:T(8,128)(2,1)S(1)}, bf16[2,10,64,256]{3,2,1,0:T(8,128)(2,1)S(1)}, u32[]{:S(2)}, u32[]{:S(2)}) collective-permute-start(bf16[2,10,64,256]{3,2,1,0:T(8,128)(2,1)S(1)} %get-tuple-element.25.hidden_ref), channel_id=1, source_target_pairs={{0,16},{16,32},{32,48},{48,64},{64,80},{80,96},{96,112},{112,128},... | collective-permute-start | bytes 1966088 | tf_op jit(solution)/shard_map/ppermute | solution.py:18
  47.4 0.0 collective-permute-done.9.d_ref
  47.4 0.0 collective-permute-done.8.c_ref
  47.4 0.0 collective-permute-done.7.b_ref
  47.4 0.0 copy-start.1
  47.4 0.1 merge_y.3
  47.5 15.9 %all_to_all.23 = f32[64,1,128]{2,1,0:T(1,128)S(1)} all-to-all(f32[64,1,128]{2,1,0:T(1,128)S(1)} %bitcast.20), channel_id=1, replica_groups={{0,1,2,3,4,5,6,7,8,9,10,11,12,13,14,15,64,65,66,67,68,69,70,71,72,73,74..., dimensions={0} | all-to-all | bytes 65536 | tf_op jit(solution)/shard_map/all_to_all | solution.py:313
  63.5 0.0 collective-permute-done.6.prev_ref
  63.5 0.0 copy-done.1
  63.5 4.3 %second_conv.1 = bf16[2,8,64,256]{3,2,1,0:T(8,128)(2,1)} custom-call(bf16[2,10,64,256]{3,2,1,0:T(8,128)(2,1)S(1)} %get-tuple-element.25.hidden_ref, bf16[2,10,64,256]{3,2,1,0:T(8,128)(2,1)S(1)} %collective-permute-done.6.prev_ref, f32[64,128]{1,0:T(8,128)S(1)} %bitcast.18, f32[8,256]{1,0:T(8,128)S(1)} %get-tuple-element.20.params_ref, ...), custom_call_target="tpu_custom_call" | custom-call | tf_op jit(solution)/shard_map/second_conv/pallas_call | solution.py:375
  (2 shorter events, 0.0 us)
Async XLA Ops:
  0.0 27.2 %collective-permute-start = (bf16[2,8,64,256]{3,2,1,0:T(8,128)(2,1)}, bf16[2,8,64,256]{3,2,1,0:T(8,128)(2,1)S(1)}, u32[]{:S(2)}, u32[]{:S(2)}) collective-permute-start(bf16[2,8,64,256]{3,2,1,0:T(8,128)(2,1)} %x_ref.1), channel_id=1, source_target_pairs={{0,16},{16,32},{32,48},{48,64},{64,80},{80,96},{96,112},{112,128},... | collective-permute-start | bytes 1572872 | tf_op jit(solution)/shard_map/ppermute | solution.py:18
  27.2 8.0 %copy-start = (bf16[3,3,3,256,256]{4,3,2,1,0:T(8,128)(2,1)S(1)}, bf16[3,3,3,256,256]{4,3,2,1,0:T(8,128)(2,1)}, u32[]{:S(2)}) copy-start(bf16[3,3,3,256,256]{4,3,2,1,0:T(8,128)(2,1)} %param.10) | copy-start | bytes 10616836
  27.2 7.9 %collective-permute-start.2 = (bf16[4,2,64,256]{3,2,1,0:T(8,128)(2,1)S(1)}, bf16[4,2,64,256]{3,2,1,0:T(8,128)(2,1)S(1)}, u32[]{:S(2)}, u32[]{:S(2)}) collective-permute-start(bf16[4,2,64,256]{3,2,1,0:T(8,128)(2,1)S(1)} %get-tuple-element.19), channel_id=1, source_target_pairs={{0,1},{1,0},{2,3},{3,2},{4,5},{5,4},{6,7},{7,6},{8,9},{9,8},{10,11... | collective-permute-start | bytes 786440 | tf_op jit(solution)/shard_map/ppermute | solution.py:26
  28.0 7.2 %collective-permute-start.5 = (f32[8,128]{1,0:T(8,128)S(1)}, f32[8,128]{1,0:T(8,128)S(1)}, u32[]{:S(2)}, u32[]{:S(2)}) collective-permute-start(f32[8,128]{1,0:T(8,128)S(1)} %merge.1.after_ref.a_ref), channel_id=1, source_target_pairs={{0,48},{16,0},{32,16},{48,32},{64,112},{80,64},{96,80},{112,96},{1... | collective-permute-start | bytes 12296 | tf_op jit(solution)/shard_map/ppermute | solution.py:314
  30.0 5.1 %collective-permute-start.4 = (f32[8,128]{1,0:T(8,128)S(1)}, f32[8,128]{1,0:T(8,128)S(1)}, u32[]{:S(2)}, u32[]{:S(2)}) collective-permute-start(f32[8,128]{1,0:T(8,128)S(1)} %merge.1.after_ref.a_ref), channel_id=1, source_target_pairs={{0,16},{16,32},{32,48},{48,0},{64,80},{80,96},{96,112},{112,64},{1... | collective-permute-start | bytes 12296 | tf_op jit(solution)/shard_map/ppermute | solution.py:314
  30.0 5.1 %collective-permute-start.3 = (f32[8,128]{1,0:T(8,128)S(1)}, f32[8,128]{1,0:T(8,128)S(1)}, u32[]{:S(2)}, u32[]{:S(2)}) collective-permute-start(f32[8,128]{1,0:T(8,128)S(1)} %merge.1.after_ref.a_ref), channel_id=1, source_target_pairs={{0,32},{16,48},{32,0},{48,16},{64,96},{80,112},{96,64},{112,80},{1... | collective-permute-start | bytes 12296 | tf_op jit(solution)/shard_map/ppermute | solution.py:314
  32.1 7.7 %collective-permute-start.1 = (bf16[4,2,64,256]{3,2,1,0:T(8,128)(2,1)S(1)}, bf16[4,2,64,256]{3,2,1,0:T(8,128)(2,1)S(1)}, u32[]{:S(2)}, u32[]{:S(2)}) collective-permute-start(bf16[4,2,64,256]{3,2,1,0:T(8,128)(2,1)S(1)} %get-tuple-element.18), channel_id=1, source_target_pairs={{1,2},{2,1},{3,4},{4,3},{5,6},{6,5},{7,8},{8,7},{9,10},{10,9},{11,... | collective-permute-start | bytes 786440 | tf_op jit(solution)/shard_map/ppermute | solution.py:26
  41.1 6.3 %collective-permute-start.9 = (f32[8,128]{1,0:T(8,128)S(1)}, f32[8,128]{1,0:T(8,128)S(1)}, u32[]{:S(2)}, u32[]{:S(2)}) collective-permute-start(f32[8,128]{1,0:T(8,128)S(1)} %get-tuple-element.26.a_ref), channel_id=1, source_target_pairs={{0,48},{16,0},{32,16},{48,32},{64,112},{80,64},{96,80},{112,96},{1... | collective-permute-start | bytes 12296 | tf_op jit(solution)/shard_map/ppermute | solution.py:314
  42.2 5.2 %collective-permute-start.8 = (f32[8,128]{1,0:T(8,128)S(1)}, f32[8,128]{1,0:T(8,128)S(1)}, u32[]{:S(2)}, u32[]{:S(2)}) collective-permute-start(f32[8,128]{1,0:T(8,128)S(1)} %get-tuple-element.26.a_ref), channel_id=1, source_target_pairs={{0,16},{16,32},{32,48},{48,0},{64,80},{80,96},{96,112},{112,64},{1... | collective-permute-start | bytes 12296 | tf_op jit(solution)/shard_map/ppermute | solution.py:314
  42.6 4.8 %collective-permute-start.7 = (f32[8,128]{1,0:T(8,128)S(1)}, f32[8,128]{1,0:T(8,128)S(1)}, u32[]{:S(2)}, u32[]{:S(2)}) collective-permute-start(f32[8,128]{1,0:T(8,128)S(1)} %get-tuple-element.26.a_ref), channel_id=1, source_target_pairs={{0,32},{16,48},{32,0},{48,16},{64,96},{80,112},{96,64},{112,80},{1... | collective-permute-start | bytes 12296 | tf_op jit(solution)/shard_map/ppermute | solution.py:314
  44.1 19.4 %collective-permute-start.6 = (bf16[2,10,64,256]{3,2,1,0:T(8,128)(2,1)S(1)}, bf16[2,10,64,256]{3,2,1,0:T(8,128)(2,1)S(1)}, u32[]{:S(2)}, u32[]{:S(2)}) collective-permute-start(bf16[2,10,64,256]{3,2,1,0:T(8,128)(2,1)S(1)} %get-tuple-element.25.hidden_ref), channel_id=1, source_target_pairs={{0,16},{16,32},{32,48},{48,64},{64,80},{80,96},{96,112},{112,128},... | collective-permute-start | bytes 1966088 | tf_op jit(solution)/shard_map/ppermute | solution.py:18
  47.4 16.1 %copy-start.1 = (bf16[3,3,3,256,256]{4,3,2,1,0:T(8,128)(2,1)S(1)}, bf16[3,3,3,256,256]{4,3,2,1,0:T(8,128)(2,1)}, u32[]{:S(2)}) copy-start(bf16[3,3,3,256,256]{4,3,2,1,0:T(8,128)(2,1)} %param.13) | copy-start | bytes 10616836
